TPU v7x, 32 devices: a whole 2x2x4 slice. The times are simulated.
32 devices in a mesh: wave: 8 (over z, y), lev: 4 (over x, core).
Axes of the slice: x: 2, y: 2, z: 4, core: 2. Of those that a mesh axis runs over, the one named last changes fastest.
Arguments:
- spectral: bfloat16 [1280, 256, 1280], P('wave', 'lev'), may hold values from -6 to 6
- legendre: bfloat16 [1280, 32, 1280], P('wave'), may hold values from -0.0034179688 to 0.0034179688
- wave_map: int32 [1280], replicated, may hold values from 0 to 1279, each once
- row_points: int32 [32], replicated, may hold values from 20 to 5136, as said below
- brackets: int32 [4], replicated, may hold values from 0 to 14, as said below
- lev_weight: float32 [4], replicated, may hold values from 0.05 to 0.95
- climatology: float32 [4, 64, 5248], P('lev', 'wave'), may hold values from 0.1 to 1
Outputs:
- anomaly: float32 [4, 64, 5248], P('lev', 'wave')
Inputs may be any that keep to these rules, and one draw needn't show every extreme that they name: `wave_map`: each wavenumber once. `row_points`: each is 20 + 4 i for a whole number i below 1280; some row has 5136 points. `brackets`: pressure level p has its lower bracket level among the 4 model levels of band p (levels b * 4 to b * 4 + 3 for band b); some pressure level outside the last band takes the last level of its band; the last pressure level takes 16 - 2.
All inputs are finite; a program needn't handle non-finite values.
Results may differ from a plain program's by a relative error of at most 0.0003.
Values sent between devices are 32-bit elements; how exact they have to be, the bound alone decides.
No kernel may reach another device: no remote copies, remote signals or barrier semaphores. Data moves between devices by JAX's collectives and lax.ppermute only.
A program may use at most 256 MiB of HBM per device.

v0:
```python
import functools
import math

import jax
import jax.numpy as jnp
import numpy as np
from jax import lax
from jax.experimental import pallas as pl
from jax.experimental.pallas import tpu as pltpu
from jax.sharding import PartitionSpec as P

M = 1280
NT = 1280
LEV_DEV = 4
STEPS = 4
FIELDS = 2
ROWPAD = 5248

FS = FIELDS * STEPS
PART = 2 * FS
SQ = 8
STEP_SLOTS = 2
HALF_M = M // 2
KPTS = 768
KBLK = 256
BUF = 1536
VMEM_LIMIT = 56 * 1024 * 1024
F32 = jnp.float32
BF16 = jnp.bfloat16


def iota(shape, dim):
    return lax.broadcasted_iota(jnp.int32, shape, dim)


def legendre_kernel(slots, wave_map, brackets, low_ref, up_ref, first_ref, leg_ref, weight_ref, own_ref, prev_ref, own_rows, prev_rows):
    step = pl.program_id(0)
    groups = slots // SQ
    half = leg_ref.shape[2]
    width = STEP_SLOTS * 2 * half
    wave = lax.axis_index("wave")
    lev = lax.axis_index("lev")
    lower = brackets[lev]
    has_upper = lower - lev * LEV_DEV < LEV_DEV - 1
    w = weight_ref[lev]
    upper_w = jnp.where(has_upper, 1.0 - w, 0.0)
    before = jnp.maximum(lev - 1, 0)
    crosses = (lev > 0) & (brackets[before] == lev * LEV_DEV - 1)
    first_w = jnp.where(crosses, 1.0 - weight_ref[before], 0.0)
    degree = iota((16, NT), 1)
    sign = (1 - 2 * (degree % 2)).astype(F32).astype(BF16)
    lane = iota((1, width), 1)
    south = lane % (2 * half) >= half
    owns, firsts = [], []
    for pair in range(SQ // 2):
        orders, values = [], []
        for a in range(2):
            sq = 2 * pair + a
            for b in range(STEP_SLOTS):
                m = wave_map[wave * slots + sq * groups + step * STEP_SLOTS + b]
                orders.append(m)
                kept = jnp.where(degree >= m, 1.0, 0.0).astype(BF16)
                plain = [leg_ref[sq, b, i : i + 16, :] * kept for i in range(0, half, 16)]
                values += plain + [x * sign for x in plain]
        columns = []
        for a in range(2):
            for b in range(STEP_SLOTS):
                columns += [ref[2 * pair + a, b] for ref in (low_ref, up_ref, first_ref)]
        sums = lax.dot_general(
            jnp.concatenate(columns, axis=0), jnp.concatenate(values, axis=0), (((1,), (1,)), ((), ())), preferred_element_type=F32
        )
        for a in range(2):
            own = jnp.zeros((PART, width), F32)
            first = jnp.zeros((PART, width), F32)
            for b in range(STEP_SLOTS):
                at = (a * STEP_SLOTS + b) * 3 * PART
                block = sums[at : at + 3 * PART, a * width : (a + 1) * width]
                parity = (1 - 2 * (orders[a * STEP_SLOTS + b] % 2)).astype(F32)
                factor = jnp.where(south, parity, 1.0)
                here = lane // (2 * half) == b
                mixed = block[:PART] * (factor * w) + block[PART : 2 * PART] * (factor * upper_w)
                own = jnp.where(here, mixed, own)
                first = jnp.where(here, block[2 * PART :] * (factor * first_w), first)
            owns.append(own)
            firsts.append(first)
    rows = 2 * half
    for ref, parts in ((own_rows, owns), (prev_rows, firsts)):
        stacked = jnp.concatenate(parts, axis=0)
        for t in range(width // 128):
            at = pl.multiple_of(step * width + t * 128, 128)
            ref[pl.ds(at, 128), :] = stacked[:, t * 128 : (t + 1) * 128].T

    @pl.when(step == pl.num_programs(0) - 1)
    def _():
        for rows_ref, ref in ((own_rows, own_ref), (prev_rows, prev_ref)):
            rows_dev = ref.shape[1] // groups
            for r in range(rows):
                ref[r // rows_dev, (r % rows_dev) * groups : (r % rows_dev + 1) * groups, :] = rows_ref[pl.ds(r, groups, stride=rows), :]


def legendre_sums(spectral, legendre, wave_map, brackets, lev_weight):
    slots, cols, _ = spectral.shape
    half = legendre.shape[1]
    groups = slots // SQ
    spec = spectral.reshape(SQ, groups, cols, NT)
    leg = legendre.reshape(SQ, groups, half, NT)

    def low_map(i, wm, br):
        lev = lax.axis_index("lev")
        return 0, i, br[lev] - lev * LEV_DEV, 0

    def up_map(i, wm, br):
        lev = lax.axis_index("lev")
        return 0, i, jnp.minimum(br[lev] - lev * LEV_DEV + 1, LEV_DEV - 1), 0

    spec_block = (SQ, STEP_SLOTS, PART, NT)
    devices = lax.axis_size("wave") * lax.axis_size("lev")
    out_shape = (devices, 2 * half // devices * groups, SQ * PART)
    out = jax.ShapeDtypeStruct(out_shape, F32)
    out_spec = pl.BlockSpec(out_shape, lambda i, wm, br: (0, 0, 0))
    return pl.pallas_call(
        functools.partial(legendre_kernel, slots),
        out_shape=[out, out],
        grid_spec=pltpu.PrefetchScalarGridSpec(
            num_scalar_prefetch=2,
            grid=(groups // STEP_SLOTS,),
            in_specs=[
                pl.BlockSpec(spec_block, low_map),
                pl.BlockSpec(spec_block, up_map),
                pl.BlockSpec(spec_block, lambda i, wm, br: (0, i, 0, 0)),
                pl.BlockSpec((SQ, STEP_SLOTS, half, NT), lambda i, wm, br: (0, i, 0, 0)),
                pl.BlockSpec(memory_space=pltpu.SMEM),
            ],
            out_specs=[out_spec, out_spec],
            scratch_shapes=[pltpu.VMEM((groups * 2 * half, SQ * PART), F32)] * 2,
        ),
        compiler_params=pltpu.CompilerParams(vmem_limit_bytes=VMEM_LIMIT),
        cost_estimate=pl.CostEstimate(flops=2 * slots * 2 * half * 48 * NT, bytes_accessed=slots * NT * 2 * (48 + half), transcendentals=0),
        name="legendre_sums",
    )(wave_map, brackets, spec, spec, spec, leg, lev_weight)


def unit_circle(product, quarter):
    turn = jnp.round(product * (1.0 / quarter))
    rest = product - turn * quarter
    x = rest * ((0.5 * math.pi) / quarter)
    x2 = x * x
    sine = x * (1.0 + x2 * (-1.0 / 6 + x2 * (1.0 / 120 + x2 * (-1.0 / 5040 + x2 * (1.0 / 362880)))))
    cosine = 1.0 + x2 * (-0.5 + x2 * (1.0 / 24 + x2 * (-1.0 / 720 + x2 * (1.0 / 40320))))
    quad = turn.astype(jnp.int32) & 3
    odd = (quad & 1) == 1
    c = jnp.where(odd, sine, cosine)
    s = jnp.where(odd, cosine, sine)
    c = jnp.where((quad == 1) | (quad == 2), -c, c)
    s = jnp.where(quad >= 2, -s, s)
    return c, s


def own_points(points_ref, r2):
    wave = lax.axis_index("wave")
    lev = lax.axis_index("lev")
    row = 2 * (wave * lax.axis_size("lev") + lev) + r2
    return points_ref[row % points_ref.shape[0]]


def table_kernel(points_ref, map_ref, hi_ref, lo_ref, perm_ref):
    r2 = pl.program_id(0)
    kb = pl.program_id(1)
    rows = hi_ref.shape[1]
    steps = pl.num_programs(1)
    quarter = (own_points(points_ref, r2) // 4).astype(F32)
    perm_rows = perm_ref.shape[0]
    order = (r2 * steps + kb) * perm_rows + iota((perm_rows, 1), 0)
    wanted = jnp.where(order < HALF_M, 2 * order, 2 * (order - HALF_M) + 1)
    perm_ref[...] = jnp.where(map_ref[...] == wanted, 1.0, 0.0).astype(BF16)

    def put(tile, chunk, value):
        lanes = slice(tile * 128, tile * 128 + 128)
        hi = value.astype(BF16)
        hi_ref[0, pl.ds(chunk, 16), lanes] = hi
        lo_ref[0, pl.ds(chunk, 16), lanes] = (value - hi.astype(F32)).astype(BF16)

    def chunk_body(i, carry):
        chunk = pl.multiple_of(i * 16, 16)
        k = (kb * rows + chunk + iota((16, 128), 0)).astype(F32)
        lane = iota((16, 128), 1).astype(F32)
        c, s = unit_circle(2.0 * lane * k, quarter)
        c1, s1 = unit_circle(k, quarter)
        ct, st = unit_circle(256.0 * k, quarter)
        co = c * c1 - s * s1
        so = s * c1 + c * s1
        for t in range(HALF_M // 128):
            if t:
                c, s = c * ct - s * st, s * ct + c * st
                co, so = co * ct - so * st, so * ct + co * st
            put(t, chunk, c)
            put(5 + t, chunk, s)
            put(10 + t, chunk, co)
            put(15 + t, chunk, so)
        return carry

    lax.fori_loop(0, rows // 16, chunk_body, 0, unroll=2)


def tables(row_points, slot_map):
    steps = 8
    rows = KPTS // steps
    table = jax.ShapeDtypeStruct((2, KPTS, 2 * M), BF16)
    table_spec = pl.BlockSpec((1, rows, 2 * M), lambda r, k: (r, k, 0))
    return pl.pallas_call(
        table_kernel,
        out_shape=[table, table, jax.ShapeDtypeStruct((M, M), BF16)],
        grid=(2, steps),
        in_specs=[pl.BlockSpec(memory_space=pltpu.SMEM), pl.BlockSpec(memory_space=pltpu.VMEM)],
        out_specs=[table_spec, table_spec, pl.BlockSpec((M // (2 * steps), M), lambda r, k: (r * steps + k, 0))],
        compiler_params=pltpu.CompilerParams(vmem_limit_bytes=VMEM_LIMIT),
        cost_estimate=pl.CostEstimate(flops=2 * KPTS * 2 * M * 12, bytes_accessed=2 * KPTS * 2 * M * 4 + M * M * 2, transcendentals=0),
        name="fourier_tables",
    )(row_points, slot_map)


def pick_tables(plev):
    wide = plev * 2 * PART
    out = np.zeros((2, 4, 2 * wide, 2 * wide), np.float32)
    plans = (
        ((0, 1), (0, 1), (0, 1), (0, 1)),
        ((1, -1), (1, 1), (1, -1), (1, 1)),
        ((0, 1), (0, 1), (1, -1), (1, -1)),
        ((1, -1), (1, 1), (0, -1), (0, 1)),
    )
    for r2 in range(2):
        for kind, plan in enumerate(plans):
            for image, (part, sgn) in enumerate(plan):
                for hl in range(2):
                    for p in range(plev):
                        for q in range(FS):
                            src = hl * wide + p * 2 * PART + r2 * PART + q * 2 + part
                            dst = hl * wide + image * plev * FS + p * FS + q
                            out[r2, kind, src, dst] = sgn
    return out.astype(jnp.bfloat16)


def mean_table(plev):
    wide = plev * FS * 4
    out = np.zeros((2 * 4 * plev, 2 * wide), np.float32)
    for quarter in range(4):
        for p in range(plev):
            for part in range(2):
                image_quarter = (quarter + part) % 4
                start = (image_quarter * 2 + part) * plev * FS + p * FS
                out[part * 4 * plev + quarter * plev + p, start : start + FS] = 0.5 / STEPS
    return out.astype(jnp.bfloat16)


def flip_table():
    return np.fliplr(np.eye(KBLK, dtype=np.float32)).astype(jnp.bfloat16)


def split(x):
    hi = x.astype(BF16)
    return hi, (x - hi.astype(F32)).astype(BF16)


def nt_dot(a, b):
    return lax.dot_general(a, b, (((1,), (1,)), ((), ())), preferred_element_type=F32)


def nn_dot(a, b):
    return jnp.dot(a, b, preferred_element_type=F32)


def synth_kernel(
    points_ref, moved_ref, pick_ref, mean_ref, flip_ref, perm_hbm, hi_hbm, lo_hbm, out_ref,
    perm_ref, hi_ref, lo_ref, mixed, coef, direct, mirror, line, sems,
):
    waves, plev, block_rows, _ = moved_ref.shape
    sub = block_rows // 2
    wide = plev * 2 * PART
    part_rows = waves * sub
    copies = [pltpu.make_async_copy(perm_hbm, perm_ref, sems.at[0])]
    for r2 in range(2):
        copies.append(pltpu.make_async_copy(hi_hbm.at[r2], hi_ref.at[r2], sems.at[1 + 2 * r2]))
        copies.append(pltpu.make_async_copy(lo_hbm.at[r2], lo_ref.at[r2], sems.at[2 + 2 * r2]))
    for copy in copies:
        copy.start()

    for base in range(0, plev * 2, 8):
        cur = []
        for g in range(base, base + 8):
            pieces = [moved_ref[w, g // 2, (g % 2) * sub : (g % 2 + 1) * sub, :] for w in range(waves)]
            cur.append(jnp.concatenate(pieces, axis=0))
        group = iota((part_rows, 128), 1) // PART
        for bit in (1, 2, 4):
            unset = (group & bit) == 0
            nxt = list(cur)
            for g in range(8):
                if g & bit == 0:
                    a, b = cur[g], cur[g + bit]
                    nxt[g] = jnp.where(unset, a, pltpu.roll(b, bit * PART, 1))
                    nxt[g + bit] = jnp.where(unset, pltpu.roll(a, 128 - bit * PART, 1), b)
            cur = nxt
        for sq in range(SQ):
            hi, lo = split(cur[sq])
            lane = base * PART
            mixed[sq * part_rows : (sq + 1) * part_rows, lane : lane + 128] = hi
            mixed[sq * part_rows : (sq + 1) * part_rows, wide + lane : wide + lane + 128] = lo

    lane_row = (iota((1, 2 * wide), 1) // PART) % 2
    limit0 = (own_points(points_ref, 0) - 1) // 2
    limit1 = (own_points(points_ref, 1) - 1) // 2
    limit = jnp.where(lane_row == 0, limit0, limit1)
    place = iota((HALF_M, 1), 0)
    turned = (iota((1, 2 * wide), 1) % wide) // (plev * FS) >= 2
    flip_sign = jnp.where(turned & (place % 2 == 1), -1.0, 1.0).astype(BF16)
    copies[0].wait()
    for odd in range(2):
        ordered = nn_dot(perm_ref[odd * HALF_M : (odd + 1) * HALF_M, :], mixed[...])
        wave = 2 * place + odd
        factor = jnp.where(wave <= limit, jnp.where(wave == 0, 1.0, 2.0), 0.0)
        ordered = (ordered * factor).astype(BF16)
        for row in range(2):
            for part in range(2):
                picked = nn_dot(ordered, pick_ref[row, odd * 2 + part]).astype(BF16)
                coef[row, odd, part * HALF_M : (part + 1) * HALF_M, :] = picked * flip_sign
    direct[...] = jnp.zeros_like(direct)
    mirror[...] = jnp.zeros_like(mirror)

    for r2 in range(2):
        copies[1 + 2 * r2].wait()
        copies[2 + 2 * r2].wait()

        def contraction(odd):
            lanes = slice(odd * M, (odd + 1) * M)
            both = nn_dot(hi_ref[r2, :, lanes], coef[r2, odd])
            rest = nn_dot(lo_ref[r2, :, lanes], coef[r2, odd, :, :wide])
            return both[:, :wide] + (both[:, wide:] + rest)

        even_sum = contraction(0)
        odd_sum = contraction(1)
        plus = even_sum + odd_sum
        minus = even_sum - odd_sum
        squares = jnp.concatenate([plus * plus, minus * minus], axis=1)
        sq_hi, sq_lo = split(squares)
        energy = nt_dot(mean_ref[...], sq_hi) + nt_dot(mean_ref[...], sq_lo)
        rows = 4 * plev
        direct[:, :KPTS] = energy[:rows]
        en_hi, en_lo = split(energy[rows:])
        for t in range(KPTS // KBLK):
            lanes = slice(t * KBLK, (t + 1) * KBLK)
            back = KPTS - (t + 1) * KBLK
            mirror[:, back : back + KBLK] = nn_dot(en_hi[:, lanes], flip_ref[...]) + nn_dot(en_lo[:, lanes], flip_ref[...])

        quarter = own_points(points_ref, r2) // 4
        lane = iota((rows, BUF), 1)
        shift = (quarter + (BUF - (KPTS - 1))) % BUF
        whole = jnp.where(lane <= quarter // 2, direct[...], pltpu.roll(mirror[...], shift, 1))
        direct[...] = whole
        line[...] = jnp.zeros_like(line)
        lane = iota((plev, BUF), 1)
        for b in range(4):
            start = quarter * b
            inner = start % 128
            base = pl.multiple_of(start - inner, 128)
            piece = pltpu.roll(direct[b * plev : (b + 1) * plev, :], inner, 1)
            old = line[:, pl.ds(base, BUF)]
            line[:, pl.ds(base, BUF)] = jnp.where((lane >= inner) & (lane < inner + quarter), piece, old)
        out_ref[:, pl.ds(r2, 1), :] = line[:, :ROWPAD].reshape(plev, 1, ROWPAD)


def synthesis(moved, perm, table_hi, table_lo, row_points):
    waves, plev, block_rows, _ = moved.shape
    wide = plev * 2 * PART
    vmem = pl.BlockSpec(memory_space=pltpu.VMEM)
    anywhere = pl.BlockSpec(memory_space=pl.ANY)
    return pl.pallas_call(
        synth_kernel,
        out_shape=jax.ShapeDtypeStruct((plev, 2, ROWPAD), F32),
        in_specs=[pl.BlockSpec(memory_space=pltpu.SMEM), vmem, vmem, vmem, vmem, anywhere, anywhere, anywhere],
        out_specs=vmem,
        scratch_shapes=[
            pltpu.VMEM((M, M), BF16),
            pltpu.VMEM((2, KPTS, 2 * M), BF16),
            pltpu.VMEM((2, KPTS, 2 * M), BF16),
            pltpu.VMEM((M, 2 * wide), BF16),
            pltpu.VMEM((2, 2, M, 2 * wide), BF16),
            pltpu.VMEM((4 * plev, BUF), F32),
            pltpu.VMEM((4 * plev, BUF), F32),
            pltpu.VMEM((plev, 3 * 1280 + BUF), F32),
            pltpu.SemaphoreType.DMA((5,)),
        ],
        compiler_params=pltpu.CompilerParams(vmem_limit_bytes=VMEM_LIMIT),
        cost_estimate=pl.CostEstimate(flops=2 * 2 * KPTS * 2 * M * 384, bytes_accessed=2 * KPTS * 2 * M * 4 + M * M * 2, transcendentals=0),
        name="synthesis",
    )(row_points, moved, pick_tables(plev), mean_table(plev), flip_table(), perm, table_hi, table_lo)


def local(spectral, legendre, wave_map, row_points, brackets, lev_weight, climatology):
    slots = spectral.shape[0]
    half = legendre.shape[1]
    groups = slots // SQ
    wave_count = lax.axis_size("wave")
    lev_count = lax.axis_size("lev")
    rows_dev = 2 * half // (wave_count * lev_count)
    own, prev = legendre_sums(spectral, legendre, wave_map, brackets, lev_weight)
    from_next = lax.ppermute(prev, "lev", [(d, d - 1) for d in range(1, lev_count)])
    moved = lax.all_to_all(own + from_next, ("wave", "lev"), split_axis=0, concat_axis=0, tiled=True)
    moved = moved.reshape(wave_count, lev_count, rows_dev * groups, SQ * PART)
    slot_map = jnp.transpose(wave_map.reshape(wave_count, SQ, groups), (1, 0, 2)).reshape(1, M)
    table_hi, table_lo, perm = tables(row_points, slot_map)
    energy = synthesis(moved, perm, table_hi, table_lo, row_points)
    result = lax.all_to_all(energy, "lev", split_axis=0, concat_axis=0, tiled=True)
    result = result.reshape(1, rows_dev * lev_count, ROWPAD)
    points_all = jnp.concatenate([row_points, row_points])
    band_rows = rows_dev * lev_count
    out_points = lax.dynamic_slice_in_dim(points_all, lax.axis_index("wave") * band_rows, band_rows, 0)
    places = jnp.arange(ROWPAD, dtype=jnp.int32)
    inside = places[None, None, :] < out_points[None, :, None]
    return jnp.where(inside, result - climatology, 0.0)


def solution(mesh):
    placed = (
        P("wave", "lev", None),
        P("wave", None, None),
        P(),
        P(),
        P(),
        P(),
        P("lev", "wave", None),
    )
    return jax.shard_map(
        local, mesh=mesh, in_specs=placed, out_specs=P("lev", "wave", None), check_vma=False
    )
```

profile of v0, /device:TPU:0, one launch (start us, length us, event | category | flops | bytes accessed | tf_op | source)
XLA Modules:
  0.0 80.9 jit_solution(11571763970567824712)
XLA Ops:
  0.0 0.0 copy-start.2
  0.0 19.9 %legendre_sums.1 = (f32[32,40,128]{2,1,0:T(8,128)}, f32[32,40,128]{2,1,0:T(8,128)}) custom-call(s32[1280]{0:T(1024)} %wave_map.1, s32[4]{0:T(128)} %brackets.1, bf16[8,20,64,1280]{3,2,1,0:T(8,128)(2,1)} %bitcast.4, bf16[8,20,64,1280]{3,2,1,0:T(8,128)(2,1)} %bitcast.5, bf16[8,20,64,1280]{3,2,1,0:T(8,128)(2,1)} %bitcast.6, bf16[8,20,32,1280]{3,2,1,0:T(8,128)(2,1)} %bitcast.7, ...), custom_call_target="tpu_custom_call" | custom-call | flops 1258291200 | bytes 32768000 | tf_op jit(solution)/shard_map/legendre_sums/pallas_call | solution.py:121
  19.9 1.3 %collective-permute-start = (f32[32,40,128]{2,1,0:T(8,128)}, f32[32,40,128]{2,1,0:T(8,128)S(1)}, u32[]{:S(2)}, u32[]{:S(2)}) collective-permute-start(f32[32,40,128]{2,1,0:T(8,128)} %get-tuple-element.11), channel_id=1, source_target_pairs={{1,0},{2,1},{3,2},{5,4},{6,5},{7,6},{9,8},{10,9},{11,10},{13,12},{... | collective-permute-start | bytes 1966088 | tf_op jit(solution)/shard_map/ppermute | solution.py:405
  21.1 2.9 %collective-permute-done = f32[32,40,128]{2,1,0:T(8,128)S(1)} collective-permute-done((f32[32,40,128]{2,1,0:T(8,128)}, f32[32,40,128]{2,1,0:T(8,128)S(1)}, u32[]{:S(2)}, u32[]{:S(2)}) %collective-permute-start) | collective-permute-done | bytes 655392 | tf_op jit(solution)/shard_map/ppermute | solution.py:405
  24.0 2.0 %add.7 = f32[32,40,128]{2,1,0:T(8,128)} add(f32[32,40,128]{2,1,0:T(8,128)} %get-tuple-element.10, f32[32,40,128]{2,1,0:T(8,128)S(1)} %collective-permute-done) | non-fusion elementwise | flops 163840 | bytes 1966080 | tf_op jit(solution)/shard_map/add | solution.py:406
  26.0 13.8 %all-to-all-start = ((f32[32,40,128]{2,1,0:T(8,128)}), f32[32,40,128]{2,1,0:T(8,128)S(1)}, u32[]{:S(2)}, u32[]{:S(2)}) async-start(f32[32,40,128]{2,1,0:T(8,128)} %add.7), calls=%async_computation | async-start | bytes 1310720 | tf_op jit(solution)/shard_map/all_to_all | solution.py:406
  39.8 0.0 copy-done.2
  39.8 0.1 reshape.53
  39.9 0.7 reshape.54.map_ref
  40.6 14.4 %fourier_tables.1 = (bf16[2,768,2560]{2,1,0:T(8,128)(2,1)}, bf16[2,768,2560]{2,1,0:T(8,128)(2,1)}, bf16[1280,1280]{1,0:T(8,128)(2,1)}) custom-call(s32[32]{0:T(128)} %points_ref.3, s32[1,1280]{1,0:T(1,128)} %reshape.54.map_ref), custom_call_target="tpu_custom_call" | custom-call | flops 47185920 | bytes 19005440 | tf_op jit(solution)/shard_map/fourier_tables/pallas_call | solution.py:210
  55.1 2.6 %all-to-all-done = f32[32,40,128]{2,1,0:T(8,128)S(1)} async-done(((f32[32,40,128]{2,1,0:T(8,128)}), f32[32,40,128]{2,1,0:T(8,128)S(1)}, u32[]{:S(2)}, u32[]{:S(2)}) %all-to-all-start) | async-done | bytes 655392 | tf_op jit(solution)/shard_map/all_to_all | solution.py:406
  57.7 0.0 copy-start
  57.7 0.8 %copy-done = f32[32,40,128]{2,1,0:T(8,128)} copy-done((f32[32,40,128]{2,1,0:T(8,128)}, f32[32,40,128]{2,1,0:T(8,128)S(1)}, u32[]{:S(2)}) %copy-start) | copy-done | bytes 655384
  58.6 0.0 copy-start.3
  58.6 0.0 copy-start.1
  58.6 13.1 %synthesis.1 = f32[4,2,5248]{2,1,0:T(2,128)} custom-call(s32[32]{0:T(128)} %points_ref.3, f32[8,4,40,128]{3,2,1,0:T(8,128)} %bitcast.8, bf16[2,4,256,256]{3,2,1,0:T(8,128)(2,1)} %constant.20.clone.pick_ref, bf16[32,256]{1,0:T(8,128)(2,1)} %constant.21.clone.mean_ref, bf16[256,256]{1,0:T(8,128)(2,1)} %constant.22.clone.flip_ref, ...), custom_call_target="tpu_custom_call" | custom-call | flops 3019898880 | bytes 19005440 | tf_op jit(solution)/shard_map/synthesis/pallas_call | solution.py:375
  71.7 3.4 %all-to-all-start.1 = ((f32[4,2,5248]{2,1,0:T(2,128)}), f32[4,2,5248]{2,1,0:T(2,128)S(1)}, u32[]{:S(2)}, u32[]{:S(2)}) async-start(f32[4,2,5248]{2,1,0:T(2,128)} %synthesis.1), calls=%async_computation.1 | async-start | bytes 335872 | tf_op jit(solution)/shard_map/all_to_all | solution.py:411
  75.0 0.0 copy-done.3
  75.0 0.1 pad_add_fusion
  75.1 0.1 dynamic_slice.3
  75.2 4.8 %all-to-all-done.1 = f32[4,2,5248]{2,1,0:T(2,128)S(1)} async-done(((f32[4,2,5248]{2,1,0:T(2,128)}), f32[4,2,5248]{2,1,0:T(2,128)S(1)}, u32[]{:S(2)}, u32[]{:S(2)}) %all-to-all-start.1) | async-done | bytes 167968 | tf_op jit(solution)/shard_map/all_to_all | solution.py:411
  80.0 0.1 reshape.55
  80.1 0.0 copy-done.1
  80.1 0.8 subtract_select_fusion
  (1 shorter events, 0.0 us)
Async XLA Ops:
  0.0 39.8 %copy-start.2 = (s32[1280]{0:T(1024)S(1)}, s32[1280]{0:T(1024)}, u32[]{:S(2)}) copy-start(s32[1280]{0:T(1024)} %wave_map.1) | copy-start | bytes 15364
  19.9 4.2 %collective-permute-start = (f32[32,40,128]{2,1,0:T(8,128)}, f32[32,40,128]{2,1,0:T(8,128)S(1)}, u32[]{:S(2)}, u32[]{:S(2)}) collective-permute-start(f32[32,40,128]{2,1,0:T(8,128)} %get-tuple-element.11), channel_id=1, source_target_pairs={{1,0},{2,1},{3,2},{5,4},{6,5},{7,6},{9,8},{10,9},{11,10},{13,12},{... | collective-permute-start | bytes 1966088 | tf_op jit(solution)/shard_map/ppermute | solution.py:405
  26.0 31.7 %all-to-all-start = ((f32[32,40,128]{2,1,0:T(8,128)}), f32[32,40,128]{2,1,0:T(8,128)S(1)}, u32[]{:S(2)}, u32[]{:S(2)}) async-start(f32[32,40,128]{2,1,0:T(8,128)} %add.7), calls=%async_computation | async-start | bytes 1310720 | tf_op jit(solution)/shard_map/all_to_all | solution.py:406
  57.7 0.8 %copy-start = (f32[32,40,128]{2,1,0:T(8,128)}, f32[32,40,128]{2,1,0:T(8,128)S(1)}, u32[]{:S(2)}) copy-start(f32[32,40,128]{2,1,0:T(8,128)S(1)} %all-to-all-done) | copy-start | bytes 1966084
  58.6 16.5 %copy-start.3 = (s32[32]{0:T(128)S(1)}, s32[32]{0:T(128)}, u32[]{:S(2)}) copy-start(s32[32]{0:T(128)} %points_ref.3) | copy-start | bytes 388
  58.6 21.6 %copy-start.1 = (f32[1,8,5248]{2,1,0:T(8,128)S(1)}, f32[1,8,5248]{2,1,0:T(8,128)}, u32[]{:S(2)}) copy-start(f32[1,8,5248]{2,1,0:T(8,128)} %param.16) | copy-start | bytes 503812
  71.7 8.4 %all-to-all-start.1 = ((f32[4,2,5248]{2,1,0:T(2,128)}), f32[4,2,5248]{2,1,0:T(2,128)S(1)}, u32[]{:S(2)}, u32[]{:S(2)}) async-start(f32[4,2,5248]{2,1,0:T(2,128)} %synthesis.1), calls=%async_computation.1 | async-start | bytes 335872 | tf_op jit(solution)/shard_map/all_to_all | solution.py:411
where the time goes:
time: 81.4 us; the launch traced here: 80.9 us
  Pallas kernels  47.4 us (58%)
  starting transfers between devices  18.4 us (23%)
  waiting for transfers between devices  10.4 us (13%)
  other arithmetic  2.83 us (3%)
  local copies, waits for them, and re-layouts  1.86 us (2%)
    pallas_call x1, Pallas kernels, legendre_sums(): pl.pallas_call(functools.partial(legendre_kernel, slots), out_shape=[out,...  19.9 us
    pallas_call x1, Pallas kernels, tables(): pl.pallas_call(table_kernel, out_shape=[table, table, jax.ShapeDtypeStruc...  14.4 us
    all_to_all x1, starting transfers between devices, local(): lax.all_to_all(own + from_next, ('wave', 'lev'), split_axis=0, concat_axi...  13.8 us
    pallas_call x1, Pallas kernels, synthesis(): pl.pallas_call(synth_kernel, out_shape=jax.ShapeDtypeStruct((plev, 2, ROW...  13.1 us
    all_to_all x1, waiting for transfers between devices, local(): lax.all_to_all(energy, 'lev', split_axis=0, concat_axis=0, tiled=True)  4.82 us
    all_to_all x1, starting transfers between devices, local(): lax.all_to_all(energy, 'lev', split_axis=0, concat_axis=0, tiled=True)  3.36 us
    ppermute x1, waiting for transfers between devices, local(): lax.ppermute(prev, 'lev', [(d, d - 1) for d in range(1, lev_count)])  2.9 us
    all_to_all x1, waiting for transfers between devices, local(): lax.all_to_all(own + from_next, ('wave', 'lev'), split_axis=0, concat_axi...  2.64 us
  transfers between devices with their start and end apart: 3, of which 3 were waited for; matrix products, arithmetic and copies ran while one was open for 1% of the time, Pallas kernels for 18%

commit v1 on v0

--- a/solution.py
+++ b/solution.py
@@ -20,6 +20,7 @@
 PART = 2 * FS
 SQ = 8
 STEP_SLOTS = 2
+DEPTH = 3
 HALF_M = M // 2
 KPTS = 768
 KBLK = 256
@@ -33,15 +34,19 @@
     return lax.broadcasted_iota(jnp.int32, shape, dim)
 
 
-def legendre_kernel(slots, wave_map, brackets, low_ref, up_ref, first_ref, leg_ref, weight_ref, own_ref, prev_ref, own_rows, prev_rows):
-    step = pl.program_id(0)
-    groups = slots // SQ
-    half = leg_ref.shape[2]
+def legendre_kernel(
+    wave_map, brackets, weight_ref, spec_hbm, leg_hbm, own_ref, prev_ref,
+    low_buf, up_buf, first_buf, leg_buf, own_rows, prev_rows, sems,
+):
+    groups = spec_hbm.shape[1]
+    slots = SQ * groups
+    steps = groups // STEP_SLOTS
+    half = leg_hbm.shape[2]
     width = STEP_SLOTS * 2 * half
     wave = lax.axis_index("wave")
     lev = lax.axis_index("lev")
-    lower = brackets[lev]
-    has_upper = lower - lev * LEV_DEV < LEV_DEV - 1
+    lower = brackets[lev] - lev * LEV_DEV
+    has_upper = lower < LEV_DEV - 1
     w = weight_ref[lev]
     upper_w = jnp.where(has_upper, 1.0 - w, 0.0)
     before = jnp.maximum(lev - 1, 0)
@@ -51,51 +56,100 @@
     sign = (1 - 2 * (degree % 2)).astype(F32).astype(BF16)
     lane = iota((1, width), 1)
     south = lane % (2 * half) >= half
-    owns, firsts = [], []
-    for pair in range(SQ // 2):
-        orders, values = [], []
-        for a in range(2):
-            sq = 2 * pair + a
-            for b in range(STEP_SLOTS):
-                m = wave_map[wave * slots + sq * groups + step * STEP_SLOTS + b]
-                orders.append(m)
-                kept = jnp.where(degree >= m, 1.0, 0.0).astype(BF16)
-                plain = [leg_ref[sq, b, i : i + 16, :] * kept for i in range(0, half, 16)]
-                values += plain + [x * sign for x in plain]
-        columns = []
-        for a in range(2):
-            for b in range(STEP_SLOTS):
-                columns += [ref[2 * pair + a, b] for ref in (low_ref, up_ref, first_ref)]
-        sums = lax.dot_general(
-            jnp.concatenate(columns, axis=0), jnp.concatenate(values, axis=0), (((1,), (1,)), ((), ())), preferred_element_type=F32
-        )
-        for a in range(2):
-            own = jnp.zeros((PART, width), F32)
-            first = jnp.zeros((PART, width), F32)
-            for b in range(STEP_SLOTS):
-                at = (a * STEP_SLOTS + b) * 3 * PART
-                block = sums[at : at + 3 * PART, a * width : (a + 1) * width]
-                parity = (1 - 2 * (orders[a * STEP_SLOTS + b] % 2)).astype(F32)
-                factor = jnp.where(south, parity, 1.0)
-                here = lane // (2 * half) == b
-                mixed = block[:PART] * (factor * w) + block[PART : 2 * PART] * (factor * upper_w)
-                own = jnp.where(here, mixed, own)
-                first = jnp.where(here, block[2 * PART :] * (factor * first_w), first)
-            owns.append(own)
-            firsts.append(first)
+
+    def columns_copy(step, level, buf, kind):
+        slot = step % DEPTH
+        rows = pl.ds(pl.multiple_of(level * PART, PART), PART)
+        src = spec_hbm.at[:, pl.ds(step * STEP_SLOTS, STEP_SLOTS), rows, :]
+        return pltpu.make_async_copy(src, buf.at[slot], sems.at[slot, kind])
+
+    def values_copy(step):
+        slot = step % DEPTH
+        return pltpu.make_async_copy(leg_hbm.at[:, pl.ds(step * STEP_SLOTS, STEP_SLOTS)], leg_buf.at[slot], sems.at[slot, 3])
+
+    def fetch(step):
+        values_copy(step).start()
+        columns_copy(step, lower, low_buf, 0).start()
+
+        @pl.when(has_upper)
+        def _():
+            columns_copy(step, lower + 1, up_buf, 1).start()
+
+        @pl.when(crosses)
+        def _():
+            columns_copy(step, 0, first_buf, 2).start()
+
+    def await_step(step):
+        values_copy(step).wait()
+        columns_copy(step, lower, low_buf, 0).wait()
+
+        @pl.when(has_upper)
+        def _():
+            columns_copy(step, lower + 1, up_buf, 1).wait()
+
+        @pl.when(crosses)
+        def _():
+            columns_copy(step, 0, first_buf, 2).wait()
+
+    for step in range(DEPTH - 1):
+        fetch(step)
+
+    @pl.when(jnp.logical_not(has_upper))
+    def _():
+        up_buf[...] = jnp.zeros_like(up_buf)
+
+    @pl.when(jnp.logical_not(crosses))
+    def _():
+        first_buf[...] = jnp.zeros_like(first_buf)
+
+    def step_body(step, carry):
+        slot = step % DEPTH
+        await_step(step)
+
+        @pl.when(step + DEPTH - 1 < steps)
+        def _():
+            fetch(step + DEPTH - 1)
+
+        owns, firsts = [], []
+        for pair in range(SQ // 2):
+            orders, values, columns = [], [], []
+            for a in range(2):
+                sq = 2 * pair + a
+                for b in range(STEP_SLOTS):
+                    m = wave_map[wave * slots + sq * groups + step * STEP_SLOTS + b]
+                    orders.append(m)
+                    kept = jnp.where(degree >= m, 1.0, 0.0).astype(BF16)
+                    plain = [leg_buf[slot, sq, b, i : i + 16, :] * kept for i in range(0, half, 16)]
+                    values += plain + [x * sign for x in plain]
+                    columns += [buf[slot, sq, b] for buf in (low_buf, up_buf, first_buf)]
+            sums = nt_dot(jnp.concatenate(columns, axis=0), jnp.concatenate(values, axis=0))
+            for a in range(2):
+                own = jnp.zeros((PART, width), F32)
+                first = jnp.zeros((PART, width), F32)
+                for b in range(STEP_SLOTS):
+                    at = (a * STEP_SLOTS + b) * 3 * PART
+                    block = sums[at : at + 3 * PART, a * width : (a + 1) * width]
+                    parity = (1 - 2 * (orders[a * STEP_SLOTS + b] % 2)).astype(F32)
+                    factor = jnp.where(south, parity, 1.0)
+                    here = lane // (2 * half) == b
+                    mixed = block[:PART] * (factor * w) + block[PART : 2 * PART] * (factor * upper_w)
+                    own = jnp.where(here, mixed, own)
+                    first = jnp.where(here, block[2 * PART :] * (factor * first_w), first)
+                owns.append(own)
+                firsts.append(first)
+        for ref, parts in ((own_rows, owns), (prev_rows, firsts)):
+            stacked = jnp.concatenate(parts, axis=0)
+            for t in range(width // 128):
+                at = pl.multiple_of(step * width + t * 128, 128)
+                ref[pl.ds(at, 128), :] = stacked[:, t * 128 : (t + 1) * 128].T
+        return carry
+
+    lax.fori_loop(0, steps, step_body, 0)
     rows = 2 * half
-    for ref, parts in ((own_rows, owns), (prev_rows, firsts)):
-        stacked = jnp.concatenate(parts, axis=0)
-        for t in range(width // 128):
-            at = pl.multiple_of(step * width + t * 128, 128)
-            ref[pl.ds(at, 128), :] = stacked[:, t * 128 : (t + 1) * 128].T
-
-    @pl.when(step == pl.num_programs(0) - 1)
-    def _():
-        for rows_ref, ref in ((own_rows, own_ref), (prev_rows, prev_ref)):
-            rows_dev = ref.shape[1] // groups
-            for r in range(rows):
-                ref[r // rows_dev, (r % rows_dev) * groups : (r % rows_dev + 1) * groups, :] = rows_ref[pl.ds(r, groups, stride=rows), :]
+    for rows_ref, ref in ((own_rows, own_ref), (prev_rows, prev_ref)):
+        rows_dev = ref.shape[1] // groups
+        for r in range(rows):
+            ref[r // rows_dev, (r % rows_dev) * groups : (r % rows_dev + 1) * groups, :] = rows_ref[pl.ds(r, groups, stride=rows), :]
 
 
 def legendre_sums(spectral, legendre, wave_map, brackets, lev_weight):
@@ -104,40 +158,24 @@
     groups = slots // SQ
     spec = spectral.reshape(SQ, groups, cols, NT)
     leg = legendre.reshape(SQ, groups, half, NT)
-
-    def low_map(i, wm, br):
-        lev = lax.axis_index("lev")
-        return 0, i, br[lev] - lev * LEV_DEV, 0
-
-    def up_map(i, wm, br):
-        lev = lax.axis_index("lev")
-        return 0, i, jnp.minimum(br[lev] - lev * LEV_DEV + 1, LEV_DEV - 1), 0
-
-    spec_block = (SQ, STEP_SLOTS, PART, NT)
     devices = lax.axis_size("wave") * lax.axis_size("lev")
-    out_shape = (devices, 2 * half // devices * groups, SQ * PART)
-    out = jax.ShapeDtypeStruct(out_shape, F32)
-    out_spec = pl.BlockSpec(out_shape, lambda i, wm, br: (0, 0, 0))
+    out = jax.ShapeDtypeStruct((devices, 2 * half // devices * groups, SQ * PART), F32)
+    smem = pl.BlockSpec(memory_space=pltpu.SMEM)
+    vmem = pl.BlockSpec(memory_space=pltpu.VMEM)
+    anywhere = pl.BlockSpec(memory_space=pl.ANY)
     return pl.pallas_call(
-        functools.partial(legendre_kernel, slots),
+        legendre_kernel,
         out_shape=[out, out],
-        grid_spec=pltpu.PrefetchScalarGridSpec(
-            num_scalar_prefetch=2,
-            grid=(groups // STEP_SLOTS,),
-            in_specs=[
-                pl.BlockSpec(spec_block, low_map),
-                pl.BlockSpec(spec_block, up_map),
-                pl.BlockSpec(spec_block, lambda i, wm, br: (0, i, 0, 0)),
-                pl.BlockSpec((SQ, STEP_SLOTS, half, NT), lambda i, wm, br: (0, i, 0, 0)),
-                pl.BlockSpec(memory_space=pltpu.SMEM),
-            ],
-            out_specs=[out_spec, out_spec],
-            scratch_shapes=[pltpu.VMEM((groups * 2 * half, SQ * PART), F32)] * 2,
-        ),
+        in_specs=[smem, smem, smem, anywhere, anywhere],
+        out_specs=[vmem, vmem],
+        scratch_shapes=[pltpu.VMEM((DEPTH, SQ, STEP_SLOTS, PART, NT), BF16)] * 3
+        + [pltpu.VMEM((DEPTH, SQ, STEP_SLOTS, half, NT), BF16)]
+        + [pltpu.VMEM((groups * 2 * half, SQ * PART), F32)] * 2
+        + [pltpu.SemaphoreType.DMA((DEPTH, 4))],
         compiler_params=pltpu.CompilerParams(vmem_limit_bytes=VMEM_LIMIT),
         cost_estimate=pl.CostEstimate(flops=2 * slots * 2 * half * 48 * NT, bytes_accessed=slots * NT * 2 * (48 + half), transcendentals=0),
         name="legendre_sums",
-    )(wave_map, brackets, spec, spec, spec, leg, lev_weight)
+    )(wave_map, brackets, lev_weight, spec, leg)
 
 
 def unit_circle(product, quarter):

time: 81.4 us -> 77.2 us (0.948)
  Pallas kernels: 47.4 us -> 43.1 us
    pallas_call x1, Pallas kernels: 19.9 us -> 15.6 us  [legendre_sums(): pl.pallas_call(legendre_kernel, out_shape=[out, out], in_specs=[smem, sme...]
  transfers between devices with their start and end apart: 3 -> 3, of which waited for: 3 -> 3; matrix products, arithmetic and copies ran while one was open for 1% -> 1% of each run, Pallas kernels for 18% -> 19%
where the time goes in v1:
time: 77.2 us; the launch traced here: 76.9 us
  Pallas kernels  43.1 us (56%)
  starting transfers between devices  18.6 us (24%)
  waiting for transfers between devices  10.4 us (13%)
  other arithmetic  2.83 us (4%)
  local copies, waits for them, and re-layouts  1.86 us (2%)
    pallas_call x1, Pallas kernels, legendre_sums(): pl.pallas_call(legendre_kernel, out_shape=[out, out], in_specs=[smem, sme...  15.6 us
    pallas_call x1, Pallas kernels, tables(): pl.pallas_call(table_kernel, out_shape=[table, table, jax.ShapeDtypeStruc...  14.4 us
    all_to_all x1, starting transfers between devices, local(): lax.all_to_all(own + from_next, ('wave', 'lev'), split_axis=0, concat_axi...  13.9 us
    pallas_call x1, Pallas kernels, synthesis(): pl.pallas_call(synth_kernel, out_shape=jax.ShapeDtypeStruct((plev, 2, ROW...  13.1 us
    all_to_all x1, waiting for transfers between devices, local(): lax.all_to_all(energy, 'lev', split_axis=0, concat_axis=0, tiled=True)  4.82 us
    all_to_all x1, starting transfers between devices, local(): lax.all_to_all(energy, 'lev', split_axis=0, concat_axis=0, tiled=True)  3.36 us
    ppermute x1, waiting for transfers between devices, local(): lax.ppermute(prev, 'lev', [(d, d - 1) for d in range(1, lev_count)])  2.9 us
    all_to_all x1, waiting for transfers between devices, local(): lax.all_to_all(own + from_next, ('wave', 'lev'), split_axis=0, concat_axi...  2.64 us
  transfers between devices with their start and end apart: 3, of which 3 were waited for; matrix products, arithmetic and copies ran while one was open for 1% of the time, Pallas kernels for 19%

profile of v1, /device:TPU:0, one launch (start us, length us, event | category | flops | bytes accessed | tf_op | source)
XLA Modules:
  0.0 76.9 jit_solution(16920098279003274499)
XLA Ops:
  0.0 0.0 copy-start.2
  0.0 15.6 %legendre_sums.1 = (f32[32,40,128]{2,1,0:T(8,128)}, f32[32,40,128]{2,1,0:T(8,128)}) custom-call(s32[1280]{0:T(1024)} %wave_map.1, s32[4]{0:T(128)} %brackets.1, f32[4]{0:T(128)} %weight_ref.1, bf16[8,20,64,1280]{3,2,1,0:T(8,128)(2,1)} %bitcast.4, bf16[8,20,32,1280]{3,2,1,0:T(8,128)(2,1)} %bitcast.5), custom_call_target="tpu_custom_call" | custom-call | flops 1258291200 | bytes 32768000 | tf_op jit(solution)/shard_map/legendre_sums/pallas_call | solution.py:166
  15.6 1.3 %collective-permute-start = (f32[32,40,128]{2,1,0:T(8,128)}, f32[32,40,128]{2,1,0:T(8,128)S(1)}, u32[]{:S(2)}, u32[]{:S(2)}) collective-permute-start(f32[32,40,128]{2,1,0:T(8,128)} %get-tuple-element.11), channel_id=1, source_target_pairs={{1,0},{2,1},{3,2},{5,4},{6,5},{7,6},{9,8},{10,9},{11,10},{13,12},{... | collective-permute-start | bytes 1966088 | tf_op jit(solution)/shard_map/ppermute | solution.py:443
  16.9 2.9 %collective-permute-done = f32[32,40,128]{2,1,0:T(8,128)S(1)} collective-permute-done((f32[32,40,128]{2,1,0:T(8,128)}, f32[32,40,128]{2,1,0:T(8,128)S(1)}, u32[]{:S(2)}, u32[]{:S(2)}) %collective-permute-start) | collective-permute-done | bytes 655392 | tf_op jit(solution)/shard_map/ppermute | solution.py:443
  19.8 2.0 %add.7 = f32[32,40,128]{2,1,0:T(8,128)} add(f32[32,40,128]{2,1,0:T(8,128)} %get-tuple-element.10, f32[32,40,128]{2,1,0:T(8,128)S(1)} %collective-permute-done) | non-fusion elementwise | flops 163840 | bytes 1966080 | tf_op jit(solution)/shard_map/add | solution.py:444
  21.8 13.9 %all-to-all-start = ((f32[32,40,128]{2,1,0:T(8,128)}), f32[32,40,128]{2,1,0:T(8,128)S(1)}, u32[]{:S(2)}, u32[]{:S(2)}) async-start(f32[32,40,128]{2,1,0:T(8,128)} %add.7), calls=%async_computation | async-start | bytes 1310720 | tf_op jit(solution)/shard_map/all_to_all | solution.py:444
  35.8 0.0 copy-done.2
  35.8 0.1 reshape.53
  35.9 0.7 reshape.54.map_ref
  36.6 14.4 %fourier_tables.1 = (bf16[2,768,2560]{2,1,0:T(8,128)(2,1)}, bf16[2,768,2560]{2,1,0:T(8,128)(2,1)}, bf16[1280,1280]{1,0:T(8,128)(2,1)}) custom-call(s32[32]{0:T(128)} %points_ref.3, s32[1,1280]{1,0:T(1,128)} %reshape.54.map_ref), custom_call_target="tpu_custom_call" | custom-call | flops 47185920 | bytes 19005440 | tf_op jit(solution)/shard_map/fourier_tables/pallas_call | solution.py:248
  51.1 2.6 %all-to-all-done = f32[32,40,128]{2,1,0:T(8,128)S(1)} async-done(((f32[32,40,128]{2,1,0:T(8,128)}), f32[32,40,128]{2,1,0:T(8,128)S(1)}, u32[]{:S(2)}, u32[]{:S(2)}) %all-to-all-start) | async-done | bytes 655392 | tf_op jit(solution)/shard_map/all_to_all | solution.py:444
  53.7 0.0 copy-start
  53.7 0.8 %copy-done = f32[32,40,128]{2,1,0:T(8,128)} copy-done((f32[32,40,128]{2,1,0:T(8,128)}, f32[32,40,128]{2,1,0:T(8,128)S(1)}, u32[]{:S(2)}) %copy-start) | copy-done | bytes 655384
  54.6 0.0 copy-start.3
  54.6 0.0 copy-start.1
  54.6 13.1 %synthesis.1 = f32[4,2,5248]{2,1,0:T(2,128)} custom-call(s32[32]{0:T(128)} %points_ref.3, f32[8,4,40,128]{3,2,1,0:T(8,128)} %bitcast.6, bf16[2,4,256,256]{3,2,1,0:T(8,128)(2,1)} %constant.20.clone.pick_ref, bf16[32,256]{1,0:T(8,128)(2,1)} %constant.21.clone.mean_ref, bf16[256,256]{1,0:T(8,128)(2,1)} %constant.22.clone.flip_ref, ...), custom_call_target="tpu_custom_call" | custom-call | flops 3019898880 | bytes 19005440 | tf_op jit(solution)/shard_map/synthesis/pallas_call | solution.py:413
  67.6 3.4 %all-to-all-start.1 = ((f32[4,2,5248]{2,1,0:T(2,128)}), f32[4,2,5248]{2,1,0:T(2,128)S(1)}, u32[]{:S(2)}, u32[]{:S(2)}) async-start(f32[4,2,5248]{2,1,0:T(2,128)} %synthesis.1), calls=%async_computation.1 | async-start | bytes 335872 | tf_op jit(solution)/shard_map/all_to_all | solution.py:449
  71.0 0.0 copy-done.3
  71.0 0.1 pad_add_fusion
  71.1 0.1 dynamic_slice.3
  71.2 4.8 %all-to-all-done.1 = f32[4,2,5248]{2,1,0:T(2,128)S(1)} async-done(((f32[4,2,5248]{2,1,0:T(2,128)}), f32[4,2,5248]{2,1,0:T(2,128)S(1)}, u32[]{:S(2)}, u32[]{:S(2)}) %all-to-all-start.1) | async-done | bytes 167968 | tf_op jit(solution)/shard_map/all_to_all | solution.py:449
  76.0 0.1 reshape.55
  76.1 0.0 copy-done.1
  76.1 0.8 subtract_select_fusion
  (1 shorter events, 0.0 us)
Async XLA Ops:
  0.0 35.8 %copy-start.2 = (s32[1280]{0:T(1024)S(1)}, s32[1280]{0:T(1024)}, u32[]{:S(2)}) copy-start(s32[1280]{0:T(1024)} %wave_map.1) | copy-start | bytes 15364
  15.6 4.2 %collective-permute-start = (f32[32,40,128]{2,1,0:T(8,128)}, f32[32,40,128]{2,1,0:T(8,128)S(1)}, u32[]{:S(2)}, u32[]{:S(2)}) collective-permute-start(f32[32,40,128]{2,1,0:T(8,128)} %get-tuple-element.11), channel_id=1, source_target_pairs={{1,0},{2,1},{3,2},{5,4},{6,5},{7,6},{9,8},{10,9},{11,10},{13,12},{... | collective-permute-start | bytes 1966088 | tf_op jit(solution)/shard_map/ppermute | solution.py:443
  21.8 31.9 %all-to-all-start = ((f32[32,40,128]{2,1,0:T(8,128)}), f32[32,40,128]{2,1,0:T(8,128)S(1)}, u32[]{:S(2)}, u32[]{:S(2)}) async-start(f32[32,40,128]{2,1,0:T(8,128)} %add.7), calls=%async_computation | async-start | bytes 1310720 | tf_op jit(solution)/shard_map/all_to_all | solution.py:444
  53.7 0.8 %copy-start = (f32[32,40,128]{2,1,0:T(8,128)}, f32[32,40,128]{2,1,0:T(8,128)S(1)}, u32[]{:S(2)}) copy-start(f32[32,40,128]{2,1,0:T(8,128)S(1)} %all-to-all-done) | copy-start | bytes 1966084
  54.6 16.5 %copy-start.3 = (s32[32]{0:T(128)S(1)}, s32[32]{0:T(128)}, u32[]{:S(2)}) copy-start(s32[32]{0:T(128)} %points_ref.3) | copy-start | bytes 388
  54.6 21.6 %copy-start.1 = (f32[1,8,5248]{2,1,0:T(8,128)S(1)}, f32[1,8,5248]{2,1,0:T(8,128)}, u32[]{:S(2)}) copy-start(f32[1,8,5248]{2,1,0:T(8,128)} %param.16) | copy-start | bytes 503812
  67.6 8.4 %all-to-all-start.1 = ((f32[4,2,5248]{2,1,0:T(2,128)}), f32[4,2,5248]{2,1,0:T(2,128)S(1)}, u32[]{:S(2)}, u32[]{:S(2)}) async-start(f32[4,2,5248]{2,1,0:T(2,128)} %synthesis.1), calls=%async_computation.1 | async-start | bytes 335872 | tf_op jit(solution)/shard_map/all_to_all | solution.py:449

commit v2 on v1

--- a/solution.py
+++ b/solution.py
@@ -22,10 +22,13 @@
 STEP_SLOTS = 2
 DEPTH = 3
 HALF_M = M // 2
-KPTS = 768
+KPTS = 672
+KPAD = 768
 KBLK = 256
+TABLE_STEPS = 7
+PERM_ROWS = 128
 BUF = 1536
-VMEM_LIMIT = 56 * 1024 * 1024
+MIB = 1024 * 1024
 F32 = jnp.float32
 BF16 = jnp.bfloat16
 
@@ -35,12 +38,12 @@
 
 
 def legendre_kernel(
-    wave_map, brackets, weight_ref, spec_hbm, leg_hbm, own_ref, prev_ref,
+    first_group, count, wave_map, brackets, weight_ref, spec_hbm, leg_hbm, own_ref, prev_ref,
     low_buf, up_buf, first_buf, leg_buf, own_rows, prev_rows, sems,
 ):
     groups = spec_hbm.shape[1]
     slots = SQ * groups
-    steps = groups // STEP_SLOTS
+    steps = count // STEP_SLOTS
     half = leg_hbm.shape[2]
     width = STEP_SLOTS * 2 * half
     wave = lax.axis_index("wave")
@@ -60,12 +63,13 @@
     def columns_copy(step, level, buf, kind):
         slot = step % DEPTH
         rows = pl.ds(pl.multiple_of(level * PART, PART), PART)
-        src = spec_hbm.at[:, pl.ds(step * STEP_SLOTS, STEP_SLOTS), rows, :]
+        src = spec_hbm.at[:, pl.ds(first_group + step * STEP_SLOTS, STEP_SLOTS), rows, :]
         return pltpu.make_async_copy(src, buf.at[slot], sems.at[slot, kind])
 
     def values_copy(step):
         slot = step % DEPTH
-        return pltpu.make_async_copy(leg_hbm.at[:, pl.ds(step * STEP_SLOTS, STEP_SLOTS)], leg_buf.at[slot], sems.at[slot, 3])
+        src = leg_hbm.at[:, pl.ds(first_group + step * STEP_SLOTS, STEP_SLOTS)]
+        return pltpu.make_async_copy(src, leg_buf.at[slot], sems.at[slot, 3])
 
     def fetch(step):
         values_copy(step).start()
@@ -116,7 +120,7 @@
             for a in range(2):
                 sq = 2 * pair + a
                 for b in range(STEP_SLOTS):
-                    m = wave_map[wave * slots + sq * groups + step * STEP_SLOTS + b]
+                    m = wave_map[wave * slots + sq * groups + first_group + step * STEP_SLOTS + b]
                     orders.append(m)
                     kept = jnp.where(degree >= m, 1.0, 0.0).astype(BF16)
                     plain = [leg_buf[slot, sq, b, i : i + 16, :] * kept for i in range(0, half, 16)]
@@ -147,51 +151,57 @@
     lax.fori_loop(0, steps, step_body, 0)
     rows = 2 * half
     for rows_ref, ref in ((own_rows, own_ref), (prev_rows, prev_ref)):
-        rows_dev = ref.shape[1] // groups
+        rows_dev = ref.shape[1] // count
         for r in range(rows):
-            ref[r // rows_dev, (r % rows_dev) * groups : (r % rows_dev + 1) * groups, :] = rows_ref[pl.ds(r, groups, stride=rows), :]
-
-
-def legendre_sums(spectral, legendre, wave_map, brackets, lev_weight):
+            at = (r % rows_dev) * count
+            ref[r // rows_dev, at : at + count, :] = rows_ref[pl.ds(r, count, stride=rows), :]
+
+
+def legendre_sums(first_group, count, spectral, legendre, wave_map, brackets, lev_weight):
     slots, cols, _ = spectral.shape
     half = legendre.shape[1]
     groups = slots // SQ
     spec = spectral.reshape(SQ, groups, cols, NT)
     leg = legendre.reshape(SQ, groups, half, NT)
     devices = lax.axis_size("wave") * lax.axis_size("lev")
-    out = jax.ShapeDtypeStruct((devices, 2 * half // devices * groups, SQ * PART), F32)
+    out = jax.ShapeDtypeStruct((devices, 2 * half // devices * count, SQ * PART), F32)
     smem = pl.BlockSpec(memory_space=pltpu.SMEM)
     vmem = pl.BlockSpec(memory_space=pltpu.VMEM)
-    anywhere = pl.BlockSpec(memory_space=pl.ANY)
+    anywhere = pl.BlockSpec(memory_space=pltpu.HBM)
     return pl.pallas_call(
-        legendre_kernel,
+        functools.partial(legendre_kernel, first_group, count),
         out_shape=[out, out],
         in_specs=[smem, smem, smem, anywhere, anywhere],
         out_specs=[vmem, vmem],
         scratch_shapes=[pltpu.VMEM((DEPTH, SQ, STEP_SLOTS, PART, NT), BF16)] * 3
         + [pltpu.VMEM((DEPTH, SQ, STEP_SLOTS, half, NT), BF16)]
-        + [pltpu.VMEM((groups * 2 * half, SQ * PART), F32)] * 2
+        + [pltpu.VMEM((count * 2 * half, SQ * PART), F32)] * 2
         + [pltpu.SemaphoreType.DMA((DEPTH, 4))],
-        compiler_params=pltpu.CompilerParams(vmem_limit_bytes=VMEM_LIMIT),
-        cost_estimate=pl.CostEstimate(flops=2 * slots * 2 * half * 48 * NT, bytes_accessed=slots * NT * 2 * (48 + half), transcendentals=0),
+        compiler_params=pltpu.CompilerParams(vmem_limit_bytes=(24 if half < 64 else 40) * MIB),
+        cost_estimate=pl.CostEstimate(
+            flops=2 * SQ * count * 2 * half * 48 * NT, bytes_accessed=SQ * count * NT * 2 * (48 + half), transcendentals=0
+        ),
         name="legendre_sums",
-    )(wave_map, brackets, lev_weight, spec, leg)
-
-
-def unit_circle(product, quarter):
-    turn = jnp.round(product * (1.0 / quarter))
-    rest = product - turn * quarter
-    x = rest * ((0.5 * math.pi) / quarter)
+    )(
+        wave_map, brackets, lev_weight,
+        pltpu.with_memory_space_constraint(spec, pltpu.HBM), pltpu.with_memory_space_constraint(leg, pltpu.HBM),
+    )
+
+
+def unit_circle(product, points, inverse):
+    big = 12582912.0
+    turn = (product * inverse + big) - big
+    x = (product - turn * points) * (math.pi * inverse)
     x2 = x * x
-    sine = x * (1.0 + x2 * (-1.0 / 6 + x2 * (1.0 / 120 + x2 * (-1.0 / 5040 + x2 * (1.0 / 362880)))))
-    cosine = 1.0 + x2 * (-0.5 + x2 * (1.0 / 24 + x2 * (-1.0 / 720 + x2 * (1.0 / 40320))))
-    quad = turn.astype(jnp.int32) & 3
-    odd = (quad & 1) == 1
-    c = jnp.where(odd, sine, cosine)
-    s = jnp.where(odd, cosine, sine)
-    c = jnp.where((quad == 1) | (quad == 2), -c, c)
-    s = jnp.where(quad >= 2, -s, s)
-    return c, s
+    sine = 0.0
+    cosine = 0.0
+    for power in (11, 9, 7, 5, 3, 1):
+        sine = sine * x2 + (-1) ** (power // 2) / math.factorial(power)
+    for power in (12, 10, 8, 6, 4, 2, 0):
+        cosine = cosine * x2 + (-1) ** (power // 2) / math.factorial(power)
+    sine = sine * x
+    twice = sine + sine
+    return 1.0 - twice * sine, twice * cosine
 
 
 def own_points(points_ref, r2):
@@ -205,53 +215,58 @@
     r2 = pl.program_id(0)
     kb = pl.program_id(1)
     rows = hi_ref.shape[1]
-    steps = pl.num_programs(1)
-    quarter = (own_points(points_ref, r2) // 4).astype(F32)
-    perm_rows = perm_ref.shape[0]
-    order = (r2 * steps + kb) * perm_rows + iota((perm_rows, 1), 0)
-    wanted = jnp.where(order < HALF_M, 2 * order, 2 * (order - HALF_M) + 1)
-    perm_ref[...] = jnp.where(map_ref[...] == wanted, 1.0, 0.0).astype(BF16)
-
-    def put(tile, chunk, value):
-        lanes = slice(tile * 128, tile * 128 + 128)
-        hi = value.astype(BF16)
-        hi_ref[0, pl.ds(chunk, 16), lanes] = hi
-        lo_ref[0, pl.ds(chunk, 16), lanes] = (value - hi.astype(F32)).astype(BF16)
+    points = own_points(points_ref, r2).astype(F32)
+    inverse = 1.0 / points
+    part = r2 * pl.num_programs(1) + kb
+
+    @pl.when(part < M // PERM_ROWS)
+    def _():
+        order = part * PERM_ROWS + iota((PERM_ROWS, 1), 0)
+        wanted = jnp.where(order < HALF_M, 2 * order, 2 * (order - HALF_M) + 1)
+        perm_ref[...] = jnp.where(map_ref[...] == wanted, 1.0, 0.0).astype(BF16)
+
+    lane = iota((16, 128), 1).astype(F32)
 
     def chunk_body(i, carry):
         chunk = pl.multiple_of(i * 16, 16)
+
+        def put(tile, value):
+            lanes = slice(tile * 128, tile * 128 + 128)
+            hi = value.astype(BF16)
+            hi_ref[0, pl.ds(chunk, 16), lanes] = hi
+            lo_ref[0, pl.ds(chunk, 16), lanes] = (value - hi.astype(F32)).astype(BF16)
+
         k = (kb * rows + chunk + iota((16, 128), 0)).astype(F32)
-        lane = iota((16, 128), 1).astype(F32)
-        c, s = unit_circle(2.0 * lane * k, quarter)
-        c1, s1 = unit_circle(k, quarter)
-        ct, st = unit_circle(256.0 * k, quarter)
+        c, s = unit_circle(2.0 * lane * k, points, inverse)
+        c1, s1 = unit_circle(k, points, inverse)
+        ct, st = unit_circle(256.0 * k, points, inverse)
         co = c * c1 - s * s1
         so = s * c1 + c * s1
         for t in range(HALF_M // 128):
             if t:
                 c, s = c * ct - s * st, s * ct + c * st
                 co, so = co * ct - so * st, so * ct + co * st
-            put(t, chunk, c)
-            put(5 + t, chunk, s)
-            put(10 + t, chunk, co)
-            put(15 + t, chunk, so)
+            put(t, c)
+            put(5 + t, s)
+            put(10 + t, co)
+            put(15 + t, so)
         return carry
 
-    lax.fori_loop(0, rows // 16, chunk_body, 0, unroll=2)
+    lax.fori_loop(0, rows // 16, chunk_body, 0, unroll=True)
 
 
 def tables(row_points, slot_map):
-    steps = 8
-    rows = KPTS // steps
+    rows = KPTS // TABLE_STEPS
     table = jax.ShapeDtypeStruct((2, KPTS, 2 * M), BF16)
     table_spec = pl.BlockSpec((1, rows, 2 * M), lambda r, k: (r, k, 0))
+    perm_spec = pl.BlockSpec((PERM_ROWS, M), lambda r, k: (jnp.minimum(r * TABLE_STEPS + k, M // PERM_ROWS - 1), 0))
     return pl.pallas_call(
         table_kernel,
         out_shape=[table, table, jax.ShapeDtypeStruct((M, M), BF16)],
-        grid=(2, steps),
+        grid=(2, TABLE_STEPS),
         in_specs=[pl.BlockSpec(memory_space=pltpu.SMEM), pl.BlockSpec(memory_space=pltpu.VMEM)],
-        out_specs=[table_spec, table_spec, pl.BlockSpec((M // (2 * steps), M), lambda r, k: (r * steps + k, 0))],
-        compiler_params=pltpu.CompilerParams(vmem_limit_bytes=VMEM_LIMIT),
+        out_specs=[table_spec, table_spec, perm_spec],
+        compiler_params=pltpu.CompilerParams(vmem_limit_bytes=16 * MIB),
         cost_estimate=pl.CostEstimate(flops=2 * KPTS * 2 * M * 12, bytes_accessed=2 * KPTS * 2 * M * 4 + M * M * 2, transcendentals=0),
         name="fourier_tables",
     )(row_points, slot_map)
@@ -307,25 +322,20 @@
     return jnp.dot(a, b, preferred_element_type=F32)
 
 
-def synth_kernel(
-    points_ref, moved_ref, pick_ref, mean_ref, flip_ref, perm_hbm, hi_hbm, lo_hbm, out_ref,
-    perm_ref, hi_ref, lo_ref, mixed, coef, direct, mirror, line, sems,
-):
-    waves, plev, block_rows, _ = moved_ref.shape
-    sub = block_rows // 2
+def synth_kernel(parts, points_ref, *refs):
+    moved_refs = refs[:parts]
+    pick_ref, mean_ref, flip_ref, perm_ref, hi_ref, lo_ref, out_ref = refs[parts : parts + 7]
+    mixed, coef, flat, mirror, line = refs[parts + 7 :]
+    waves, plev, _, _ = moved_refs[0].shape
     wide = plev * 2 * PART
-    part_rows = waves * sub
-    copies = [pltpu.make_async_copy(perm_hbm, perm_ref, sems.at[0])]
-    for r2 in range(2):
-        copies.append(pltpu.make_async_copy(hi_hbm.at[r2], hi_ref.at[r2], sems.at[1 + 2 * r2]))
-        copies.append(pltpu.make_async_copy(lo_hbm.at[r2], lo_ref.at[r2], sems.at[2 + 2 * r2]))
-    for copy in copies:
-        copy.start()
-
+    part_rows = M // SQ
     for base in range(0, plev * 2, 8):
         cur = []
         for g in range(base, base + 8):
-            pieces = [moved_ref[w, g // 2, (g % 2) * sub : (g % 2 + 1) * sub, :] for w in range(waves)]
+            pieces = []
+            for ref in moved_refs:
+                sub = ref.shape[2] // 2
+                pieces += [ref[w, g // 2, (g % 2) * sub : (g % 2 + 1) * sub, :] for w in range(waves)]
             cur.append(jnp.concatenate(pieces, axis=0))
         group = iota((part_rows, 128), 1) // PART
         for bit in (1, 2, 4):
@@ -350,7 +360,6 @@
     place = iota((HALF_M, 1), 0)
     turned = (iota((1, 2 * wide), 1) % wide) // (plev * FS) >= 2
     flip_sign = jnp.where(turned & (place % 2 == 1), -1.0, 1.0).astype(BF16)
-    copies[0].wait()
     for odd in range(2):
         ordered = nn_dot(perm_ref[odd * HALF_M : (odd + 1) * HALF_M, :], mixed[...])
         wave = 2 * place + odd
@@ -360,13 +369,10 @@
             for part in range(2):
                 picked = nn_dot(ordered, pick_ref[row, odd * 2 + part]).astype(BF16)
                 coef[row, odd, part * HALF_M : (part + 1) * HALF_M, :] = picked * flip_sign
-    direct[...] = jnp.zeros_like(direct)
+    flat[...] = jnp.zeros_like(flat)
     mirror[...] = jnp.zeros_like(mirror)
 
     for r2 in range(2):
-        copies[1 + 2 * r2].wait()
-        copies[2 + 2 * r2].wait()
-
         def contraction(odd):
             lanes = slice(odd * M, (odd + 1) * M)
             both = nn_dot(hi_ref[r2, :, lanes], coef[r2, odd])
@@ -381,55 +387,49 @@
         sq_hi, sq_lo = split(squares)
         energy = nt_dot(mean_ref[...], sq_hi) + nt_dot(mean_ref[...], sq_lo)
         rows = 4 * plev
-        direct[:, :KPTS] = energy[:rows]
-        en_hi, en_lo = split(energy[rows:])
-        for t in range(KPTS // KBLK):
+        flat[:, :KPTS] = energy
+        en_hi, en_lo = split(flat[rows:, :KPAD])
+        for t in range(KPAD // KBLK):
             lanes = slice(t * KBLK, (t + 1) * KBLK)
-            back = KPTS - (t + 1) * KBLK
+            back = KPAD - (t + 1) * KBLK
             mirror[:, back : back + KBLK] = nn_dot(en_hi[:, lanes], flip_ref[...]) + nn_dot(en_lo[:, lanes], flip_ref[...])
 
         quarter = own_points(points_ref, r2) // 4
         lane = iota((rows, BUF), 1)
-        shift = (quarter + (BUF - (KPTS - 1))) % BUF
-        whole = jnp.where(lane <= quarter // 2, direct[...], pltpu.roll(mirror[...], shift, 1))
-        direct[...] = whole
+        shift = (quarter + (BUF - (KPAD - 1))) % BUF
+        flat[:rows, :] = jnp.where(lane <= quarter // 2, flat[:rows, :], pltpu.roll(mirror[...], shift, 1))
         line[...] = jnp.zeros_like(line)
         lane = iota((plev, BUF), 1)
         for b in range(4):
             start = quarter * b
             inner = start % 128
             base = pl.multiple_of(start - inner, 128)
-            piece = pltpu.roll(direct[b * plev : (b + 1) * plev, :], inner, 1)
+            piece = pltpu.roll(flat[b * plev : (b + 1) * plev, :], inner, 1)
             old = line[:, pl.ds(base, BUF)]
             line[:, pl.ds(base, BUF)] = jnp.where((lane >= inner) & (lane < inner + quarter), piece, old)
         out_ref[:, pl.ds(r2, 1), :] = line[:, :ROWPAD].reshape(plev, 1, ROWPAD)
 
 
 def synthesis(moved, perm, table_hi, table_lo, row_points):
-    waves, plev, block_rows, _ = moved.shape
+    plev = moved[0].shape[1]
     wide = plev * 2 * PART
     vmem = pl.BlockSpec(memory_space=pltpu.VMEM)
-    anywhere = pl.BlockSpec(memory_space=pl.ANY)
     return pl.pallas_call(
-        synth_kernel,
+        functools.partial(synth_kernel, len(moved)),
         out_shape=jax.ShapeDtypeStruct((plev, 2, ROWPAD), F32),
-        in_specs=[pl.BlockSpec(memory_space=pltpu.SMEM), vmem, vmem, vmem, vmem, anywhere, anywhere, anywhere],
+        in_specs=[pl.BlockSpec(memory_space=pltpu.SMEM)] + [vmem] * (len(moved) + 6),
         out_specs=vmem,
         scratch_shapes=[
-            pltpu.VMEM((M, M), BF16),
-            pltpu.VMEM((2, KPTS, 2 * M), BF16),
-            pltpu.VMEM((2, KPTS, 2 * M), BF16),
             pltpu.VMEM((M, 2 * wide), BF16),
             pltpu.VMEM((2, 2, M, 2 * wide), BF16),
-            pltpu.VMEM((4 * plev, BUF), F32),
+            pltpu.VMEM((8 * plev, BUF), F32),
             pltpu.VMEM((4 * plev, BUF), F32),
             pltpu.VMEM((plev, 3 * 1280 + BUF), F32),
-            pltpu.SemaphoreType.DMA((5,)),
         ],
-        compiler_params=pltpu.CompilerParams(vmem_limit_bytes=VMEM_LIMIT),
+        compiler_params=pltpu.CompilerParams(vmem_limit_bytes=(20 if plev <= 4 else 32) * MIB),
         cost_estimate=pl.CostEstimate(flops=2 * 2 * KPTS * 2 * M * 384, bytes_accessed=2 * KPTS * 2 * M * 4 + M * M * 2, transcendentals=0),
         name="synthesis",
-    )(row_points, moved, pick_tables(plev), mean_table(plev), flip_table(), perm, table_hi, table_lo)
+    )(row_points, *moved, pick_tables(plev), mean_table(plev), flip_table(), perm, table_hi, table_lo)
 
 
 def local(spectral, legendre, wave_map, row_points, brackets, lev_weight, climatology):
@@ -439,12 +439,23 @@
     wave_count = lax.axis_size("wave")
     lev_count = lax.axis_size("lev")
     rows_dev = 2 * half // (wave_count * lev_count)
-    own, prev = legendre_sums(spectral, legendre, wave_map, brackets, lev_weight)
-    from_next = lax.ppermute(prev, "lev", [(d, d - 1) for d in range(1, lev_count)])
-    moved = lax.all_to_all(own + from_next, ("wave", "lev"), split_axis=0, concat_axis=0, tiled=True)
-    moved = moved.reshape(wave_count, lev_count, rows_dev * groups, SQ * PART)
-    slot_map = jnp.transpose(wave_map.reshape(wave_count, SQ, groups), (1, 0, 2)).reshape(1, M)
-    table_hi, table_lo, perm = tables(row_points, slot_map)
+    cuts = (0, 12, groups) if groups >= 16 else (0, groups)
+    own_maps = wave_map.reshape(wave_count, SQ, groups)
+    moved, maps, sent = [], [], []
+    order = wave_map
+    for start, stop in zip(cuts[:-1], cuts[1:]):
+        own, prev = legendre_sums(start, stop - start, spectral, legendre, order, brackets, lev_weight)
+        order, prev = lax.optimization_barrier((wave_map, prev))
+        if sent:
+            prev, _ = lax.optimization_barrier((prev, sent[-1]))
+        from_next = lax.ppermute(prev, "lev", [(d, d - 1) for d in range(1, lev_count)])
+        sent.append(own + from_next)
+        part = lax.all_to_all(sent[-1], ("wave", "lev"), split_axis=0, concat_axis=0, tiled=True)
+        moved.append(part.reshape(wave_count, lev_count, rows_dev * (stop - start), SQ * PART))
+        maps.append(jnp.transpose(own_maps[:, :, start:stop], (1, 0, 2)).reshape(SQ, wave_count * (stop - start)))
+    slot_map = jnp.concatenate(maps, axis=1).reshape(1, M)
+    table_points, _ = lax.optimization_barrier((row_points, sent))
+    table_hi, table_lo, perm = tables(table_points, slot_map)
     energy = synthesis(moved, perm, table_hi, table_lo, row_points)
     result = lax.all_to_all(energy, "lev", split_axis=0, concat_axis=0, tiled=True)
     result = result.reshape(1, rows_dev * lev_count, ROWPAD)

time: 77.2 us -> 93.9 us (1.22)
  local copies, waits for them, and re-layouts: 1.86 us -> 20.6 us
  Pallas kernels: 43.1 us -> 33.7 us
  starting transfers between devices: 18.6 us -> 24.2 us
  other arithmetic: 2.83 us -> 4.09 us
    unnamed x8 -> x38, local copies, waits for them, and re-layouts: 0.85 us -> 19.4 us
    pallas_call x1, Pallas kernels: 14.4 us -> 8.02 us  [tables(): pl.pallas_call(table_kernel, out_shape=[table, table, jax.ShapeDtypeStruc...]
    all_to_all x1 -> x2, starting transfers between devices: 13.9 us -> 18.3 us  [local(): lax.all_to_all(sent[-1], ('wave', 'lev'), split_axis=0, concat_axis=0, ti...]
    pallas_call x2 -> x3, Pallas kernels: 28.7 us -> 25.7 us  [the longest x2 16.9 us: legendre_sums(): pl.pallas_call(functools.partial(legendre_kernel, first_group, count), ou...]
    ppermute x1 -> x2, waiting for transfers between devices: 2.9 us -> 4.34 us  [local(): lax.ppermute(prev, 'lev', [(d, d - 1) for d in range(1, lev_count)])]
    ppermute x1 -> x2, starting transfers between devices: 1.29 us -> 2.58 us  [local(): lax.ppermute(prev, 'lev', [(d, d - 1) for d in range(1, lev_count)])]
    all_to_all x1 -> x2, waiting for transfers between devices: 2.64 us -> 1.73 us  [local(): lax.all_to_all(sent[-1], ('wave', 'lev'), split_axis=0, concat_axis=0, ti...]
    add x1 -> x2, other arithmetic: 2 us -> 1.54 us  [local(): sent.append(own + from_next)]
  transfers between devices with their start and end apart: 3 -> 5, of which waited for: 3 -> 4; matrix products, arithmetic and copies ran while one was open for 1% -> 3% of each run, Pallas kernels for 19% -> 16%
where the time goes in v2:
time: 93.9 us; the launch traced here: 93 us
  Pallas kernels  33.7 us (36%)
  starting transfers between devices  24.2 us (26%)
  local copies, waits for them, and re-layouts  20.6 us (22%)
  waiting for transfers between devices  10.2 us (11%)
  other arithmetic  4.09 us (4%)
    unnamed x38, local copies, waits for them, and re-layouts  19.4 us
    all_to_all x2, starting transfers between devices, local(): lax.all_to_all(sent[-1], ('wave', 'lev'), split_axis=0, concat_axis=0, ti...  18.3 us
    pallas_call x2, Pallas kernels, legendre_sums(): pl.pallas_call(functools.partial(legendre_kernel, first_group, count), ou...  16.9 us
    pallas_call x1, Pallas kernels, synthesis(): pl.pallas_call(functools.partial(synth_kernel, len(moved)), out_shape=jax...  8.81 us
    pallas_call x1, Pallas kernels, tables(): pl.pallas_call(table_kernel, out_shape=[table, table, jax.ShapeDtypeStruc...  8.02 us
    ppermute x2, waiting for transfers between devices, local(): lax.ppermute(prev, 'lev', [(d, d - 1) for d in range(1, lev_count)])  4.34 us
    all_to_all x1, waiting for transfers between devices, local(): lax.all_to_all(energy, 'lev', split_axis=0, concat_axis=0, tiled=True)  4.1 us
    all_to_all x1, starting transfers between devices, local(): lax.all_to_all(energy, 'lev', split_axis=0, concat_axis=0, tiled=True)  3.35 us
  transfers between devices with their start and end apart: 5, of which 4 were waited for; matrix products, arithmetic and copies ran while one was open for 3% of the time, Pallas kernels for 16%

profile of v2, /device:TPU:0, one launch (start us, length us, event | category | flops | bytes accessed | tf_op | source)
XLA Modules:
  0.0 93.0 jit_solution(5690154652161442999)
XLA Ops:
  0.0 0.7 copy-done.9
  0.7 0.7 copy-done.13
  1.4 0.7 copy-done.15
  2.0 9.6 %legendre_sums.2 = (f32[32,24,128]{2,1,0:T(8,128)S(1)}, f32[32,24,128]{2,1,0:T(8,128)S(1)}) custom-call(s32[1280]{0:T(1024)S(1)} %copy-done.9, s32[4]{0:T(128)S(1)} %copy-done.13, f32[4]{0:T(128)S(1)} %copy-done.15, bf16[8,20,64,1280]{3,2,1,0:T(8,128)(2,1)} %bitcast.10, bf16[8,20,32,1280]{3,2,1,0:T(8,128)(2,1)} %bitcast.12), custom_call_target="tpu_custom_call" | custom-call | flops 754974720 | bytes 19660800 | tf_op jit(solution)/shard_map/legendre_sums/pallas_call | solution.py:171
  11.6 1.3 %collective-permute-start = (f32[32,24,128]{2,1,0:T(8,128)S(1)}, f32[32,24,128]{2,1,0:T(8,128)S(1)}, u32[]{:S(2)}, u32[]{:S(2)}) collective-permute-start(f32[32,24,128]{2,1,0:T(8,128)S(1)} %get-tuple-element.19), channel_id=1, source_target_pairs={{1,0},{2,1},{3,2},{5,4},{6,5},{7,6},{9,8},{10,9},{11,10},{13,12},{... | collective-permute-start | bytes 1179656 | tf_op jit(solution)/shard_map/ppermute | solution.py:451
  12.9 2.3 %collective-permute-done = f32[32,24,128]{2,1,0:T(8,128)S(1)} collective-permute-done((f32[32,24,128]{2,1,0:T(8,128)S(1)}, f32[32,24,128]{2,1,0:T(8,128)S(1)}, u32[]{:S(2)}, u32[]{:S(2)}) %collective-permute-start) | collective-permute-done | bytes 393248 | tf_op jit(solution)/shard_map/ppermute | solution.py:451
  15.3 0.8 add.10
  16.1 11.3 %all-to-all-start = ((f32[32,24,128]{2,1,0:T(8,128)}), f32[32,24,128]{2,1,0:T(8,128)S(1)}, u32[]{:S(2)}, u32[]{:S(2)}) async-start(f32[32,24,128]{2,1,0:T(8,128)} %add.10), calls=%async_computation | async-start | bytes 786432 | tf_op jit(solution)/shard_map/all_to_all | solution.py:453
  27.4 0.0 copy-done.10
  27.4 0.0 copy-done.14
  27.4 0.0 copy-done.16
  27.4 0.0 copy-start.11
  27.4 7.2 %legendre_sums.3 = (f32[32,16,128]{2,1,0:T(8,128)S(1)}, f32[32,16,128]{2,1,0:T(8,128)S(1)}) custom-call(s32[1280]{0:T(1024)S(1)} %copy-done.10, s32[4]{0:T(128)S(1)} %copy-done.14, f32[4]{0:T(128)S(1)} %copy-done.16, bf16[8,20,64,1280]{3,2,1,0:T(8,128)(2,1)} %bitcast.11, bf16[8,20,32,1280]{3,2,1,0:T(8,128)(2,1)} %bitcast.13), custom_call_target="tpu_custom_call" | custom-call | flops 503316480 | bytes 13107200 | tf_op jit(solution)/shard_map/legendre_sums/pallas_call | solution.py:171
  34.7 1.3 %collective-permute-start.1 = (f32[32,16,128]{2,1,0:T(8,128)S(1)}, f32[32,16,128]{2,1,0:T(8,128)S(1)}, u32[]{:S(2)}, u32[]{:S(2)}) collective-permute-start(f32[32,16,128]{2,1,0:T(8,128)S(1)} %get-tuple-element.24), channel_id=1, source_target_pairs={{1,0},{2,1},{3,2},{5,4},{6,5},{7,6},{9,8},{10,9},{11,10},{13,12},{... | collective-permute-start | bytes 786440 | tf_op jit(solution)/shard_map/ppermute | solution.py:451
  36.0 0.1 reshape.65
  36.1 2.0 %collective-permute-done.1 = f32[32,16,128]{2,1,0:T(8,128)S(1)} collective-permute-done((f32[32,16,128]{2,1,0:T(8,128)S(1)}, f32[32,16,128]{2,1,0:T(8,128)S(1)}, u32[]{:S(2)}, u32[]{:S(2)}) %collective-permute-start.1) | collective-permute-done | bytes 262176 | tf_op jit(solution)/shard_map/ppermute | solution.py:451
  38.1 0.7 add.11
  38.8 1.7 %all-to-all-done = f32[32,24,128]{2,1,0:T(8,128)S(1)} async-done(((f32[32,24,128]{2,1,0:T(8,128)}), f32[32,24,128]{2,1,0:T(8,128)S(1)}, u32[]{:S(2)}, u32[]{:S(2)}) %all-to-all-start) | async-done | bytes 393248 | tf_op jit(solution)/shard_map/all_to_all | solution.py:453
  40.6 7.0 %all-to-all-start.1 = ((f32[32,16,128]{2,1,0:T(8,128)}), f32[32,16,128]{2,1,0:T(8,128)S(1)}, u32[]{:S(2)}, u32[]{:S(2)}) async-start(f32[32,16,128]{2,1,0:T(8,128)} %add.11), calls=%async_computation.1 | async-start | bytes 524288 | tf_op jit(solution)/shard_map/all_to_all | solution.py:453
  47.6 0.1 slice_bitcast_fusion
  47.6 0.1 reshape.67
  47.7 0.1 reshape.66
  47.8 0.1 pad_add_fusion
  47.9 0.0 copy-done.4
  47.9 0.7 reshape.68.map_ref
  48.6 0.7 copy-done.12
  49.3 0.7 copy-done.17
  49.9 8.0 %fourier_tables.1 = (bf16[2,672,2560]{2,1,0:T(8,128)(2,1)S(1)}, bf16[2,672,2560]{2,1,0:T(8,128)(2,1)S(1)}, bf16[1280,1280]{1,0:T(8,128)(2,1)S(1)}) custom-call(s32[32]{0:T(128)S(1)} %copy-done.17, s32[1,1280]{1,0:T(1,128)S(1)} %copy-done.12), custom_call_target="tpu_custom_call" | custom-call | flops 41287680 | bytes 17039360 | tf_op jit(solution)/shard_map/fourier_tables/pallas_call | solution.py:263
  58.0 0.0 copy-start
  58.0 2.8 %copy-done = bf16[2,672,2560]{2,1,0:T(8,128)(2,1)} copy-done((bf16[2,672,2560]{2,1,0:T(8,128)(2,1)}, bf16[2,672,2560]{2,1,0:T(8,128)(2,1)S(1)}, u32[]{:S(2)}) %copy-start) | copy-done | bytes 6881304
  60.8 2.9 %copy-done.2 = bf16[2,672,2560]{2,1,0:T(8,128)(2,1)} copy-done((bf16[2,672,2560]{2,1,0:T(8,128)(2,1)}, bf16[2,672,2560]{2,1,0:T(8,128)(2,1)S(1)}, u32[]{:S(2)}) %copy-start.2) | copy-done | bytes 6881304
  63.7 0.0 all-to-all-done.1
  63.7 0.0 copy-done.11
  63.7 3.0 %copy-done.1 = bf16[2,672,2560]{2,1,0:T(8,128)(2,1)S(1)} copy-done((bf16[2,672,2560]{2,1,0:T(8,128)(2,1)S(1)}, bf16[2,672,2560]{2,1,0:T(8,128)(2,1)}, u32[]{:S(2)}) %copy-start.1) | copy-done | bytes 6881304
  66.6 3.0 %copy-done.3 = bf16[2,672,2560]{2,1,0:T(8,128)(2,1)S(1)} copy-done((bf16[2,672,2560]{2,1,0:T(8,128)(2,1)S(1)}, bf16[2,672,2560]{2,1,0:T(8,128)(2,1)}, u32[]{:S(2)}) %copy-start.3) | copy-done | bytes 6881304
  69.6 1.0 %copy-done.5 = f32[32,24,128]{2,1,0:T(8,128)S(1)} copy-done((f32[32,24,128]{2,1,0:T(8,128)S(1)}, f32[32,24,128]{2,1,0:T(8,128)}, u32[]{:S(2)}) %copy-start.5) | copy-done | bytes 393240
  70.6 1.2 %copy-done.6 = bf16[2,4,256,256]{3,2,1,0:T(8,128)(2,1)S(1)} copy-done((bf16[2,4,256,256]{3,2,1,0:T(8,128)(2,1)S(1)}, bf16[2,4,256,256]{3,2,1,0:T(8,128)(2,1)}, u32[]{:S(2)}) %copy-start.6) | copy-done | bytes 1048600
  71.8 0.9 copy-done.8
  72.7 0.7 copy-done.18
  73.4 8.8 %synthesis.1 = f32[4,2,5248]{2,1,0:T(2,128)S(1)} custom-call(s32[32]{0:T(128)S(1)} %copy-done.18, f32[8,4,24,128]{3,2,1,0:T(8,128)S(1)} %bitcast.8, f32[8,4,16,128]{3,2,1,0:T(8,128)S(1)} %bitcast.9, bf16[2,4,256,256]{3,2,1,0:T(8,128)(2,1)S(1)} %copy-done.6, bf16[32,256]{1,0:T(8,128)(2,1)S(1)} %copy-done.11, bf16[256,256]{1,0:T(8,128)(2,1)S(1)} %copy-done.8, ...), custom_call_target="tpu_custom_call" | custom-call | flops 2642411520 | bytes 17039360 | tf_op jit(solution)/shard_map/synthesis/pallas_call | solution.py:417
  82.2 0.0 copy-start.7
  82.2 0.7 copy-done.7
  82.9 3.3 %all-to-all-start.2 = ((f32[4,2,5248]{2,1,0:T(2,128)}), f32[4,2,5248]{2,1,0:T(2,128)S(1)}, u32[]{:S(2)}, u32[]{:S(2)}) async-start(f32[4,2,5248]{2,1,0:T(2,128)} %copy-done.7), calls=%async_computation.2 | async-start | bytes 335872 | tf_op jit(solution)/shard_map/all_to_all | solution.py:460
  86.2 0.8 pad_add_fusion.1
  87.0 0.1 dynamic_slice.3
  87.1 4.1 %all-to-all-done.2 = f32[4,2,5248]{2,1,0:T(2,128)S(1)} async-done(((f32[4,2,5248]{2,1,0:T(2,128)}), f32[4,2,5248]{2,1,0:T(2,128)S(1)}, u32[]{:S(2)}, u32[]{:S(2)}) %all-to-all-start.2) | async-done | bytes 167968 | tf_op jit(solution)/shard_map/all_to_all | solution.py:460
  91.2 0.1 reshape.69
  91.3 1.7 %subtract_select_fusion = f32[1,8,5248]{2,1,0:T(8,128)} fusion(f32[1,8,5248]{2,1,0:T(8,128)S(1)} %reshape.69, f32[1,8,5248]{2,1,0:T(8,128)} %param.16, s32[8]{0:T(128)S(1)} %dynamic_slice.3), kind=kLoop, calls=%fused_computation | loop fusion | flops 125952 | bytes 503840 | tf_op jit(solution)/shard_map/jit(_where)/select_n | solution.py:467
  (19 shorter events, 0.0 us)
Async XLA Ops:
  0.0 0.7 copy-start.9
  0.7 0.7 copy-start.13
  1.4 0.7 copy-start.15
  2.0 25.4 %copy-start.10 = (s32[1280]{0:T(1024)S(1)}, s32[1280]{0:T(1024)}, u32[]{:S(2)}) copy-start(s32[1280]{0:T(1024)} %wave_map.2) | copy-start | bytes 15364
  2.0 25.4 %copy-start.14 = (s32[4]{0:T(128)S(1)}, s32[4]{0:T(128)}, u32[]{:S(2)}) copy-start(s32[4]{0:T(128)} %brackets.3) | copy-start | bytes 52
  2.0 25.4 %copy-start.16 = (f32[4]{0:T(128)S(1)}, f32[4]{0:T(128)}, u32[]{:S(2)}) copy-start(f32[4]{0:T(128)} %weight_ref.3) | copy-start | bytes 52
  11.6 3.6 %collective-permute-start = (f32[32,24,128]{2,1,0:T(8,128)S(1)}, f32[32,24,128]{2,1,0:T(8,128)S(1)}, u32[]{:S(2)}, u32[]{:S(2)}) collective-permute-start(f32[32,24,128]{2,1,0:T(8,128)S(1)} %get-tuple-element.19), channel_id=1, source_target_pairs={{1,0},{2,1},{3,2},{5,4},{6,5},{7,6},{9,8},{10,9},{11,10},{13,12},{... | collective-permute-start | bytes 1179656 | tf_op jit(solution)/shard_map/ppermute | solution.py:451
  16.1 24.5 %all-to-all-start = ((f32[32,24,128]{2,1,0:T(8,128)}), f32[32,24,128]{2,1,0:T(8,128)S(1)}, u32[]{:S(2)}, u32[]{:S(2)}) async-start(f32[32,24,128]{2,1,0:T(8,128)} %add.10), calls=%async_computation | async-start | bytes 786432 | tf_op jit(solution)/shard_map/all_to_all | solution.py:453
  27.4 36.2 %copy-start.11 = (bf16[32,256]{1,0:T(8,128)(2,1)S(1)}, bf16[32,256]{1,0:T(8,128)(2,1)}, u32[]{:S(2)}) copy-start(bf16[32,256]{1,0:T(8,128)(2,1)} %constant.21.clone.refs_3_) | copy-start | bytes 49156
  34.7 3.4 %collective-permute-start.1 = (f32[32,16,128]{2,1,0:T(8,128)S(1)}, f32[32,16,128]{2,1,0:T(8,128)S(1)}, u32[]{:S(2)}, u32[]{:S(2)}) collective-permute-start(f32[32,16,128]{2,1,0:T(8,128)S(1)} %get-tuple-element.24), channel_id=1, source_target_pairs={{1,0},{2,1},{3,2},{5,4},{6,5},{7,6},{9,8},{10,9},{11,10},{13,12},{... | collective-permute-start | bytes 786440 | tf_op jit(solution)/shard_map/ppermute | solution.py:451
  40.6 7.3 %copy-start.4 = (f32[32,24,128]{2,1,0:T(8,128)}, f32[32,24,128]{2,1,0:T(8,128)S(1)}, u32[]{:S(2)}) copy-start(f32[32,24,128]{2,1,0:T(8,128)S(1)} %all-to-all-done) | copy-start | bytes 1179652
  40.6 23.1 %all-to-all-start.1 = ((f32[32,16,128]{2,1,0:T(8,128)}), f32[32,16,128]{2,1,0:T(8,128)S(1)}, u32[]{:S(2)}, u32[]{:S(2)}) async-start(f32[32,16,128]{2,1,0:T(8,128)} %add.11), calls=%async_computation.1 | async-start | bytes 524288 | tf_op jit(solution)/shard_map/all_to_all | solution.py:453
  48.6 0.7 copy-start.12
  49.3 0.7 copy-start.17
  58.0 2.8 %copy-start = (bf16[2,672,2560]{2,1,0:T(8,128)(2,1)}, bf16[2,672,2560]{2,1,0:T(8,128)(2,1)S(1)}, u32[]{:S(2)}) copy-start(bf16[2,672,2560]{2,1,0:T(8,128)(2,1)S(1)} %get-tuple-element.27.refs_6_) | copy-start | bytes 20643844
  60.8 2.9 %copy-start.2 = (bf16[2,672,2560]{2,1,0:T(8,128)(2,1)}, bf16[2,672,2560]{2,1,0:T(8,128)(2,1)S(1)}, u32[]{:S(2)}) copy-start(bf16[2,672,2560]{2,1,0:T(8,128)(2,1)S(1)} %get-tuple-element.28.refs_7_) | copy-start | bytes 20643844
  63.7 3.0 %copy-start.1 = (bf16[2,672,2560]{2,1,0:T(8,128)(2,1)S(1)}, bf16[2,672,2560]{2,1,0:T(8,128)(2,1)}, u32[]{:S(2)}) copy-start(bf16[2,672,2560]{2,1,0:T(8,128)(2,1)} %copy-done) | copy-start | bytes 20643844
  66.6 3.0 %copy-start.3 = (bf16[2,672,2560]{2,1,0:T(8,128)(2,1)S(1)}, bf16[2,672,2560]{2,1,0:T(8,128)(2,1)}, u32[]{:S(2)}) copy-start(bf16[2,672,2560]{2,1,0:T(8,128)(2,1)} %copy-done.2) | copy-start | bytes 20643844
  69.6 1.0 %copy-start.5 = (f32[32,24,128]{2,1,0:T(8,128)S(1)}, f32[32,24,128]{2,1,0:T(8,128)}, u32[]{:S(2)}) copy-start(f32[32,24,128]{2,1,0:T(8,128)} %copy-done.4) | copy-start | bytes 1179652
  70.6 1.2 %copy-start.6 = (bf16[2,4,256,256]{3,2,1,0:T(8,128)(2,1)S(1)}, bf16[2,4,256,256]{3,2,1,0:T(8,128)(2,1)}, u32[]{:S(2)}) copy-start(bf16[2,4,256,256]{3,2,1,0:T(8,128)(2,1)} %constant.20.clone.refs_2_) | copy-start | bytes 3145732
  71.8 0.9 copy-start.8
  72.7 0.7 copy-start.18
  82.2 0.7 copy-start.7
  82.9 8.3 %all-to-all-start.2 = ((f32[4,2,5248]{2,1,0:T(2,128)}), f32[4,2,5248]{2,1,0:T(2,128)S(1)}, u32[]{:S(2)}, u32[]{:S(2)}) async-start(f32[4,2,5248]{2,1,0:T(2,128)} %copy-done.7), calls=%async_computation.2 | async-start | bytes 335872 | tf_op jit(solution)/shard_map/all_to_all | solution.py:460

commit v3 on v2

--- a/solution.py
+++ b/solution.py
@@ -60,40 +60,45 @@
     lane = iota((1, width), 1)
     south = lane % (2 * half) >= half
 
-    def columns_copy(step, level, buf, kind):
+    def columns_copy(step, pair, level, buf, kind):
         slot = step % DEPTH
         rows = pl.ds(pl.multiple_of(level * PART, PART), PART)
-        src = spec_hbm.at[:, pl.ds(first_group + step * STEP_SLOTS, STEP_SLOTS), rows, :]
-        return pltpu.make_async_copy(src, buf.at[slot], sems.at[slot, kind])
-
-    def values_copy(step):
+        here = pl.ds(first_group + step * STEP_SLOTS, STEP_SLOTS)
+        src = spec_hbm.at[pl.ds(2 * pair, 2), here, rows, :]
+        return pltpu.make_async_copy(src, buf.at[slot, pl.ds(2 * pair, 2)], sems.at[slot, pair, kind])
+
+    def values_copy(step, pair):
         slot = step % DEPTH
-        src = leg_hbm.at[:, pl.ds(first_group + step * STEP_SLOTS, STEP_SLOTS)]
-        return pltpu.make_async_copy(src, leg_buf.at[slot], sems.at[slot, 3])
+        here = pl.ds(first_group + step * STEP_SLOTS, STEP_SLOTS)
+        src = leg_hbm.at[pl.ds(2 * pair, 2), here]
+        return pltpu.make_async_copy(src, leg_buf.at[slot, pl.ds(2 * pair, 2)], sems.at[slot, pair, 3])
 
     def fetch(step):
-        values_copy(step).start()
-        columns_copy(step, lower, low_buf, 0).start()
+        for pair in range(SQ // 2):
+            values_copy(step, pair).start()
+            columns_copy(step, pair, lower, low_buf, 0).start()
 
         @pl.when(has_upper)
         def _():
-            columns_copy(step, lower + 1, up_buf, 1).start()
+            for pair in range(SQ // 2):
+                columns_copy(step, pair, lower + 1, up_buf, 1).start()
 
         @pl.when(crosses)
         def _():
-            columns_copy(step, 0, first_buf, 2).start()
-
-    def await_step(step):
-        values_copy(step).wait()
-        columns_copy(step, lower, low_buf, 0).wait()
+            for pair in range(SQ // 2):
+                columns_copy(step, pair, 0, first_buf, 2).start()
+
+    def await_pair(step, pair):
+        values_copy(step, pair).wait()
+        columns_copy(step, pair, lower, low_buf, 0).wait()
 
         @pl.when(has_upper)
         def _():
-            columns_copy(step, lower + 1, up_buf, 1).wait()
+            columns_copy(step, pair, lower + 1, up_buf, 1).wait()
 
         @pl.when(crosses)
         def _():
-            columns_copy(step, 0, first_buf, 2).wait()
+            columns_copy(step, pair, 0, first_buf, 2).wait()
 
     for step in range(DEPTH - 1):
         fetch(step)
@@ -108,12 +113,13 @@
 
     def step_body(step, carry):
         slot = step % DEPTH
-        await_step(step)
 
         @pl.when(step + DEPTH - 1 < steps)
         def _():
             fetch(step + DEPTH - 1)
 
+        for pair in range(SQ // 2):
+            await_pair(step, pair)
         owns, firsts = [], []
         for pair in range(SQ // 2):
             orders, values, columns = [], [], []
@@ -164,7 +170,7 @@
     spec = spectral.reshape(SQ, groups, cols, NT)
     leg = legendre.reshape(SQ, groups, half, NT)
     devices = lax.axis_size("wave") * lax.axis_size("lev")
-    out = jax.ShapeDtypeStruct((devices, 2 * half // devices * count, SQ * PART), F32)
+    out = pltpu.VMEM((devices, 2 * half // devices * count, SQ * PART), F32)
     smem = pl.BlockSpec(memory_space=pltpu.SMEM)
     vmem = pl.BlockSpec(memory_space=pltpu.VMEM)
     anywhere = pl.BlockSpec(memory_space=pltpu.HBM)
@@ -176,15 +182,14 @@
         scratch_shapes=[pltpu.VMEM((DEPTH, SQ, STEP_SLOTS, PART, NT), BF16)] * 3
         + [pltpu.VMEM((DEPTH, SQ, STEP_SLOTS, half, NT), BF16)]
         + [pltpu.VMEM((count * 2 * half, SQ * PART), F32)] * 2
-        + [pltpu.SemaphoreType.DMA((DEPTH, 4))],
-        compiler_params=pltpu.CompilerParams(vmem_limit_bytes=(24 if half < 64 else 40) * MIB),
+        + [pltpu.SemaphoreType.DMA((DEPTH, SQ // 2, 4))],
+        compiler_params=pltpu.CompilerParams(vmem_limit_bytes=48 * MIB),
         cost_estimate=pl.CostEstimate(
             flops=2 * SQ * count * 2 * half * 48 * NT, bytes_accessed=SQ * count * NT * 2 * (48 + half), transcendentals=0
         ),
         name="legendre_sums",
     )(
-        wave_map, brackets, lev_weight,
-        pltpu.with_memory_space_constraint(spec, pltpu.HBM), pltpu.with_memory_space_constraint(leg, pltpu.HBM),
+        *[pltpu.with_memory_space_constraint(x, pltpu.HBM) for x in (wave_map, brackets, lev_weight, spec, leg)]
     )
 
 
@@ -257,19 +262,19 @@
 
 def tables(row_points, slot_map):
     rows = KPTS // TABLE_STEPS
-    table = jax.ShapeDtypeStruct((2, KPTS, 2 * M), BF16)
+    table = pltpu.HBM((2, KPTS, 2 * M), BF16)
     table_spec = pl.BlockSpec((1, rows, 2 * M), lambda r, k: (r, k, 0))
     perm_spec = pl.BlockSpec((PERM_ROWS, M), lambda r, k: (jnp.minimum(r * TABLE_STEPS + k, M // PERM_ROWS - 1), 0))
     return pl.pallas_call(
         table_kernel,
-        out_shape=[table, table, jax.ShapeDtypeStruct((M, M), BF16)],
+        out_shape=[table, table, pltpu.HBM((M, M), BF16)],
         grid=(2, TABLE_STEPS),
         in_specs=[pl.BlockSpec(memory_space=pltpu.SMEM), pl.BlockSpec(memory_space=pltpu.VMEM)],
         out_specs=[table_spec, table_spec, perm_spec],
-        compiler_params=pltpu.CompilerParams(vmem_limit_bytes=16 * MIB),
+        compiler_params=pltpu.CompilerParams(vmem_limit_bytes=48 * MIB),
         cost_estimate=pl.CostEstimate(flops=2 * KPTS * 2 * M * 12, bytes_accessed=2 * KPTS * 2 * M * 4 + M * M * 2, transcendentals=0),
         name="fourier_tables",
-    )(row_points, slot_map)
+    )(pltpu.with_memory_space_constraint(row_points, pltpu.HBM), slot_map)
 
 
 def pick_tables(plev):
@@ -324,11 +329,18 @@
 
 def synth_kernel(parts, points_ref, *refs):
     moved_refs = refs[:parts]
-    pick_ref, mean_ref, flip_ref, perm_ref, hi_ref, lo_ref, out_ref = refs[parts : parts + 7]
-    mixed, coef, flat, mirror, line = refs[parts + 7 :]
+    pick_ref, mean_ref, flip_ref, perm_hbm, hi_hbm, lo_hbm, out_ref = refs[parts : parts + 7]
+    perm_ref, hi_ref, lo_ref, mixed, coef, flat, mirror, line, sems = refs[parts + 7 :]
     waves, plev, _, _ = moved_refs[0].shape
     wide = plev * 2 * PART
     part_rows = M // SQ
+    copies = [pltpu.make_async_copy(perm_hbm, perm_ref, sems.at[0])]
+    for r2 in range(2):
+        copies.append(pltpu.make_async_copy(hi_hbm.at[r2], hi_ref.at[r2], sems.at[1 + 2 * r2]))
+        copies.append(pltpu.make_async_copy(lo_hbm.at[r2], lo_ref.at[r2], sems.at[2 + 2 * r2]))
+    for copy in copies:
+        copy.start()
+
     for base in range(0, plev * 2, 8):
         cur = []
         for g in range(base, base + 8):
@@ -360,6 +372,7 @@
     place = iota((HALF_M, 1), 0)
     turned = (iota((1, 2 * wide), 1) % wide) // (plev * FS) >= 2
     flip_sign = jnp.where(turned & (place % 2 == 1), -1.0, 1.0).astype(BF16)
+    copies[0].wait()
     for odd in range(2):
         ordered = nn_dot(perm_ref[odd * HALF_M : (odd + 1) * HALF_M, :], mixed[...])
         wave = 2 * place + odd
@@ -373,6 +386,9 @@
     mirror[...] = jnp.zeros_like(mirror)
 
     for r2 in range(2):
+        copies[1 + 2 * r2].wait()
+        copies[2 + 2 * r2].wait()
+
         def contraction(odd):
             lanes = slice(odd * M, (odd + 1) * M)
             both = nn_dot(hi_ref[r2, :, lanes], coef[r2, odd])
@@ -417,19 +433,28 @@
     return pl.pallas_call(
         functools.partial(synth_kernel, len(moved)),
         out_shape=jax.ShapeDtypeStruct((plev, 2, ROWPAD), F32),
-        in_specs=[pl.BlockSpec(memory_space=pltpu.SMEM)] + [vmem] * (len(moved) + 6),
+        in_specs=[pl.BlockSpec(memory_space=pltpu.SMEM)] + [vmem] * (len(moved) + 3) + [pl.BlockSpec(memory_space=pltpu.HBM)] * 3,
         out_specs=vmem,
         scratch_shapes=[
+            pltpu.VMEM((M, M), BF16),
+            pltpu.VMEM((2, KPTS, 2 * M), BF16),
+            pltpu.VMEM((2, KPTS, 2 * M), BF16),
             pltpu.VMEM((M, 2 * wide), BF16),
             pltpu.VMEM((2, 2, M, 2 * wide), BF16),
             pltpu.VMEM((8 * plev, BUF), F32),
             pltpu.VMEM((4 * plev, BUF), F32),
             pltpu.VMEM((plev, 3 * 1280 + BUF), F32),
+            pltpu.SemaphoreType.DMA((5,)),
         ],
-        compiler_params=pltpu.CompilerParams(vmem_limit_bytes=(20 if plev <= 4 else 32) * MIB),
+        compiler_params=pltpu.CompilerParams(vmem_limit_bytes=48 * MIB),
         cost_estimate=pl.CostEstimate(flops=2 * 2 * KPTS * 2 * M * 384, bytes_accessed=2 * KPTS * 2 * M * 4 + M * M * 2, transcendentals=0),
         name="synthesis",
-    )(row_points, *moved, pick_tables(plev), mean_table(plev), flip_table(), perm, table_hi, table_lo)
+    )(
+        pltpu.with_memory_space_constraint(row_points, pltpu.HBM),
+        *[pltpu.with_memory_space_constraint(x, pltpu.VMEM) for x in moved],
+        pick_tables(plev), mean_table(plev), flip_table(),
+        *[pltpu.with_memory_space_constraint(x, pltpu.HBM) for x in (perm, table_hi, table_lo)],
+    )
 
 
 def local(spectral, legendre, wave_map, row_points, brackets, lev_weight, climatology):
@@ -441,16 +466,25 @@
     rows_dev = 2 * half // (wave_count * lev_count)
     cuts = (0, 12, groups) if groups >= 16 else (0, groups)
     own_maps = wave_map.reshape(wave_count, SQ, groups)
-    moved, maps, sent = [], [], []
+    pairs = [(d, d - 1) for d in range(1, lev_count)]
+    parts = list(zip(cuts[:-1], cuts[1:]))
+    owns, prevs, sent = [], [], []
     order = wave_map
-    for start, stop in zip(cuts[:-1], cuts[1:]):
+    for start, stop in parts:
         own, prev = legendre_sums(start, stop - start, spectral, legendre, order, brackets, lev_weight)
         order, prev = lax.optimization_barrier((wave_map, prev))
-        if sent:
+        owns.append(own)
+        prevs.append(prev)
+    for i in range(len(parts)):
+        prev = prevs[i]
+        if i:
             prev, _ = lax.optimization_barrier((prev, sent[-1]))
-        from_next = lax.ppermute(prev, "lev", [(d, d - 1) for d in range(1, lev_count)])
-        sent.append(own + from_next)
-        part = lax.all_to_all(sent[-1], ("wave", "lev"), split_axis=0, concat_axis=0, tiled=True)
+        whole = owns[i] + lax.ppermute(prev, "lev", pairs)
+        whole, _ = lax.optimization_barrier((whole, owns[-1]))
+        sent.append(whole)
+    moved, maps = [], []
+    for (start, stop), whole in zip(parts, sent):
+        part = lax.all_to_all(whole, ("wave", "lev"), split_axis=0, concat_axis=0, tiled=True)
         moved.append(part.reshape(wave_count, lev_count, rows_dev * (stop - start), SQ * PART))
         maps.append(jnp.transpose(own_maps[:, :, start:stop], (1, 0, 2)).reshape(SQ, wave_count * (stop - start)))
     slot_map = jnp.concatenate(maps, axis=1).reshape(1, M)

time: 93.9 us -> 79.2 us (0.84)
  local copies, waits for them, and re-layouts: 20.6 us -> 0.66 us
  Pallas kernels: 33.7 us -> 42.4 us
  starting transfers between devices: 24.2 us -> 17.1 us
  waiting for transfers between devices: 10.2 us -> 15.9 us
  other arithmetic: 4.09 us -> 2.44 us
    unnamed x38 -> x12, local copies, waits for them, and re-layouts: 19.4 us -> 0.04 us
    all_to_all x2, waiting for transfers between devices: 1.73 us -> 9.02 us  [local(): lax.all_to_all(whole, ('wave', 'lev'), split_axis=0, concat_axis=0, tiled...]
    all_to_all x2, starting transfers between devices: 18.3 us -> 11 us  [local(): lax.all_to_all(whole, ('wave', 'lev'), split_axis=0, concat_axis=0, tiled...]
    pallas_call x1, Pallas kernels: 8.02 us -> 12.2 us  [tables(): pl.pallas_call(table_kernel, out_shape=[table, table, pltpu.HBM((M, M), B...]
    pallas_call x1, Pallas kernels: 8.81 us -> 12.2 us  [synthesis(): pl.pallas_call(functools.partial(synth_kernel, len(moved)), out_shape=jax...]
    ppermute x2, waiting for transfers between devices: 4.34 us -> 2.02 us  [local(): whole = owns[i] + lax.ppermute(prev, 'lev', pairs)]
    pallas_call x2, Pallas kernels: 16.9 us -> 18 us  [legendre_sums(): pl.pallas_call(functools.partial(legendre_kernel, first_group, count), ou...]
  transfers between devices with their start and end apart: 5 -> 5, of which waited for: 4 -> 3; matrix products, arithmetic and copies ran while one was open for 3% -> 2% of each run, Pallas kernels for 16% -> 25%
where the time goes in v3:
time: 79.2 us; the launch traced here: 78.6 us
  Pallas kernels  42.4 us (54%)
  starting transfers between devices  17.1 us (22%)
  waiting for transfers between devices  15.9 us (20%)
  other arithmetic  2.44 us (3%)
    pallas_call x2, Pallas kernels, legendre_sums(): pl.pallas_call(functools.partial(legendre_kernel, first_group, count), ou...  18 us
    pallas_call x1, Pallas kernels, synthesis(): pl.pallas_call(functools.partial(synth_kernel, len(moved)), out_shape=jax...  12.2 us
    pallas_call x1, Pallas kernels, tables(): pl.pallas_call(table_kernel, out_shape=[table, table, pltpu.HBM((M, M), B...  12.2 us
    all_to_all x2, starting transfers between devices, local(): lax.all_to_all(whole, ('wave', 'lev'), split_axis=0, concat_axis=0, tiled...  11 us
    all_to_all x2, waiting for transfers between devices, local(): lax.all_to_all(whole, ('wave', 'lev'), split_axis=0, concat_axis=0, tiled...  9.02 us
    all_to_all x1, waiting for transfers between devices, local(): lax.all_to_all(energy, 'lev', split_axis=0, concat_axis=0, tiled=True)  4.82 us
    all_to_all x1, starting transfers between devices, local(): lax.all_to_all(energy, 'lev', split_axis=0, concat_axis=0, tiled=True)  3.36 us
    ppermute x2, starting transfers between devices, local(): whole = owns[i] + lax.ppermute(prev, 'lev', pairs)  2.72 us
  transfers between devices with their start and end apart: 5, of which 3 were waited for; matrix products, arithmetic and copies ran while one was open for 2% of the time, Pallas kernels for 25%

profile of v3, /device:TPU:0, one launch (start us, length us, event | category | flops | bytes accessed | tf_op | source)
XLA Modules:
  0.0 78.6 jit_solution(11517041029992356423)
XLA Ops:
  0.0 10.3 %legendre_sums.2 = (f32[32,24,128]{2,1,0:T(8,128)S(1)}, f32[32,24,128]{2,1,0:T(8,128)S(1)}) custom-call(s32[1280]{0:T(1024)} %wave_map.2, s32[4]{0:T(128)} %brackets.3, f32[4]{0:T(128)} %weight_ref.3, bf16[8,20,64,1280]{3,2,1,0:T(8,128)(2,1)} %bitcast.10, bf16[8,20,32,1280]{3,2,1,0:T(8,128)(2,1)} %bitcast.12), custom_call_target="tpu_custom_call" | custom-call | flops 754974720 | bytes 19660800 | tf_op jit(solution)/shard_map/legendre_sums/pallas_call | solution.py:177
  10.3 0.0 copy-start.4
  10.3 0.0 copy-start
  10.3 0.0 copy-start.1
  10.3 0.0 copy-start.2
  10.3 1.4 %collective-permute-start = (f32[32,24,128]{2,1,0:T(8,128)S(1)}, f32[32,24,128]{2,1,0:T(8,128)S(1)}, u32[]{:S(2)}, u32[]{:S(2)}) collective-permute-start(f32[32,24,128]{2,1,0:T(8,128)S(1)} %get-tuple-element.21), channel_id=1, source_target_pairs={{1,0},{2,1},{3,2},{5,4},{6,5},{7,6},{9,8},{10,9},{11,10},{13,12},{... | collective-permute-start | bytes 1179656 | tf_op jit(solution)/shard_map/ppermute | solution.py:482
  11.8 7.7 %legendre_sums.3 = (f32[32,16,128]{2,1,0:T(8,128)S(1)}, f32[32,16,128]{2,1,0:T(8,128)S(1)}) custom-call(s32[1280]{0:T(1024)} %wave_map.2, s32[4]{0:T(128)} %brackets.3, f32[4]{0:T(128)} %weight_ref.3, bf16[8,20,64,1280]{3,2,1,0:T(8,128)(2,1)} %bitcast.11, bf16[8,20,32,1280]{3,2,1,0:T(8,128)(2,1)} %bitcast.13), custom_call_target="tpu_custom_call" | custom-call | flops 503316480 | bytes 13107200 | tf_op jit(solution)/shard_map/legendre_sums/pallas_call | solution.py:177
  19.5 0.0 collective-permute-done
  19.5 0.8 %add.10 = f32[32,24,128]{2,1,0:T(8,128)} add(f32[32,24,128]{2,1,0:T(8,128)S(1)} %get-tuple-element.19, f32[32,24,128]{2,1,0:T(8,128)S(1)} %collective-permute-done) | non-fusion elementwise | flops 98304 | bytes 1179648 | tf_op jit(solution)/shard_map/add | solution.py:482
  20.3 8.4 %all-to-all-start = ((f32[32,24,128]{2,1,0:T(8,128)}), f32[32,24,128]{2,1,0:T(8,128)S(1)}, u32[]{:S(2)}, u32[]{:S(2)}) async-start(f32[32,24,128]{2,1,0:T(8,128)} %add.10), calls=%async_computation | async-start | bytes 786432 | tf_op jit(solution)/shard_map/all_to_all | solution.py:487
  28.7 1.3 %collective-permute-start.1 = (f32[32,16,128]{2,1,0:T(8,128)S(1)}, f32[32,16,128]{2,1,0:T(8,128)S(1)}, u32[]{:S(2)}, u32[]{:S(2)}) collective-permute-start(f32[32,16,128]{2,1,0:T(8,128)S(1)} %get-tuple-element.27), channel_id=1, source_target_pairs={{1,0},{2,1},{3,2},{5,4},{6,5},{7,6},{9,8},{10,9},{11,10},{13,12},{... | collective-permute-start | bytes 786440 | tf_op jit(solution)/shard_map/ppermute | solution.py:482
  30.0 0.0 copy-done.4
  30.0 0.1 reshape.65
  30.2 2.0 %collective-permute-done.1 = f32[32,16,128]{2,1,0:T(8,128)S(1)} collective-permute-done((f32[32,16,128]{2,1,0:T(8,128)S(1)}, f32[32,16,128]{2,1,0:T(8,128)S(1)}, u32[]{:S(2)}, u32[]{:S(2)}) %collective-permute-start.1) | collective-permute-done | bytes 262176 | tf_op jit(solution)/shard_map/ppermute | solution.py:482
  32.2 0.7 add.11
  32.9 9.0 %all-to-all-done = f32[32,24,128]{2,1,0:T(8,128)S(1)} async-done(((f32[32,24,128]{2,1,0:T(8,128)}), f32[32,24,128]{2,1,0:T(8,128)S(1)}, u32[]{:S(2)}, u32[]{:S(2)}) %all-to-all-start) | async-done | bytes 393248 | tf_op jit(solution)/shard_map/all_to_all | solution.py:487
  41.9 2.6 %all-to-all-start.1 = ((f32[32,16,128]{2,1,0:T(8,128)}), f32[32,16,128]{2,1,0:T(8,128)S(1)}, u32[]{:S(2)}, u32[]{:S(2)}) async-start(f32[32,16,128]{2,1,0:T(8,128)} %add.11), calls=%async_computation.1 | async-start | bytes 524288 | tf_op jit(solution)/shard_map/all_to_all | solution.py:487
  44.6 0.1 slice_bitcast_fusion
  44.6 0.1 reshape.67
  44.7 0.1 reshape.66
  44.8 0.1 pad_add_fusion
  44.9 0.1 reshape.68.map_ref
  45.0 12.2 %fourier_tables.1 = (bf16[2,672,2560]{2,1,0:T(8,128)(2,1)}, bf16[2,672,2560]{2,1,0:T(8,128)(2,1)}, bf16[1280,1280]{1,0:T(8,128)(2,1)}) custom-call(s32[32]{0:T(128)} %points_ref.2, s32[1,1280]{1,0:T(1,128)S(1)} %reshape.68.map_ref), custom_call_target="tpu_custom_call" | custom-call | flops 41287680 | bytes 17039360 | tf_op jit(solution)/shard_map/fourier_tables/pallas_call | solution.py:268
  57.1 0.0 all-to-all-done.1
  57.1 0.0 copy-done
  57.1 0.0 copy-done.1
  57.2 0.0 copy-done.2
  57.2 0.0 copy-start.5
  57.2 0.0 copy-start.3
  57.2 12.2 %synthesis.1 = f32[4,2,5248]{2,1,0:T(2,128)} custom-call(s32[32]{0:T(128)} %points_ref.2, f32[8,4,24,128]{3,2,1,0:T(8,128)S(1)} %bitcast.8, f32[8,4,16,128]{3,2,1,0:T(8,128)S(1)} %bitcast.9, bf16[2,4,256,256]{3,2,1,0:T(8,128)(2,1)S(1)} %copy-done, bf16[32,256]{1,0:T(8,128)(2,1)S(1)} %copy-done.2, bf16[256,256]{1,0:T(8,128)(2,1)S(1)} %copy-done.1, ...), custom_call_target="tpu_custom_call" | custom-call | flops 2642411520 | bytes 17039360 | tf_op jit(solution)/shard_map/synthesis/pallas_call | solution.py:433
  69.4 3.4 %all-to-all-start.2 = ((f32[4,2,5248]{2,1,0:T(2,128)}), f32[4,2,5248]{2,1,0:T(2,128)S(1)}, u32[]{:S(2)}, u32[]{:S(2)}) async-start(f32[4,2,5248]{2,1,0:T(2,128)} %synthesis.1), calls=%async_computation.2 | async-start | bytes 335872 | tf_op jit(solution)/shard_map/all_to_all | solution.py:494
  72.8 0.0 copy-done.5
  72.8 0.1 pad_add_fusion.1
  72.9 0.1 dynamic_slice.3
  72.9 4.8 %all-to-all-done.2 = f32[4,2,5248]{2,1,0:T(2,128)S(1)} async-done(((f32[4,2,5248]{2,1,0:T(2,128)}), f32[4,2,5248]{2,1,0:T(2,128)S(1)}, u32[]{:S(2)}, u32[]{:S(2)}) %all-to-all-start.2) | async-done | bytes 167968 | tf_op jit(solution)/shard_map/all_to_all | solution.py:494
  77.8 0.1 reshape.69
  77.9 0.0 copy-done.3
  77.9 0.8 subtract_select_fusion
  (3 shorter events, 0.0 us)
Async XLA Ops:
  10.3 19.7 %copy-start.4 = (s32[1280]{0:T(1024)S(1)}, s32[1280]{0:T(1024)}, u32[]{:S(2)}) copy-start(s32[1280]{0:T(1024)} %wave_map.2) | copy-start | bytes 15364
  10.3 46.8 %copy-start = (bf16[2,4,256,256]{3,2,1,0:T(8,128)(2,1)S(1)}, bf16[2,4,256,256]{3,2,1,0:T(8,128)(2,1)}, u32[]{:S(2)}) copy-start(bf16[2,4,256,256]{3,2,1,0:T(8,128)(2,1)} %constant.20.clone.refs_2_) | copy-start | bytes 3145732
  10.3 46.8 %copy-start.1 = (bf16[256,256]{1,0:T(8,128)(2,1)S(1)}, bf16[256,256]{1,0:T(8,128)(2,1)}, u32[]{:S(2)}) copy-start(bf16[256,256]{1,0:T(8,128)(2,1)} %constant.22.clone.refs_4_) | copy-start | bytes 393220
  10.3 46.8 %copy-start.2 = (bf16[32,256]{1,0:T(8,128)(2,1)S(1)}, bf16[32,256]{1,0:T(8,128)(2,1)}, u32[]{:S(2)}) copy-start(bf16[32,256]{1,0:T(8,128)(2,1)} %constant.21.clone.refs_3_) | copy-start | bytes 49156
  10.3 9.2 %collective-permute-start = (f32[32,24,128]{2,1,0:T(8,128)S(1)}, f32[32,24,128]{2,1,0:T(8,128)S(1)}, u32[]{:S(2)}, u32[]{:S(2)}) collective-permute-start(f32[32,24,128]{2,1,0:T(8,128)S(1)} %get-tuple-element.21), channel_id=1, source_target_pairs={{1,0},{2,1},{3,2},{5,4},{6,5},{7,6},{9,8},{10,9},{11,10},{13,12},{... | collective-permute-start | bytes 1179656 | tf_op jit(solution)/shard_map/ppermute | solution.py:482
  20.3 21.6 %all-to-all-start = ((f32[32,24,128]{2,1,0:T(8,128)}), f32[32,24,128]{2,1,0:T(8,128)S(1)}, u32[]{:S(2)}, u32[]{:S(2)}) async-start(f32[32,24,128]{2,1,0:T(8,128)} %add.10), calls=%async_computation | async-start | bytes 786432 | tf_op jit(solution)/shard_map/all_to_all | solution.py:487
  28.7 3.4 %collective-permute-start.1 = (f32[32,16,128]{2,1,0:T(8,128)S(1)}, f32[32,16,128]{2,1,0:T(8,128)S(1)}, u32[]{:S(2)}, u32[]{:S(2)}) collective-permute-start(f32[32,16,128]{2,1,0:T(8,128)S(1)} %get-tuple-element.27), channel_id=1, source_target_pairs={{1,0},{2,1},{3,2},{5,4},{6,5},{7,6},{9,8},{10,9},{11,10},{13,12},{... | collective-permute-start | bytes 786440 | tf_op jit(solution)/shard_map/ppermute | solution.py:482
  41.9 15.2 %all-to-all-start.1 = ((f32[32,16,128]{2,1,0:T(8,128)}), f32[32,16,128]{2,1,0:T(8,128)S(1)}, u32[]{:S(2)}, u32[]{:S(2)}) async-start(f32[32,16,128]{2,1,0:T(8,128)} %add.11), calls=%async_computation.1 | async-start | bytes 524288 | tf_op jit(solution)/shard_map/all_to_all | solution.py:487
  57.2 15.6 %copy-start.5 = (s32[32]{0:T(128)S(1)}, s32[32]{0:T(128)}, u32[]{:S(2)}) copy-start(s32[32]{0:T(128)} %points_ref.2) | copy-start | bytes 388
  57.2 20.7 %copy-start.3 = (f32[1,8,5248]{2,1,0:T(8,128)S(1)}, f32[1,8,5248]{2,1,0:T(8,128)}, u32[]{:S(2)}) copy-start(f32[1,8,5248]{2,1,0:T(8,128)} %param.16) | copy-start | bytes 503812
  69.4 8.4 %all-to-all-start.2 = ((f32[4,2,5248]{2,1,0:T(2,128)}), f32[4,2,5248]{2,1,0:T(2,128)S(1)}, u32[]{:S(2)}, u32[]{:S(2)}) async-start(f32[4,2,5248]{2,1,0:T(2,128)} %synthesis.1), calls=%async_computation.2 | async-start | bytes 335872 | tf_op jit(solution)/shard_map/all_to_all | solution.py:494

commit v4 on v2

--- a/solution.py
+++ b/solution.py
@@ -25,8 +25,6 @@
 KPTS = 672
 KPAD = 768
 KBLK = 256
-TABLE_STEPS = 7
-PERM_ROWS = 128
 BUF = 1536
 MIB = 1024 * 1024
 F32 = jnp.float32
@@ -55,8 +53,8 @@
     before = jnp.maximum(lev - 1, 0)
     crosses = (lev > 0) & (brackets[before] == lev * LEV_DEV - 1)
     first_w = jnp.where(crosses, 1.0 - weight_ref[before], 0.0)
-    degree = iota((16, NT), 1)
-    sign = (1 - 2 * (degree % 2)).astype(F32).astype(BF16)
+    degree = iota((16, NT), 1).astype(jnp.int16)
+    sign = (1 - 2 * (iota((16, NT), 1) % 2)).astype(F32).astype(BF16)
     lane = iota((1, width), 1)
     south = lane % (2 * half) >= half
 
@@ -122,8 +120,8 @@
                 for b in range(STEP_SLOTS):
                     m = wave_map[wave * slots + sq * groups + first_group + step * STEP_SLOTS + b]
                     orders.append(m)
-                    kept = jnp.where(degree >= m, 1.0, 0.0).astype(BF16)
-                    plain = [leg_buf[slot, sq, b, i : i + 16, :] * kept for i in range(0, half, 16)]
+                    kept = degree >= m.astype(jnp.int16)
+                    plain = [jnp.where(kept, leg_buf[slot, sq, b, i : i + 16, :], 0) for i in range(0, half, 16)]
                     values += plain + [x * sign for x in plain]
                     columns += [buf[slot, sq, b] for buf in (low_buf, up_buf, first_buf)]
             sums = nt_dot(jnp.concatenate(columns, axis=0), jnp.concatenate(values, axis=0))
@@ -164,7 +162,7 @@
     spec = spectral.reshape(SQ, groups, cols, NT)
     leg = legendre.reshape(SQ, groups, half, NT)
     devices = lax.axis_size("wave") * lax.axis_size("lev")
-    out = jax.ShapeDtypeStruct((devices, 2 * half // devices * count, SQ * PART), F32)
+    out = pltpu.VMEM((devices, 2 * half // devices * count, SQ * PART), F32)
     smem = pl.BlockSpec(memory_space=pltpu.SMEM)
     vmem = pl.BlockSpec(memory_space=pltpu.VMEM)
     anywhere = pl.BlockSpec(memory_space=pltpu.HBM)
@@ -177,14 +175,13 @@
         + [pltpu.VMEM((DEPTH, SQ, STEP_SLOTS, half, NT), BF16)]
         + [pltpu.VMEM((count * 2 * half, SQ * PART), F32)] * 2
         + [pltpu.SemaphoreType.DMA((DEPTH, 4))],
-        compiler_params=pltpu.CompilerParams(vmem_limit_bytes=(24 if half < 64 else 40) * MIB),
+        compiler_params=pltpu.CompilerParams(vmem_limit_bytes=48 * MIB),
         cost_estimate=pl.CostEstimate(
             flops=2 * SQ * count * 2 * half * 48 * NT, bytes_accessed=SQ * count * NT * 2 * (48 + half), transcendentals=0
         ),
         name="legendre_sums",
     )(
-        wave_map, brackets, lev_weight,
-        pltpu.with_memory_space_constraint(spec, pltpu.HBM), pltpu.with_memory_space_constraint(leg, pltpu.HBM),
+        *[pltpu.with_memory_space_constraint(x, pltpu.HBM) for x in (wave_map, brackets, lev_weight, spec, leg)]
     )
 
 
@@ -212,64 +209,60 @@
 
 
 def table_kernel(points_ref, map_ref, hi_ref, lo_ref, perm_ref):
-    r2 = pl.program_id(0)
-    kb = pl.program_id(1)
-    rows = hi_ref.shape[1]
-    points = own_points(points_ref, r2).astype(F32)
-    inverse = 1.0 / points
-    part = r2 * pl.num_programs(1) + kb
-
-    @pl.when(part < M // PERM_ROWS)
-    def _():
-        order = part * PERM_ROWS + iota((PERM_ROWS, 1), 0)
+    lane = iota((16, 128), 1).astype(F32)
+
+    def perm_body(i, carry):
+        row = pl.multiple_of(i * 16, 16)
+        order = row + iota((16, 1), 0)
         wanted = jnp.where(order < HALF_M, 2 * order, 2 * (order - HALF_M) + 1)
-        perm_ref[...] = jnp.where(map_ref[...] == wanted, 1.0, 0.0).astype(BF16)
-
-    lane = iota((16, 128), 1).astype(F32)
-
-    def chunk_body(i, carry):
-        chunk = pl.multiple_of(i * 16, 16)
-
-        def put(tile, value):
-            lanes = slice(tile * 128, tile * 128 + 128)
-            hi = value.astype(BF16)
-            hi_ref[0, pl.ds(chunk, 16), lanes] = hi
-            lo_ref[0, pl.ds(chunk, 16), lanes] = (value - hi.astype(F32)).astype(BF16)
-
-        k = (kb * rows + chunk + iota((16, 128), 0)).astype(F32)
-        c, s = unit_circle(2.0 * lane * k, points, inverse)
-        c1, s1 = unit_circle(k, points, inverse)
-        ct, st = unit_circle(256.0 * k, points, inverse)
-        co = c * c1 - s * s1
-        so = s * c1 + c * s1
-        for t in range(HALF_M // 128):
-            if t:
-                c, s = c * ct - s * st, s * ct + c * st
-                co, so = co * ct - so * st, so * ct + co * st
-            put(t, c)
-            put(5 + t, s)
-            put(10 + t, co)
-            put(15 + t, so)
+        perm_ref[pl.ds(row, 16), :] = jnp.where(map_ref[...] == wanted, 1.0, 0.0).astype(BF16)
         return carry
 
-    lax.fori_loop(0, rows // 16, chunk_body, 0, unroll=True)
+    lax.fori_loop(0, M // 16, perm_body, 0, unroll=4)
+    for r2 in range(2):
+        points = own_points(points_ref, r2).astype(F32)
+        inverse = 1.0 / points
+
+        def chunk_body(i, carry):
+            chunk = pl.multiple_of(i * 16, 16)
+
+            def put(tile, value):
+                lanes = slice(tile * 128, tile * 128 + 128)
+                hi = value.astype(BF16)
+                hi_ref[r2, pl.ds(chunk, 16), lanes] = hi
+                lo_ref[r2, pl.ds(chunk, 16), lanes] = (value - hi.astype(F32)).astype(BF16)
+
+            k = (chunk + iota((16, 128), 0)).astype(F32)
+            c, s = unit_circle(2.0 * lane * k, points, inverse)
+            c1, s1 = unit_circle(k, points, inverse)
+            ct, st = unit_circle(256.0 * k, points, inverse)
+            co = c * c1 - s * s1
+            so = s * c1 + c * s1
+            for t in range(HALF_M // 128):
+                if t:
+                    c, s = c * ct - s * st, s * ct + c * st
+                    co, so = co * ct - so * st, so * ct + co * st
+                put(t, c)
+                put(5 + t, s)
+                put(10 + t, co)
+                put(15 + t, so)
+            return carry
+
+        lax.fori_loop(0, KPTS // 16, chunk_body, 0, unroll=6)
 
 
 def tables(row_points, slot_map):
-    rows = KPTS // TABLE_STEPS
-    table = jax.ShapeDtypeStruct((2, KPTS, 2 * M), BF16)
-    table_spec = pl.BlockSpec((1, rows, 2 * M), lambda r, k: (r, k, 0))
-    perm_spec = pl.BlockSpec((PERM_ROWS, M), lambda r, k: (jnp.minimum(r * TABLE_STEPS + k, M // PERM_ROWS - 1), 0))
+    table = pltpu.VMEM((2, KPTS, 2 * M), BF16)
+    vmem = pl.BlockSpec(memory_space=pltpu.VMEM)
     return pl.pallas_call(
         table_kernel,
-        out_shape=[table, table, jax.ShapeDtypeStruct((M, M), BF16)],
-        grid=(2, TABLE_STEPS),
-        in_specs=[pl.BlockSpec(memory_space=pltpu.SMEM), pl.BlockSpec(memory_space=pltpu.VMEM)],
-        out_specs=[table_spec, table_spec, perm_spec],
-        compiler_params=pltpu.CompilerParams(vmem_limit_bytes=16 * MIB),
+        out_shape=[table, table, pltpu.VMEM((M, M), BF16)],
+        in_specs=[pl.BlockSpec(memory_space=pltpu.SMEM), vmem],
+        out_specs=[vmem] * 3,
+        compiler_params=pltpu.CompilerParams(vmem_limit_bytes=20 * MIB),
         cost_estimate=pl.CostEstimate(flops=2 * KPTS * 2 * M * 12, bytes_accessed=2 * KPTS * 2 * M * 4 + M * M * 2, transcendentals=0),
         name="fourier_tables",
-    )(row_points, slot_map)
+    )(pltpu.with_memory_space_constraint(row_points, pltpu.HBM), slot_map)
 
 
 def pick_tables(plev):
@@ -323,19 +316,17 @@
 
 
 def synth_kernel(parts, points_ref, *refs):
-    moved_refs = refs[:parts]
-    pick_ref, mean_ref, flip_ref, perm_ref, hi_ref, lo_ref, out_ref = refs[parts : parts + 7]
-    mixed, coef, flat, mirror, line = refs[parts + 7 :]
-    waves, plev, _, _ = moved_refs[0].shape
+    moved_ref, pick_ref, mean_ref, flip_ref, perm_ref, hi_ref, lo_ref, out_ref, mixed, coef, flat, mirror, line = refs
+    waves, plev, _, _ = moved_ref.shape
     wide = plev * 2 * PART
     part_rows = M // SQ
     for base in range(0, plev * 2, 8):
         cur = []
         for g in range(base, base + 8):
             pieces = []
-            for ref in moved_refs:
-                sub = ref.shape[2] // 2
-                pieces += [ref[w, g // 2, (g % 2) * sub : (g % 2 + 1) * sub, :] for w in range(waves)]
+            for start, stop in parts:
+                first = 2 * start + (g % 2) * (stop - start)
+                pieces += [moved_ref[w, g // 2, first : first + stop - start, :] for w in range(waves)]
             cur.append(jnp.concatenate(pieces, axis=0))
         group = iota((part_rows, 128), 1) // PART
         for bit in (1, 2, 4):
@@ -373,6 +364,7 @@
     mirror[...] = jnp.zeros_like(mirror)
 
     for r2 in range(2):
+
         def contraction(odd):
             lanes = slice(odd * M, (odd + 1) * M)
             both = nn_dot(hi_ref[r2, :, lanes], coef[r2, odd])
@@ -410,14 +402,14 @@
         out_ref[:, pl.ds(r2, 1), :] = line[:, :ROWPAD].reshape(plev, 1, ROWPAD)
 
 
-def synthesis(moved, perm, table_hi, table_lo, row_points):
-    plev = moved[0].shape[1]
+def synthesis(parts, moved, perm, table_hi, table_lo, row_points):
+    plev = moved.shape[1]
     wide = plev * 2 * PART
     vmem = pl.BlockSpec(memory_space=pltpu.VMEM)
     return pl.pallas_call(
-        functools.partial(synth_kernel, len(moved)),
+        functools.partial(synth_kernel, parts),
         out_shape=jax.ShapeDtypeStruct((plev, 2, ROWPAD), F32),
-        in_specs=[pl.BlockSpec(memory_space=pltpu.SMEM)] + [vmem] * (len(moved) + 6),
+        in_specs=[pl.BlockSpec(memory_space=pltpu.SMEM)] + [vmem] * 7,
         out_specs=vmem,
         scratch_shapes=[
             pltpu.VMEM((M, 2 * wide), BF16),
@@ -426,10 +418,37 @@
             pltpu.VMEM((4 * plev, BUF), F32),
             pltpu.VMEM((plev, 3 * 1280 + BUF), F32),
         ],
-        compiler_params=pltpu.CompilerParams(vmem_limit_bytes=(20 if plev <= 4 else 32) * MIB),
+        compiler_params=pltpu.CompilerParams(vmem_limit_bytes=(24 if plev <= 4 else 36) * MIB),
         cost_estimate=pl.CostEstimate(flops=2 * 2 * KPTS * 2 * M * 384, bytes_accessed=2 * KPTS * 2 * M * 4 + M * M * 2, transcendentals=0),
         name="synthesis",
-    )(row_points, *moved, pick_tables(plev), mean_table(plev), flip_table(), perm, table_hi, table_lo)
+    )(
+        pltpu.with_memory_space_constraint(row_points, pltpu.HBM),
+        pltpu.with_memory_space_constraint(moved, pltpu.VMEM),
+        pick_tables(plev), mean_table(plev), flip_table(),
+        *[pltpu.with_memory_space_constraint(x, pltpu.VMEM) for x in (perm, table_hi, table_lo)],
+    )
+
+
+def join_kernel(*refs):
+    parts = (len(refs) - 1) // 2
+    at = 0
+    for own_ref, other_ref in zip(refs[:parts], refs[parts:-1]):
+        rows = own_ref.shape[1]
+        refs[-1][:, at : at + rows, :] = own_ref[...] + other_ref[...]
+        at += rows
+
+
+def join(owns, others):
+    rows = sum(x.shape[1] for x in owns)
+    vmem = pl.BlockSpec(memory_space=pltpu.VMEM)
+    return pl.pallas_call(
+        join_kernel,
+        out_shape=jax.ShapeDtypeStruct((owns[0].shape[0], rows, SQ * PART), F32),
+        in_specs=[vmem] * (2 * len(owns)),
+        out_specs=vmem,
+        compiler_params=pltpu.CompilerParams(vmem_limit_bytes=32 * MIB),
+        name="join",
+    )(*[pltpu.with_memory_space_constraint(x, pltpu.VMEM) for x in owns + others])
 
 
 def local(spectral, legendre, wave_map, row_points, brackets, lev_weight, climatology):
@@ -441,22 +460,25 @@
     rows_dev = 2 * half // (wave_count * lev_count)
     cuts = (0, 12, groups) if groups >= 16 else (0, groups)
     own_maps = wave_map.reshape(wave_count, SQ, groups)
-    moved, maps, sent = [], [], []
+    pairs = [(d, d - 1) for d in range(1, lev_count)]
+    parts = list(zip(cuts[:-1], cuts[1:]))
+    owns, others, maps = [], [], []
     order = wave_map
-    for start, stop in zip(cuts[:-1], cuts[1:]):
+    for start, stop in parts:
         own, prev = legendre_sums(start, stop - start, spectral, legendre, order, brackets, lev_weight)
         order, prev = lax.optimization_barrier((wave_map, prev))
-        if sent:
-            prev, _ = lax.optimization_barrier((prev, sent[-1]))
-        from_next = lax.ppermute(prev, "lev", [(d, d - 1) for d in range(1, lev_count)])
-        sent.append(own + from_next)
-        part = lax.all_to_all(sent[-1], ("wave", "lev"), split_axis=0, concat_axis=0, tiled=True)
-        moved.append(part.reshape(wave_count, lev_count, rows_dev * (stop - start), SQ * PART))
+        if others:
+            prev, _ = lax.optimization_barrier((prev, others[-1]))
+        owns.append(own)
+        others.append(lax.ppermute(prev, "lev", pairs))
         maps.append(jnp.transpose(own_maps[:, :, start:stop], (1, 0, 2)).reshape(SQ, wave_count * (stop - start)))
+    sent = join(owns, others)
+    moved = lax.all_to_all(sent, ("wave", "lev"), split_axis=0, concat_axis=0, tiled=True)
+    moved = moved.reshape(wave_count, lev_count, rows_dev * groups, SQ * PART)
     slot_map = jnp.concatenate(maps, axis=1).reshape(1, M)
     table_points, _ = lax.optimization_barrier((row_points, sent))
     table_hi, table_lo, perm = tables(table_points, slot_map)
-    energy = synthesis(moved, perm, table_hi, table_lo, row_points)
+    energy = synthesis(parts, moved, perm, table_hi, table_lo, row_points)
     result = lax.all_to_all(energy, "lev", split_axis=0, concat_axis=0, tiled=True)
     result = result.reshape(1, rows_dev * lev_count, ROWPAD)
     points_all = jnp.concatenate([row_points, row_points])

time: 93.9 us -> 79.9 us (0.85)
  starting transfers between devices: 24.2 us -> 16 us
  local copies, waits for them, and re-layouts: 20.6 us -> 13.5 us
  Pallas kernels: 33.7 us -> 36.3 us
  other arithmetic: 4.09 us -> 1.83 us
  waiting for transfers between devices: 10.2 us -> 11.4 us
    all_to_all x2 -> x1, starting transfers between devices: 18.3 us -> 9.96 us  [local(): lax.all_to_all(sent, ('wave', 'lev'), split_axis=0, concat_axis=0, tiled=...]
    unnamed x38 -> x18, local copies, waits for them, and re-layouts: 19.4 us -> 12.9 us
    pallas_call x2 -> x3, Pallas kernels: 16.8 us -> 19.4 us  [the longest x1 10 us: synthesis(): pl.pallas_call(functools.partial(synth_kernel, parts), out_shape=jax.Shap...]
    add x2 -> x0, other arithmetic: 1.54 us -> none  [local(): sent.append(own + from_next)]
    all_to_all x2 -> x1, waiting for transfers between devices: 1.73 us -> 3.18 us  [local(): lax.all_to_all(sent, ('wave', 'lev'), split_axis=0, concat_axis=0, tiled=...]
  transfers between devices with their start and end apart: 5 -> 4, of which waited for: 4 -> 3; matrix products, arithmetic and copies ran while one was open for 3% -> 1% of each run, Pallas kernels for 16% -> 20%
where the time goes in v4:
time: 79.9 us; the launch traced here: 79.3 us
  Pallas kernels  36.3 us (45%)
  starting transfers between devices  16 us (20%)
  local copies, waits for them, and re-layouts  13.5 us (17%)
  waiting for transfers between devices  11.4 us (14%)
  other arithmetic  1.83 us (2%)
    pallas_call x2, Pallas kernels, legendre_sums(): pl.pallas_call(functools.partial(legendre_kernel, first_group, count), ou...  17 us
    unnamed x18, local copies, waits for them, and re-layouts  12.9 us
    pallas_call x1, Pallas kernels, synthesis(): pl.pallas_call(functools.partial(synth_kernel, parts), out_shape=jax.Shap...  10 us
    all_to_all x1, starting transfers between devices, local(): lax.all_to_all(sent, ('wave', 'lev'), split_axis=0, concat_axis=0, tiled=...  9.96 us
    pallas_call x1, Pallas kernels, tables(): pl.pallas_call(table_kernel, out_shape=[table, table, pltpu.VMEM((M, M),...  8.4 us
    all_to_all x1, waiting for transfers between devices, local(): lax.all_to_all(energy, 'lev', split_axis=0, concat_axis=0, tiled=True)  4.82 us
    ppermute x2, waiting for transfers between devices, local(): others.append(lax.ppermute(prev, 'lev', pairs))  3.44 us
    all_to_all x1, starting transfers between devices, local(): lax.all_to_all(energy, 'lev', split_axis=0, concat_axis=0, tiled=True)  3.35 us
  transfers between devices with their start and end apart: 4, of which 3 were waited for; matrix products, arithmetic and copies ran while one was open for 1% of the time, Pallas kernels for 20%

profile of v4, /device:TPU:0, one launch (start us, length us, event | category | flops | bytes accessed | tf_op | source)
XLA Modules:
  0.0 79.3 jit_solution(7907675762124187462)
XLA Ops:
  0.0 9.7 %legendre_sums.2 = (f32[32,24,128]{2,1,0:T(8,128)S(1)}, f32[32,24,128]{2,1,0:T(8,128)S(1)}) custom-call(s32[1280]{0:T(1024)} %wave_map.2, s32[4]{0:T(128)} %brackets.3, f32[4]{0:T(128)} %weight_ref.3, bf16[8,20,64,1280]{3,2,1,0:T(8,128)(2,1)} %bitcast.7, bf16[8,20,32,1280]{3,2,1,0:T(8,128)(2,1)} %bitcast.9), custom_call_target="tpu_custom_call" | custom-call | flops 754974720 | bytes 19660800 | tf_op jit(solution)/shard_map/legendre_sums/pallas_call | solution.py:169
  9.7 0.0 copy-start.7
  9.7 0.0 copy-start.5
  9.7 0.0 copy-start.6
  9.7 1.4 %collective-permute-start = (f32[32,24,128]{2,1,0:T(8,128)S(1)}, f32[32,24,128]{2,1,0:T(8,128)S(1)}, u32[]{:S(2)}, u32[]{:S(2)}) collective-permute-start(f32[32,24,128]{2,1,0:T(8,128)S(1)} %get-tuple-element.21), channel_id=1, source_target_pairs={{1,0},{2,1},{3,2},{5,4},{6,5},{7,6},{9,8},{10,9},{11,10},{13,12},{... | collective-permute-start | bytes 1179656 | tf_op jit(solution)/shard_map/ppermute | solution.py:473
  11.2 7.3 %legendre_sums.3 = (f32[32,16,128]{2,1,0:T(8,128)S(1)}, f32[32,16,128]{2,1,0:T(8,128)S(1)}) custom-call(s32[1280]{0:T(1024)} %wave_map.2, s32[4]{0:T(128)} %brackets.3, f32[4]{0:T(128)} %weight_ref.3, bf16[8,20,64,1280]{3,2,1,0:T(8,128)(2,1)} %bitcast.8, bf16[8,20,32,1280]{3,2,1,0:T(8,128)(2,1)} %bitcast.10), custom_call_target="tpu_custom_call" | custom-call | flops 503316480 | bytes 13107200 | tf_op jit(solution)/shard_map/legendre_sums/pallas_call | solution.py:169
  18.5 0.0 collective-permute-done.refs_2_
  18.5 1.3 %collective-permute-start.1 = (f32[32,16,128]{2,1,0:T(8,128)S(1)}, f32[32,16,128]{2,1,0:T(8,128)S(1)}, u32[]{:S(2)}, u32[]{:S(2)}) collective-permute-start(f32[32,16,128]{2,1,0:T(8,128)S(1)} %get-tuple-element.24), channel_id=1, source_target_pairs={{1,0},{2,1},{3,2},{5,4},{6,5},{7,6},{9,8},{10,9},{11,10},{13,12},{... | collective-permute-start | bytes 786440 | tf_op jit(solution)/shard_map/ppermute | solution.py:473
  19.8 3.4 %collective-permute-done.1.refs_3_ = f32[32,16,128]{2,1,0:T(8,128)S(1)} collective-permute-done((f32[32,16,128]{2,1,0:T(8,128)S(1)}, f32[32,16,128]{2,1,0:T(8,128)S(1)}, u32[]{:S(2)}, u32[]{:S(2)}) %collective-permute-start.1) | collective-permute-done | bytes 262176 | tf_op jit(solution)/shard_map/ppermute | solution.py:473
  23.2 0.9 %join.1 = f32[32,40,128]{2,1,0:T(8,128)} custom-call(f32[32,24,128]{2,1,0:T(8,128)S(1)} %get-tuple-element.17.refs_0_, f32[32,16,128]{2,1,0:T(8,128)S(1)} %get-tuple-element.20.refs_1_, f32[32,24,128]{2,1,0:T(8,128)S(1)} %collective-permute-done.refs_2_, f32[32,16,128]{2,1,0:T(8,128)S(1)} %collective-permute-done.1.refs_3_), custom_call_target="tpu_custom_call" | custom-call | tf_op jit(solution)/shard_map/join/pallas_call | solution.py:444
  24.1 10.0 %all-to-all-start = ((f32[32,40,128]{2,1,0:T(8,128)}), f32[32,40,128]{2,1,0:T(8,128)}, u32[]{:S(2)}, u32[]{:S(2)}) async-start(f32[32,40,128]{2,1,0:T(8,128)} %join.1), calls=%async_computation | async-start | bytes 1310720 | tf_op jit(solution)/shard_map/all_to_all | solution.py:476
  34.1 0.0 copy-done.7
  34.1 0.1 reshape.61
  34.2 0.1 slice_bitcast_fusion
  34.3 0.1 reshape.63
  34.4 0.1 reshape.62
  34.5 0.1 pad_add_fusion
  34.6 0.1 reshape.64.map_ref
  34.6 8.4 %fourier_tables.1 = (bf16[2,672,2560]{2,1,0:T(8,128)(2,1)S(1)}, bf16[2,672,2560]{2,1,0:T(8,128)(2,1)S(1)}, bf16[1280,1280]{1,0:T(8,128)(2,1)S(1)}) custom-call(s32[32]{0:T(128)} %points_ref.2, s32[1,1280]{1,0:T(1,128)S(1)} %reshape.64.map_ref), custom_call_target="tpu_custom_call" | custom-call | flops 41287680 | bytes 17039360 | tf_op jit(solution)/shard_map/fourier_tables/pallas_call | solution.py:257
  43.1 0.0 copy-start
  43.1 2.9 %copy-done = bf16[2,672,2560]{2,1,0:T(8,128)(2,1)} copy-done((bf16[2,672,2560]{2,1,0:T(8,128)(2,1)}, bf16[2,672,2560]{2,1,0:T(8,128)(2,1)S(1)}, u32[]{:S(2)}) %copy-start) | copy-done | bytes 6881304
  45.9 0.0 copy-start.2
  45.9 2.9 %copy-done.2 = bf16[2,672,2560]{2,1,0:T(8,128)(2,1)} copy-done((bf16[2,672,2560]{2,1,0:T(8,128)(2,1)}, bf16[2,672,2560]{2,1,0:T(8,128)(2,1)S(1)}, u32[]{:S(2)}) %copy-start.2) | copy-done | bytes 6881304
  48.8 3.2 %all-to-all-done = f32[32,40,128]{2,1,0:T(8,128)} async-done(((f32[32,40,128]{2,1,0:T(8,128)}), f32[32,40,128]{2,1,0:T(8,128)}, u32[]{:S(2)}, u32[]{:S(2)}) %all-to-all-start) | async-done | bytes 655392 | tf_op jit(solution)/shard_map/all_to_all | solution.py:476
  52.0 0.0 copy-done.5
  52.0 0.0 copy-done.6
  52.0 0.0 copy-start.1
  52.0 3.0 %copy-done.1 = bf16[2,672,2560]{2,1,0:T(8,128)(2,1)S(1)} copy-done((bf16[2,672,2560]{2,1,0:T(8,128)(2,1)S(1)}, bf16[2,672,2560]{2,1,0:T(8,128)(2,1)}, u32[]{:S(2)}) %copy-start.1) | copy-done | bytes 6881304
  55.0 0.0 copy-start.3
  55.0 3.0 %copy-done.3 = bf16[2,672,2560]{2,1,0:T(8,128)(2,1)S(1)} copy-done((bf16[2,672,2560]{2,1,0:T(8,128)(2,1)S(1)}, bf16[2,672,2560]{2,1,0:T(8,128)(2,1)}, u32[]{:S(2)}) %copy-start.3) | copy-done | bytes 6881304
  57.9 0.0 copy-start.4
  57.9 1.2 %copy-done.4 = bf16[2,4,256,256]{3,2,1,0:T(8,128)(2,1)S(1)} copy-done((bf16[2,4,256,256]{3,2,1,0:T(8,128)(2,1)S(1)}, bf16[2,4,256,256]{3,2,1,0:T(8,128)(2,1)}, u32[]{:S(2)}) %copy-start.4) | copy-done | bytes 1048600
  59.1 0.0 copy-start.8
  59.1 10.0 %synthesis.1 = f32[4,2,5248]{2,1,0:T(2,128)} custom-call(s32[32]{0:T(128)} %points_ref.2, f32[8,4,40,128]{3,2,1,0:T(8,128)} %bitcast.2.refs_0_, bf16[2,4,256,256]{3,2,1,0:T(8,128)(2,1)S(1)} %copy-done.4, bf16[32,256]{1,0:T(8,128)(2,1)S(1)} %copy-done.6, bf16[256,256]{1,0:T(8,128)(2,1)S(1)} %copy-done.5, bf16[1280,1280]{1,0:T(8,128)(2,1)S(1)} %get-tuple-element.26.refs_4_, ...), custom_call_target="tpu_custom_call" | custom-call | flops 2642411520 | bytes 17039360 | tf_op jit(solution)/shard_map/synthesis/pallas_call | solution.py:409
  69.2 3.3 %all-to-all-start.1 = ((f32[4,2,5248]{2,1,0:T(2,128)}), f32[4,2,5248]{2,1,0:T(2,128)S(1)}, u32[]{:S(2)}, u32[]{:S(2)}) async-start(f32[4,2,5248]{2,1,0:T(2,128)} %synthesis.1), calls=%async_computation.1 | async-start | bytes 335872 | tf_op jit(solution)/shard_map/all_to_all | solution.py:482
  72.6 0.0 copy-done.8
  72.6 0.1 pad_add_fusion.1
  72.6 0.1 dynamic_slice.3
  72.7 4.8 %all-to-all-done.1 = f32[4,2,5248]{2,1,0:T(2,128)S(1)} async-done(((f32[4,2,5248]{2,1,0:T(2,128)}), f32[4,2,5248]{2,1,0:T(2,128)S(1)}, u32[]{:S(2)}, u32[]{:S(2)}) %all-to-all-start.1) | async-done | bytes 167968 | tf_op jit(solution)/shard_map/all_to_all | solution.py:482
  77.5 0.1 reshape.65
  77.7 1.7 %subtract_select_fusion = f32[1,8,5248]{2,1,0:T(8,128)} fusion(f32[1,8,5248]{2,1,0:T(8,128)S(1)} %reshape.65, f32[1,8,5248]{2,1,0:T(8,128)} %param.16, s32[8]{0:T(128)S(1)} %dynamic_slice.3), kind=kLoop, calls=%fused_computation | loop fusion | flops 125952 | bytes 503840 | tf_op jit(solution)/shard_map/jit(_where)/select_n | solution.py:489
  (3 shorter events, 0.0 us)
Async XLA Ops:
  9.7 24.4 %copy-start.7 = (s32[1280]{0:T(1024)S(1)}, s32[1280]{0:T(1024)}, u32[]{:S(2)}) copy-start(s32[1280]{0:T(1024)} %wave_map.2) | copy-start | bytes 15364
  9.7 42.3 %copy-start.5 = (bf16[256,256]{1,0:T(8,128)(2,1)S(1)}, bf16[256,256]{1,0:T(8,128)(2,1)}, u32[]{:S(2)}) copy-start(bf16[256,256]{1,0:T(8,128)(2,1)} %constant.22.clone.refs_3_) | copy-start | bytes 393220
  9.7 42.3 %copy-start.6 = (bf16[32,256]{1,0:T(8,128)(2,1)S(1)}, bf16[32,256]{1,0:T(8,128)(2,1)}, u32[]{:S(2)}) copy-start(bf16[32,256]{1,0:T(8,128)(2,1)} %constant.21.clone.refs_2_) | copy-start | bytes 49156
  9.7 8.7 %collective-permute-start = (f32[32,24,128]{2,1,0:T(8,128)S(1)}, f32[32,24,128]{2,1,0:T(8,128)S(1)}, u32[]{:S(2)}, u32[]{:S(2)}) collective-permute-start(f32[32,24,128]{2,1,0:T(8,128)S(1)} %get-tuple-element.21), channel_id=1, source_target_pairs={{1,0},{2,1},{3,2},{5,4},{6,5},{7,6},{9,8},{10,9},{11,10},{13,12},{... | collective-permute-start | bytes 1179656 | tf_op jit(solution)/shard_map/ppermute | solution.py:473
  18.5 4.7 %collective-permute-start.1 = (f32[32,16,128]{2,1,0:T(8,128)S(1)}, f32[32,16,128]{2,1,0:T(8,128)S(1)}, u32[]{:S(2)}, u32[]{:S(2)}) collective-permute-start(f32[32,16,128]{2,1,0:T(8,128)S(1)} %get-tuple-element.24), channel_id=1, source_target_pairs={{1,0},{2,1},{3,2},{5,4},{6,5},{7,6},{9,8},{10,9},{11,10},{13,12},{... | collective-permute-start | bytes 786440 | tf_op jit(solution)/shard_map/ppermute | solution.py:473
  24.1 27.9 %all-to-all-start = ((f32[32,40,128]{2,1,0:T(8,128)}), f32[32,40,128]{2,1,0:T(8,128)}, u32[]{:S(2)}, u32[]{:S(2)}) async-start(f32[32,40,128]{2,1,0:T(8,128)} %join.1), calls=%async_computation | async-start | bytes 1310720 | tf_op jit(solution)/shard_map/all_to_all | solution.py:476
  43.1 2.9 %copy-start = (bf16[2,672,2560]{2,1,0:T(8,128)(2,1)}, bf16[2,672,2560]{2,1,0:T(8,128)(2,1)S(1)}, u32[]{:S(2)}) copy-start(bf16[2,672,2560]{2,1,0:T(8,128)(2,1)S(1)} %get-tuple-element.27.refs_5_) | copy-start | bytes 20643844
  45.9 2.9 %copy-start.2 = (bf16[2,672,2560]{2,1,0:T(8,128)(2,1)}, bf16[2,672,2560]{2,1,0:T(8,128)(2,1)S(1)}, u32[]{:S(2)}) copy-start(bf16[2,672,2560]{2,1,0:T(8,128)(2,1)S(1)} %get-tuple-element.28.refs_6_) | copy-start | bytes 20643844
  52.0 3.0 %copy-start.1 = (bf16[2,672,2560]{2,1,0:T(8,128)(2,1)S(1)}, bf16[2,672,2560]{2,1,0:T(8,128)(2,1)}, u32[]{:S(2)}) copy-start(bf16[2,672,2560]{2,1,0:T(8,128)(2,1)} %copy-done) | copy-start | bytes 20643844
  55.0 3.0 %copy-start.3 = (bf16[2,672,2560]{2,1,0:T(8,128)(2,1)S(1)}, bf16[2,672,2560]{2,1,0:T(8,128)(2,1)}, u32[]{:S(2)}) copy-start(bf16[2,672,2560]{2,1,0:T(8,128)(2,1)} %copy-done.2) | copy-start | bytes 20643844
  57.9 1.2 %copy-start.4 = (bf16[2,4,256,256]{3,2,1,0:T(8,128)(2,1)S(1)}, bf16[2,4,256,256]{3,2,1,0:T(8,128)(2,1)}, u32[]{:S(2)}) copy-start(bf16[2,4,256,256]{3,2,1,0:T(8,128)(2,1)} %constant.20.clone.refs_1_) | copy-start | bytes 3145732
  59.1 13.4 %copy-start.8 = (s32[32]{0:T(128)S(1)}, s32[32]{0:T(128)}, u32[]{:S(2)}) copy-start(s32[32]{0:T(128)} %points_ref.2) | copy-start | bytes 388
  69.2 8.3 %all-to-all-start.1 = ((f32[4,2,5248]{2,1,0:T(2,128)}), f32[4,2,5248]{2,1,0:T(2,128)S(1)}, u32[]{:S(2)}, u32[]{:S(2)}) async-start(f32[4,2,5248]{2,1,0:T(2,128)} %synthesis.1), calls=%async_computation.1 | async-start | bytes 335872 | tf_op jit(solution)/shard_map/all_to_all | solution.py:482

commit v5 on v4

--- a/solution.py
+++ b/solution.py
@@ -25,6 +25,8 @@
 KPTS = 672
 KPAD = 768
 KBLK = 256
+TABLE_STEPS = 7
+PERM_ROWS = 128
 BUF = 1536
 MIB = 1024 * 1024
 F32 = jnp.float32
@@ -43,7 +45,6 @@
     slots = SQ * groups
     steps = count // STEP_SLOTS
     half = leg_hbm.shape[2]
-    width = STEP_SLOTS * 2 * half
     wave = lax.axis_index("wave")
     lev = lax.axis_index("lev")
     lower = brackets[lev] - lev * LEV_DEV
@@ -55,8 +56,9 @@
     first_w = jnp.where(crosses, 1.0 - weight_ref[before], 0.0)
     degree = iota((16, NT), 1).astype(jnp.int16)
     sign = (1 - 2 * (iota((16, NT), 1) % 2)).astype(F32).astype(BF16)
-    lane = iota((1, width), 1)
-    south = lane % (2 * half) >= half
+    lane_group = iota((1, 2 * SQ * PART), 1) % 64 // PART
+    left = iota((1, SQ * PART), 1) < 64
+    south = iota((2 * half, 1), 0) >= half
 
     def columns_copy(step, level, buf, kind):
         slot = step % DEPTH
@@ -112,38 +114,30 @@
         def _():
             fetch(step + DEPTH - 1)
 
-        owns, firsts = [], []
-        for pair in range(SQ // 2):
-            orders, values, columns = [], [], []
-            for a in range(2):
-                sq = 2 * pair + a
-                for b in range(STEP_SLOTS):
+        for b in range(STEP_SLOTS):
+            owns, firsts = [], []
+            for quad in range(2):
+                values, factors = [], []
+                for sq in range(4 * quad, 4 * quad + 4):
                     m = wave_map[wave * slots + sq * groups + first_group + step * STEP_SLOTS + b]
-                    orders.append(m)
                     kept = degree >= m.astype(jnp.int16)
                     plain = [jnp.where(kept, leg_buf[slot, sq, b, i : i + 16, :], 0) for i in range(0, half, 16)]
                     values += plain + [x * sign for x in plain]
-                    columns += [buf[slot, sq, b] for buf in (low_buf, up_buf, first_buf)]
-            sums = nt_dot(jnp.concatenate(columns, axis=0), jnp.concatenate(values, axis=0))
-            for a in range(2):
-                own = jnp.zeros((PART, width), F32)
-                first = jnp.zeros((PART, width), F32)
-                for b in range(STEP_SLOTS):
-                    at = (a * STEP_SLOTS + b) * 3 * PART
-                    block = sums[at : at + 3 * PART, a * width : (a + 1) * width]
-                    parity = (1 - 2 * (orders[a * STEP_SLOTS + b] % 2)).astype(F32)
-                    factor = jnp.where(south, parity, 1.0)
-                    here = lane // (2 * half) == b
-                    mixed = block[:PART] * (factor * w) + block[PART : 2 * PART] * (factor * upper_w)
-                    own = jnp.where(here, mixed, own)
-                    first = jnp.where(here, block[2 * PART :] * (factor * first_w), first)
-                owns.append(own)
-                firsts.append(first)
-        for ref, parts in ((own_rows, owns), (prev_rows, firsts)):
-            stacked = jnp.concatenate(parts, axis=0)
-            for t in range(width // 128):
-                at = pl.multiple_of(step * width + t * 128, 128)
-                ref[pl.ds(at, 128), :] = stacked[:, t * 128 : (t + 1) * 128].T
+                    factors.append(jnp.where(south, (1 - 2 * (m % 2)).astype(F32), 1.0))
+                bufs = (low_buf, up_buf, first_buf) if quad == 0 else (up_buf, low_buf, first_buf)
+                columns = [buf[slot, sq, b] for buf in bufs for sq in range(4 * quad, 4 * quad + 4)]
+                sums = nt_dot(jnp.concatenate(values, axis=0), jnp.concatenate(columns, axis=0))
+                kept_sums = sums[: 2 * half] * factors[0]
+                for a in range(1, 4):
+                    block = sums[2 * half * a : 2 * half * (a + 1)] * factors[a]
+                    kept_sums = jnp.where(lane_group[:, :192] == a, block, kept_sums)
+                both = kept_sums[:, :128]
+                other = pltpu.roll(both, 64, 1)
+                owns.append(both * w + other * upper_w)
+                firsts.append(jnp.concatenate([kept_sums[:, 128:]] * 2, axis=1))
+            at = pl.multiple_of((step * STEP_SLOTS + b) * 2 * half, 2 * half)
+            own_rows[pl.ds(at, 2 * half), :] = jnp.where(left, owns[0], owns[1])
+            prev_rows[pl.ds(at, 2 * half), :] = jnp.where(left, firsts[0], firsts[1]) * first_w
         return carry
 
     lax.fori_loop(0, steps, step_body, 0)
@@ -209,57 +203,61 @@
 
 
 def table_kernel(points_ref, map_ref, hi_ref, lo_ref, perm_ref):
+    r2 = pl.program_id(0)
+    kb = pl.program_id(1)
+    rows = hi_ref.shape[1]
+    points = own_points(points_ref, r2).astype(F32)
+    inverse = 1.0 / points
+    part = r2 * pl.num_programs(1) + kb
+
+    @pl.when(part < M // PERM_ROWS)
+    def _():
+        order = part * PERM_ROWS + iota((PERM_ROWS, 1), 0)
+        wanted = jnp.where(order < HALF_M, 2 * order, 2 * (order - HALF_M) + 1)
+        perm_ref[...] = jnp.where(map_ref[...] == wanted, 1.0, 0.0).astype(BF16)
+
     lane = iota((16, 128), 1).astype(F32)
 
-    def perm_body(i, carry):
-        row = pl.multiple_of(i * 16, 16)
-        order = row + iota((16, 1), 0)
-        wanted = jnp.where(order < HALF_M, 2 * order, 2 * (order - HALF_M) + 1)
-        perm_ref[pl.ds(row, 16), :] = jnp.where(map_ref[...] == wanted, 1.0, 0.0).astype(BF16)
+    def chunk_body(i, carry):
+        chunk = pl.multiple_of(i * 16, 16)
+
+        def put(tile, value):
+            lanes = slice(tile * 128, tile * 128 + 128)
+            hi = value.astype(BF16)
+            hi_ref[0, pl.ds(chunk, 16), lanes] = hi
+            lo_ref[0, pl.ds(chunk, 16), lanes] = (value - hi.astype(F32)).astype(BF16)
+
+        k = (kb * rows + chunk + iota((16, 128), 0)).astype(F32)
+        c, s = unit_circle(2.0 * lane * k, points, inverse)
+        c1, s1 = unit_circle(k, points, inverse)
+        ct, st = unit_circle(256.0 * k, points, inverse)
+        co = c * c1 - s * s1
+        so = s * c1 + c * s1
+        for t in range(HALF_M // 128):
+            if t:
+                c, s = c * ct - s * st, s * ct + c * st
+                co, so = co * ct - so * st, so * ct + co * st
+            put(t, c)
+            put(5 + t, s)
+            put(10 + t, co)
+            put(15 + t, so)
         return carry
 
-    lax.fori_loop(0, M // 16, perm_body, 0, unroll=4)
-    for r2 in range(2):
-        points = own_points(points_ref, r2).astype(F32)
-        inverse = 1.0 / points
-
-        def chunk_body(i, carry):
-            chunk = pl.multiple_of(i * 16, 16)
-
-            def put(tile, value):
-                lanes = slice(tile * 128, tile * 128 + 128)
-                hi = value.astype(BF16)
-                hi_ref[r2, pl.ds(chunk, 16), lanes] = hi
-                lo_ref[r2, pl.ds(chunk, 16), lanes] = (value - hi.astype(F32)).astype(BF16)
-
-            k = (chunk + iota((16, 128), 0)).astype(F32)
-            c, s = unit_circle(2.0 * lane * k, points, inverse)
-            c1, s1 = unit_circle(k, points, inverse)
-            ct, st = unit_circle(256.0 * k, points, inverse)
-            co = c * c1 - s * s1
-            so = s * c1 + c * s1
-            for t in range(HALF_M // 128):
-                if t:
-                    c, s = c * ct - s * st, s * ct + c * st
-                    co, so = co * ct - so * st, so * ct + co * st
-                put(t, c)
-                put(5 + t, s)
-                put(10 + t, co)
-                put(15 + t, so)
-            return carry
-
-        lax.fori_loop(0, KPTS // 16, chunk_body, 0, unroll=6)
+    lax.fori_loop(0, rows // 16, chunk_body, 0, unroll=True)
 
 
 def tables(row_points, slot_map):
-    table = pltpu.VMEM((2, KPTS, 2 * M), BF16)
-    vmem = pl.BlockSpec(memory_space=pltpu.VMEM)
+    rows = KPTS // TABLE_STEPS
+    table = pltpu.HBM((2, KPTS, 2 * M), BF16)
+    table_spec = pl.BlockSpec((1, rows, 2 * M), lambda r, k: (r, k, 0))
+    perm_spec = pl.BlockSpec((PERM_ROWS, M), lambda r, k: (jnp.minimum(r * TABLE_STEPS + k, M // PERM_ROWS - 1), 0))
     return pl.pallas_call(
         table_kernel,
-        out_shape=[table, table, pltpu.VMEM((M, M), BF16)],
-        in_specs=[pl.BlockSpec(memory_space=pltpu.SMEM), vmem],
-        out_specs=[vmem] * 3,
-        compiler_params=pltpu.CompilerParams(vmem_limit_bytes=20 * MIB),
+        out_shape=[table, table, pltpu.HBM((M, M), BF16)],
+        grid=(2, TABLE_STEPS),
+        in_specs=[pl.BlockSpec(memory_space=pltpu.SMEM), pl.BlockSpec(memory_space=pltpu.VMEM)],
+        out_specs=[table_spec, table_spec, perm_spec],
+        compiler_params=pltpu.CompilerParams(vmem_limit_bytes=48 * MIB),
         cost_estimate=pl.CostEstimate(flops=2 * KPTS * 2 * M * 12, bytes_accessed=2 * KPTS * 2 * M * 4 + M * M * 2, transcendentals=0),
         name="fourier_tables",
     )(pltpu.with_memory_space_constraint(row_points, pltpu.HBM), slot_map)
@@ -316,7 +314,14 @@
 
 
 def synth_kernel(parts, points_ref, *refs):
-    moved_ref, pick_ref, mean_ref, flip_ref, perm_ref, hi_ref, lo_ref, out_ref, mixed, coef, flat, mirror, line = refs
+    moved_ref, pick_ref, mean_ref, flip_ref, perm_hbm, hi_hbm, lo_hbm, out_ref = refs[:8]
+    perm_ref, hi_ref, lo_ref, mixed, coef, flat, mirror, line, sems = refs[8:]
+    perm_copy = pltpu.make_async_copy(perm_hbm, perm_ref, sems.at[0])
+    table_copies = [
+        [pltpu.make_async_copy(src.at[r2], dst.at[r2], sems.at[1 + 2 * r2 + i]) for i, (src, dst) in enumerate(((hi_hbm, hi_ref), (lo_hbm, lo_ref)))]
+        for r2 in range(2)
+    ]
+    perm_copy.start()
     waves, plev, _, _ = moved_ref.shape
     wide = plev * 2 * PART
     part_rows = M // SQ
@@ -351,6 +356,9 @@
     place = iota((HALF_M, 1), 0)
     turned = (iota((1, 2 * wide), 1) % wide) // (plev * FS) >= 2
     flip_sign = jnp.where(turned & (place % 2 == 1), -1.0, 1.0).astype(BF16)
+    perm_copy.wait()
+    for copy in table_copies[0]:
+        copy.start()
     for odd in range(2):
         ordered = nn_dot(perm_ref[odd * HALF_M : (odd + 1) * HALF_M, :], mixed[...])
         wave = 2 * place + odd
@@ -364,6 +372,10 @@
     mirror[...] = jnp.zeros_like(mirror)
 
     for r2 in range(2):
+        for copy in table_copies[r2]:
+            copy.wait()
+        for copy in table_copies[1] if r2 == 0 else []:
+            copy.start()
 
         def contraction(odd):
             lanes = slice(odd * M, (odd + 1) * M)
@@ -409,23 +421,27 @@
     return pl.pallas_call(
         functools.partial(synth_kernel, parts),
         out_shape=jax.ShapeDtypeStruct((plev, 2, ROWPAD), F32),
-        in_specs=[pl.BlockSpec(memory_space=pltpu.SMEM)] + [vmem] * 7,
+        in_specs=[pl.BlockSpec(memory_space=pltpu.SMEM)] + [vmem] * 4 + [pl.BlockSpec(memory_space=pltpu.HBM)] * 3,
         out_specs=vmem,
         scratch_shapes=[
+            pltpu.VMEM((M, M), BF16),
+            pltpu.VMEM((2, KPTS, 2 * M), BF16),
+            pltpu.VMEM((2, KPTS, 2 * M), BF16),
             pltpu.VMEM((M, 2 * wide), BF16),
             pltpu.VMEM((2, 2, M, 2 * wide), BF16),
             pltpu.VMEM((8 * plev, BUF), F32),
             pltpu.VMEM((4 * plev, BUF), F32),
             pltpu.VMEM((plev, 3 * 1280 + BUF), F32),
+            pltpu.SemaphoreType.DMA((5,)),
         ],
-        compiler_params=pltpu.CompilerParams(vmem_limit_bytes=(24 if plev <= 4 else 36) * MIB),
+        compiler_params=pltpu.CompilerParams(vmem_limit_bytes=44 * MIB),
         cost_estimate=pl.CostEstimate(flops=2 * 2 * KPTS * 2 * M * 384, bytes_accessed=2 * KPTS * 2 * M * 4 + M * M * 2, transcendentals=0),
         name="synthesis",
     )(
         pltpu.with_memory_space_constraint(row_points, pltpu.HBM),
         pltpu.with_memory_space_constraint(moved, pltpu.VMEM),
         pick_tables(plev), mean_table(plev), flip_table(),
-        *[pltpu.with_memory_space_constraint(x, pltpu.VMEM) for x in (perm, table_hi, table_lo)],
+        *[pltpu.with_memory_space_constraint(x, pltpu.HBM) for x in (perm, table_hi, table_lo)],
     )
 
 
@@ -458,7 +474,7 @@
     wave_count = lax.axis_size("wave")
     lev_count = lax.axis_size("lev")
     rows_dev = 2 * half // (wave_count * lev_count)
-    cuts = (0, 12, groups) if groups >= 16 else (0, groups)
+    cuts = (0, groups)
     own_maps = wave_map.reshape(wave_count, SQ, groups)
     pairs = [(d, d - 1) for d in range(1, lev_count)]
     parts = list(zip(cuts[:-1], cuts[1:]))

time: 79.9 us -> 75.2 us (0.941)
  local copies, waits for them, and re-layouts: 13.5 us -> 0.43 us
  Pallas kernels: 36.3 us -> 41.6 us
  starting transfers between devices: 16 us -> 19.2 us
  waiting for transfers between devices: 11.4 us -> 13 us
  other arithmetic: 1.83 us -> 0.83 us
    unnamed x18 -> x12, local copies, waits for them, and re-layouts: 12.9 us -> 0.03 us
    pallas_call x1, Pallas kernels: 10 us -> 15.2 us  [synthesis(): pl.pallas_call(functools.partial(synth_kernel, parts), out_shape=jax.Shap...]
    all_to_all x1, starting transfers between devices: 9.96 us -> 14.5 us  [local(): lax.all_to_all(sent, ('wave', 'lev'), split_axis=0, concat_axis=0, tiled=...]
    pallas_call x1, Pallas kernels: 8.4 us -> 12.2 us  [tables(): pl.pallas_call(table_kernel, out_shape=[table, table, pltpu.HBM((M, M), B...]
    pallas_call x2 -> x1, Pallas kernels: 17 us -> 13.2 us  [legendre_sums(): pl.pallas_call(functools.partial(legendre_kernel, first_group, count), ou...]
    all_to_all x1, waiting for transfers between devices: 3.18 us -> 5.51 us  [local(): lax.all_to_all(sent, ('wave', 'lev'), split_axis=0, concat_axis=0, tiled=...]
    ppermute x2 -> x1, starting transfers between devices: 2.72 us -> 1.29 us  [local(): others.append(lax.ppermute(prev, 'lev', pairs))]
    select_n x1, other arithmetic: 1.67 us -> 0.76 us  [local(): return jnp.where(inside, result - climatology, 0.0)]
  transfers between devices with their start and end apart: 4 -> 3, of which waited for: 3 -> 3; matrix products, arithmetic and copies ran while one was open for 1% -> 0% of each run, Pallas kernels for 20% -> 16%
where the time goes in v5:
time: 75.2 us
  Pallas kernels  41.6 us (55%)
  starting transfers between devices  19.2 us (26%)
  waiting for transfers between devices  13 us (17%)
  other arithmetic  0.83 us (1%)
    pallas_call x1, Pallas kernels, synthesis(): pl.pallas_call(functools.partial(synth_kernel, parts), out_shape=jax.Shap...  15.2 us
    all_to_all x1, starting transfers between devices, local(): lax.all_to_all(sent, ('wave', 'lev'), split_axis=0, concat_axis=0, tiled=...  14.5 us
    pallas_call x1, Pallas kernels, legendre_sums(): pl.pallas_call(functools.partial(legendre_kernel, first_group, count), ou...  13.2 us
    pallas_call x1, Pallas kernels, tables(): pl.pallas_call(table_kernel, out_shape=[table, table, pltpu.HBM((M, M), B...  12.2 us
    all_to_all x1, waiting for transfers between devices, local(): lax.all_to_all(sent, ('wave', 'lev'), split_axis=0, concat_axis=0, tiled=...  5.51 us
    all_to_all x1, waiting for transfers between devices, local(): lax.all_to_all(energy, 'lev', split_axis=0, concat_axis=0, tiled=True)  4.82 us
    all_to_all x1, starting transfers between devices, local(): lax.all_to_all(energy, 'lev', split_axis=0, concat_axis=0, tiled=True)  3.36 us
    ppermute x1, waiting for transfers between devices, local(): others.append(lax.ppermute(prev, 'lev', pairs))  2.69 us
  transfers between devices with their start and end apart: 3, of which 3 were waited for; matrix products, arithmetic and copies ran while one was open for 0% of the time, Pallas kernels for 16%

profile of v5, /device:TPU:0, one launch (start us, length us, event | category | flops | bytes accessed | tf_op | source)
XLA Modules:
  0.0 75.2 jit_solution(8753126144395136341)
XLA Ops:
  0.0 0.0 copy-start.4
  0.0 0.0 copy-start
  0.0 0.0 copy-start.1
  0.0 0.0 copy-start.2
  0.0 13.2 %legendre_sums.1 = (f32[32,40,128]{2,1,0:T(8,128)S(1)}, f32[32,40,128]{2,1,0:T(8,128)S(1)}) custom-call(s32[1280]{0:T(1024)} %wave_map.1, s32[4]{0:T(128)} %brackets.1, f32[4]{0:T(128)} %weight_ref.1, bf16[8,20,64,1280]{3,2,1,0:T(8,128)(2,1)} %bitcast.5, bf16[8,20,32,1280]{3,2,1,0:T(8,128)(2,1)} %bitcast.6), custom_call_target="tpu_custom_call" | custom-call | flops 1258291200 | bytes 32768000 | tf_op jit(solution)/shard_map/legendre_sums/pallas_call | solution.py:163
  13.3 1.3 %collective-permute-start = (f32[32,40,128]{2,1,0:T(8,128)S(1)}, f32[32,40,128]{2,1,0:T(8,128)S(1)}, u32[]{:S(2)}, u32[]{:S(2)}) collective-permute-start(f32[32,40,128]{2,1,0:T(8,128)S(1)} %get-tuple-element.14), channel_id=1, source_target_pairs={{1,0},{2,1},{3,2},{5,4},{6,5},{7,6},{9,8},{10,9},{11,10},{13,12},{... | collective-permute-start | bytes 1966088 | tf_op jit(solution)/shard_map/ppermute | solution.py:489
  14.6 2.7 %collective-permute-done.refs_1_ = f32[32,40,128]{2,1,0:T(8,128)S(1)} collective-permute-done((f32[32,40,128]{2,1,0:T(8,128)S(1)}, f32[32,40,128]{2,1,0:T(8,128)S(1)}, u32[]{:S(2)}, u32[]{:S(2)}) %collective-permute-start) | collective-permute-done | bytes 655392 | tf_op jit(solution)/shard_map/ppermute | solution.py:489
  17.3 0.9 %join.1 = f32[32,40,128]{2,1,0:T(8,128)} custom-call(f32[32,40,128]{2,1,0:T(8,128)S(1)} %get-tuple-element.12.refs_0_, f32[32,40,128]{2,1,0:T(8,128)S(1)} %collective-permute-done.refs_1_), custom_call_target="tpu_custom_call" | custom-call | tf_op jit(solution)/shard_map/join/pallas_call | solution.py:460
  18.2 14.5 %all-to-all-start = ((f32[32,40,128]{2,1,0:T(8,128)}), f32[32,40,128]{2,1,0:T(8,128)S(1)}, u32[]{:S(2)}, u32[]{:S(2)}) async-start(f32[32,40,128]{2,1,0:T(8,128)} %join.1), calls=%async_computation | async-start | bytes 1310720 | tf_op jit(solution)/shard_map/all_to_all | solution.py:492
  32.7 0.0 copy-done.4
  32.7 0.1 reshape.50
  32.9 0.1 reshape_reshape.3.map_ref
  33.0 12.2 %fourier_tables.1 = (bf16[2,672,2560]{2,1,0:T(8,128)(2,1)}, bf16[2,672,2560]{2,1,0:T(8,128)(2,1)}, bf16[1280,1280]{1,0:T(8,128)(2,1)}) custom-call(s32[32]{0:T(128)} %points_ref.2, s32[1,1280]{1,0:T(1,128)S(1)} %reshape_reshape.3.map_ref), custom_call_target="tpu_custom_call" | custom-call | flops 41287680 | bytes 17039360 | tf_op jit(solution)/shard_map/fourier_tables/pallas_call | solution.py:254
  45.1 5.5 %all-to-all-done = f32[32,40,128]{2,1,0:T(8,128)S(1)} async-done(((f32[32,40,128]{2,1,0:T(8,128)}), f32[32,40,128]{2,1,0:T(8,128)S(1)}, u32[]{:S(2)}, u32[]{:S(2)}) %all-to-all-start) | async-done | bytes 655392 | tf_op jit(solution)/shard_map/all_to_all | solution.py:492
  50.6 0.0 copy-done
  50.6 0.0 copy-done.1
  50.6 0.0 copy-done.2
  50.6 0.0 copy-start.5
  50.7 0.0 copy-start.3
  50.7 15.2 %synthesis.1 = f32[4,2,5248]{2,1,0:T(2,128)} custom-call(s32[32]{0:T(128)} %points_ref.2, f32[8,4,40,128]{3,2,1,0:T(8,128)S(1)} %bitcast.4, bf16[2,4,256,256]{3,2,1,0:T(8,128)(2,1)S(1)} %copy-done, bf16[32,256]{1,0:T(8,128)(2,1)S(1)} %copy-done.2, bf16[256,256]{1,0:T(8,128)(2,1)S(1)} %copy-done.1, bf16[1280,1280]{1,0:T(8,128)(2,1)} %get-tuple-element.16.refs_4_, ...), custom_call_target="tpu_custom_call" | custom-call | flops 2642411520 | bytes 17039360 | tf_op jit(solution)/shard_map/synthesis/pallas_call | solution.py:421
  65.9 3.4 %all-to-all-start.1 = ((f32[4,2,5248]{2,1,0:T(2,128)}), f32[4,2,5248]{2,1,0:T(2,128)S(1)}, u32[]{:S(2)}, u32[]{:S(2)}) async-start(f32[4,2,5248]{2,1,0:T(2,128)} %synthesis.1), calls=%async_computation.1 | async-start | bytes 335872 | tf_op jit(solution)/shard_map/all_to_all | solution.py:498
  69.3 0.0 copy-done.5
  69.3 0.1 pad_add_fusion
  69.4 0.1 dynamic_slice.3
  69.4 4.8 %all-to-all-done.1 = f32[4,2,5248]{2,1,0:T(2,128)S(1)} async-done(((f32[4,2,5248]{2,1,0:T(2,128)}), f32[4,2,5248]{2,1,0:T(2,128)S(1)}, u32[]{:S(2)}, u32[]{:S(2)}) %all-to-all-start.1) | async-done | bytes 167968 | tf_op jit(solution)/shard_map/all_to_all | solution.py:498
  74.3 0.1 reshape.51
  74.4 0.0 copy-done.3
  74.4 0.8 %subtract_select_fusion = f32[1,8,5248]{2,1,0:T(8,128)} fusion(f32[1,8,5248]{2,1,0:T(8,128)S(1)} %reshape.51, f32[1,8,5248]{2,1,0:T(8,128)S(1)} %copy-done.3, s32[8]{0:T(128)S(1)} %dynamic_slice.3), kind=kLoop, calls=%fused_computation | loop fusion | flops 125952 | bytes 503840 | tf_op jit(solution)/shard_map/jit(_where)/select_n | solution.py:505
  (1 shorter events, 0.0 us)
Async XLA Ops:
  0.0 32.7 %copy-start.4 = (s32[1280]{0:T(1024)S(1)}, s32[1280]{0:T(1024)}, u32[]{:S(2)}) copy-start(s32[1280]{0:T(1024)} %wave_map.1) | copy-start | bytes 15364
  0.0 50.6 %copy-start = (bf16[2,4,256,256]{3,2,1,0:T(8,128)(2,1)S(1)}, bf16[2,4,256,256]{3,2,1,0:T(8,128)(2,1)}, u32[]{:S(2)}) copy-start(bf16[2,4,256,256]{3,2,1,0:T(8,128)(2,1)} %constant.20.clone.refs_1_) | copy-start | bytes 3145732
  0.0 50.6 %copy-start.1 = (bf16[256,256]{1,0:T(8,128)(2,1)S(1)}, bf16[256,256]{1,0:T(8,128)(2,1)}, u32[]{:S(2)}) copy-start(bf16[256,256]{1,0:T(8,128)(2,1)} %constant.22.clone.refs_3_) | copy-start | bytes 393220
  0.0 50.6 %copy-start.2 = (bf16[32,256]{1,0:T(8,128)(2,1)S(1)}, bf16[32,256]{1,0:T(8,128)(2,1)}, u32[]{:S(2)}) copy-start(bf16[32,256]{1,0:T(8,128)(2,1)} %constant.21.clone.refs_2_) | copy-start | bytes 49156
  13.3 4.0 %collective-permute-start = (f32[32,40,128]{2,1,0:T(8,128)S(1)}, f32[32,40,128]{2,1,0:T(8,128)S(1)}, u32[]{:S(2)}, u32[]{:S(2)}) collective-permute-start(f32[32,40,128]{2,1,0:T(8,128)S(1)} %get-tuple-element.14), channel_id=1, source_target_pairs={{1,0},{2,1},{3,2},{5,4},{6,5},{7,6},{9,8},{10,9},{11,10},{13,12},{... | collective-permute-start | bytes 1966088 | tf_op jit(solution)/shard_map/ppermute | solution.py:489
  18.2 32.5 %all-to-all-start = ((f32[32,40,128]{2,1,0:T(8,128)}), f32[32,40,128]{2,1,0:T(8,128)S(1)}, u32[]{:S(2)}, u32[]{:S(2)}) async-start(f32[32,40,128]{2,1,0:T(8,128)} %join.1), calls=%async_computation | async-start | bytes 1310720 | tf_op jit(solution)/shard_map/all_to_all | solution.py:492
  50.6 18.6 %copy-start.5 = (s32[32]{0:T(128)S(1)}, s32[32]{0:T(128)}, u32[]{:S(2)}) copy-start(s32[32]{0:T(128)} %points_ref.2) | copy-start | bytes 388
  50.7 23.7 %copy-start.3 = (f32[1,8,5248]{2,1,0:T(8,128)S(1)}, f32[1,8,5248]{2,1,0:T(8,128)}, u32[]{:S(2)}) copy-start(f32[1,8,5248]{2,1,0:T(8,128)} %param.16) | copy-start | bytes 503812
  65.9 8.4 %all-to-all-start.1 = ((f32[4,2,5248]{2,1,0:T(2,128)}), f32[4,2,5248]{2,1,0:T(2,128)S(1)}, u32[]{:S(2)}, u32[]{:S(2)}) async-start(f32[4,2,5248]{2,1,0:T(2,128)} %synthesis.1), calls=%async_computation.1 | async-start | bytes 335872 | tf_op jit(solution)/shard_map/all_to_all | solution.py:498

commit v6 on v5

--- a/solution.py
+++ b/solution.py
@@ -214,7 +214,8 @@
     def _():
         order = part * PERM_ROWS + iota((PERM_ROWS, 1), 0)
         wanted = jnp.where(order < HALF_M, 2 * order, 2 * (order - HALF_M) + 1)
-        perm_ref[...] = jnp.where(map_ref[...] == wanted, 1.0, 0.0).astype(BF16)
+        here = pl.ds(pl.multiple_of(part * PERM_ROWS, PERM_ROWS), PERM_ROWS)
+        perm_ref[here, :] = jnp.where(map_ref[...] == wanted, 1.0, 0.0).astype(BF16)
 
     lane = iota((16, 128), 1).astype(F32)
 
@@ -250,10 +251,10 @@
     rows = KPTS // TABLE_STEPS
     table = pltpu.HBM((2, KPTS, 2 * M), BF16)
     table_spec = pl.BlockSpec((1, rows, 2 * M), lambda r, k: (r, k, 0))
-    perm_spec = pl.BlockSpec((PERM_ROWS, M), lambda r, k: (jnp.minimum(r * TABLE_STEPS + k, M // PERM_ROWS - 1), 0))
+    perm_spec = pl.BlockSpec(memory_space=pltpu.VMEM)
     return pl.pallas_call(
         table_kernel,
-        out_shape=[table, table, pltpu.HBM((M, M), BF16)],
+        out_shape=[table, table, pltpu.VMEM((M, M), BF16)],
         grid=(2, TABLE_STEPS),
         in_specs=[pl.BlockSpec(memory_space=pltpu.SMEM), pl.BlockSpec(memory_space=pltpu.VMEM)],
         out_specs=[table_spec, table_spec, perm_spec],
@@ -314,14 +315,17 @@
 
 
 def synth_kernel(parts, points_ref, *refs):
-    moved_ref, pick_ref, mean_ref, flip_ref, perm_hbm, hi_hbm, lo_hbm, out_ref = refs[:8]
-    perm_ref, hi_ref, lo_ref, mixed, coef, flat, mirror, line, sems = refs[8:]
-    perm_copy = pltpu.make_async_copy(perm_hbm, perm_ref, sems.at[0])
-    table_copies = [
-        [pltpu.make_async_copy(src.at[r2], dst.at[r2], sems.at[1 + 2 * r2 + i]) for i, (src, dst) in enumerate(((hi_hbm, hi_ref), (lo_hbm, lo_ref)))]
-        for r2 in range(2)
-    ]
-    perm_copy.start()
+    moved_ref, pick_ref, mean_ref, flip_ref, perm_ref, hi_hbm, lo_hbm, out_ref = refs[:8]
+    hi_ref, lo_ref, mixed, coef, flat, mirror, line, sems = refs[8:]
+    table_copies = []
+    for r2 in range(2):
+        table_copies.append([])
+        for i, (src, dst) in enumerate(((hi_hbm, hi_ref), (lo_hbm, lo_ref))):
+            for c in range(2):
+                rows = pl.ds(c * (KPTS // 2), KPTS // 2)
+                table_copies[r2].append(pltpu.make_async_copy(src.at[r2, rows], dst.at[r2, rows], sems.at[r2, i, c]))
+    for copy in table_copies[0]:
+        copy.start()
     waves, plev, _, _ = moved_ref.shape
     wide = plev * 2 * PART
     part_rows = M // SQ
@@ -356,9 +360,6 @@
     place = iota((HALF_M, 1), 0)
     turned = (iota((1, 2 * wide), 1) % wide) // (plev * FS) >= 2
     flip_sign = jnp.where(turned & (place % 2 == 1), -1.0, 1.0).astype(BF16)
-    perm_copy.wait()
-    for copy in table_copies[0]:
-        copy.start()
     for odd in range(2):
         ordered = nn_dot(perm_ref[odd * HALF_M : (odd + 1) * HALF_M, :], mixed[...])
         wave = 2 * place + odd
@@ -421,10 +422,9 @@
     return pl.pallas_call(
         functools.partial(synth_kernel, parts),
         out_shape=jax.ShapeDtypeStruct((plev, 2, ROWPAD), F32),
-        in_specs=[pl.BlockSpec(memory_space=pltpu.SMEM)] + [vmem] * 4 + [pl.BlockSpec(memory_space=pltpu.HBM)] * 3,
+        in_specs=[pl.BlockSpec(memory_space=pltpu.SMEM)] + [vmem] * 5 + [pl.BlockSpec(memory_space=pltpu.HBM)] * 2,
         out_specs=vmem,
         scratch_shapes=[
-            pltpu.VMEM((M, M), BF16),
             pltpu.VMEM((2, KPTS, 2 * M), BF16),
             pltpu.VMEM((2, KPTS, 2 * M), BF16),
             pltpu.VMEM((M, 2 * wide), BF16),
@@ -432,7 +432,7 @@
             pltpu.VMEM((8 * plev, BUF), F32),
             pltpu.VMEM((4 * plev, BUF), F32),
             pltpu.VMEM((plev, 3 * 1280 + BUF), F32),
-            pltpu.SemaphoreType.DMA((5,)),
+            pltpu.SemaphoreType.DMA((2, 2, 2)),
         ],
         compiler_params=pltpu.CompilerParams(vmem_limit_bytes=44 * MIB),
         cost_estimate=pl.CostEstimate(flops=2 * 2 * KPTS * 2 * M * 384, bytes_accessed=2 * KPTS * 2 * M * 4 + M * M * 2, transcendentals=0),
@@ -441,7 +441,8 @@
         pltpu.with_memory_space_constraint(row_points, pltpu.HBM),
         pltpu.with_memory_space_constraint(moved, pltpu.VMEM),
         pick_tables(plev), mean_table(plev), flip_table(),
-        *[pltpu.with_memory_space_constraint(x, pltpu.HBM) for x in (perm, table_hi, table_lo)],
+        pltpu.with_memory_space_constraint(perm, pltpu.VMEM),
+        *[pltpu.with_memory_space_constraint(x, pltpu.HBM) for x in (table_hi, table_lo)],
     )
 
 
@@ -480,13 +481,21 @@
     parts = list(zip(cuts[:-1], cuts[1:]))
     owns, others, maps = [], [], []
     order = wave_map
+    between_chips = jnp.any(brackets[1:-1:2] == jnp.arange(2, lev_count, 2) * LEV_DEV - 1)
     for start, stop in parts:
         own, prev = legendre_sums(start, stop - start, spectral, legendre, order, brackets, lev_weight)
         order, prev = lax.optimization_barrier((wave_map, prev))
         if others:
             prev, _ = lax.optimization_barrier((prev, others[-1]))
         owns.append(own)
-        others.append(lax.ppermute(prev, "lev", pairs))
+        others.append(
+            lax.cond(
+                between_chips,
+                lambda x: lax.ppermute(x, "lev", pairs),
+                lambda x: lax.ppermute(x, "lev", pairs[::2]),
+                prev,
+            )
+        )
         maps.append(jnp.transpose(own_maps[:, :, start:stop], (1, 0, 2)).reshape(SQ, wave_count * (stop - start)))
     sent = join(owns, others)
     moved = lax.all_to_all(sent, ("wave", "lev"), split_axis=0, concat_axis=0, tiled=True)

time: 75.2 us -> 79 us (1.051)
  local copies, waits for them, and re-layouts: 0.43 us -> 2.89 us
  Pallas kernels: 41.6 us -> 40.6 us
  other arithmetic: 0.83 us -> 1.75 us
    pallas_call x1, Pallas kernels: 15.2 us -> 13.7 us  [synthesis(): pl.pallas_call(functools.partial(synth_kernel, parts), out_shape=jax.Shap...]
    slice x0 -> x1, local copies, waits for them, and re-layouts: none -> 1.24 us  [local(): brackets[1:-1:2] == jnp.arange(2, lev_count, 2) * LEV_DEV - 1]
    unnamed x12 -> x10, local copies, waits for them, and re-layouts: 0.03 us -> 1.25 us
    pallas_call x1, Pallas kernels: 0.91 us -> 1.99 us  [join(): pl.pallas_call(join_kernel, out_shape=jax.ShapeDtypeStruct((owns[0].shape...]
    select_n x1, other arithmetic: 0.76 us -> 1.67 us  [local(): return jnp.where(inside, result - climatology, 0.0)]
  transfers between devices with their start and end apart: 3 -> 3, of which waited for: 3 -> 3; matrix products, arithmetic and copies ran while one was open for 0% -> 0% of each run, Pallas kernels for 16% -> 15%
where the time goes in v6:
time: 79 us; the launch traced here: 78.9 us
  Pallas kernels  40.6 us (51%)
  starting transfers between devices  19.3 us (24%)
  waiting for transfers between devices  13.6 us (17%)
  local copies, waits for them, and re-layouts  2.89 us (4%)
  other arithmetic  1.75 us (2%)
    all_to_all x1, starting transfers between devices, local(): lax.all_to_all(sent, ('wave', 'lev'), split_axis=0, concat_axis=0, tiled=...  14.6 us
    pallas_call x1, Pallas kernels, synthesis(): pl.pallas_call(functools.partial(synth_kernel, parts), out_shape=jax.Shap...  13.7 us
    pallas_call x1, Pallas kernels, legendre_sums(): pl.pallas_call(functools.partial(legendre_kernel, first_group, count), ou...  13.3 us
    pallas_call x1, Pallas kernels, tables(): pl.pallas_call(table_kernel, out_shape=[table, table, pltpu.VMEM((M, M),...  11.7 us
    all_to_all x1, waiting for transfers between devices, local(): lax.all_to_all(sent, ('wave', 'lev'), split_axis=0, concat_axis=0, tiled=...  6 us
    all_to_all x1, waiting for transfers between devices, local(): lax.all_to_all(energy, 'lev', split_axis=0, concat_axis=0, tiled=True)  4.82 us
    all_to_all x1, starting transfers between devices, local(): lax.all_to_all(energy, 'lev', split_axis=0, concat_axis=0, tiled=True)  3.36 us
    ppermute x1, waiting for transfers between devices, local(): lax.ppermute(x, 'lev', pairs)  2.82 us
  transfers between devices with their start and end apart: 3, of which 3 were waited for; matrix products, arithmetic and copies ran while one was open for 0% of the time, Pallas kernels for 15%

profile of v6, /device:TPU:0, one launch (start us, length us, event | category | flops | bytes accessed | tf_op | source)
XLA Modules:
  0.0 78.9 jit_solution(1081081916771309683)
XLA Ops:
  0.0 1.2 %slice.4 = s32[1]{0:T(128)} slice(s32[4]{0:T(128)} %brackets.1), slice={[1:2]} | slice | bytes 8 | tf_op jit(solution)/shard_map/slice | solution.py:484
  1.9 0.0 copy-start.3
  1.9 0.0 copy-start.1
  1.9 0.0 copy-start.2
  1.9 13.3 %legendre_sums.1 = (f32[32,40,128]{2,1,0:T(8,128)S(1)}, f32[32,40,128]{2,1,0:T(8,128)S(1)}) custom-call(s32[1280]{0:T(1024)} %wave_map.1, s32[4]{0:T(128)} %brackets.1, f32[4]{0:T(128)} %weight_ref.1, bf16[8,20,64,1280]{3,2,1,0:T(8,128)(2,1)} %bitcast.5, bf16[8,20,32,1280]{3,2,1,0:T(8,128)(2,1)} %bitcast.6), custom_call_target="tpu_custom_call" | custom-call | flops 1258291200 | bytes 32768000 | tf_op jit(solution)/shard_map/legendre_sums/pallas_call | solution.py:163
  15.2 4.1 %conditional.1 = (f32[32,40,128]{2,1,0:T(8,128)}) conditional(s32[]{:T(128)} %bitcast.2, f32[32,40,128]{2,1,0:T(8,128)S(1)} %get-tuple-element.19, f32[32,40,128]{2,1,0:T(8,128)S(1)} %get-tuple-element.19), branch_computations={%region_0.0_spmd, %region_1.0_spmd} | conditional | bytes 2621488 | solution.py:492
  15.2 1.3 %collective-permute-start.1 = (f32[32,40,128]{2,1,0:T(8,128)S(1)}, f32[32,40,128]{2,1,0:T(8,128)}, u32[]{:S(2)}, u32[]{:S(2)}) collective-permute-start(f32[32,40,128]{2,1,0:T(8,128)S(1)} %param.1), channel_id=1, source_target_pairs={{1,0},{2,1},{3,2},{5,4},{6,5},{7,6},{9,8},{10,9},{11,10},{13,12},{... | collective-permute-start | bytes 1966088 | tf_op jit(solution)/shard_map/cond/branch_1_fun/ppermute | solution.py:494
  16.5 2.8 %collective-permute-done.1 = f32[32,40,128]{2,1,0:T(8,128)} collective-permute-done((f32[32,40,128]{2,1,0:T(8,128)S(1)}, f32[32,40,128]{2,1,0:T(8,128)}, u32[]{:S(2)}, u32[]{:S(2)}) %collective-permute-start.1) | collective-permute-done | bytes 655392 | tf_op jit(solution)/shard_map/cond/branch_1_fun/ppermute | solution.py:494
  19.3 2.0 %join.1 = f32[32,40,128]{2,1,0:T(8,128)} custom-call(f32[32,40,128]{2,1,0:T(8,128)S(1)} %get-tuple-element.17.refs_0_, f32[32,40,128]{2,1,0:T(8,128)} %get-tuple-element.24.refs_1_), custom_call_target="tpu_custom_call" | custom-call | tf_op jit(solution)/shard_map/join/pallas_call | solution.py:461
  21.3 14.6 %all-to-all-start = ((f32[32,40,128]{2,1,0:T(8,128)}), f32[32,40,128]{2,1,0:T(8,128)}, u32[]{:S(2)}, u32[]{:S(2)}) async-start(f32[32,40,128]{2,1,0:T(8,128)} %join.1), calls=%async_computation | async-start | bytes 1310720 | tf_op jit(solution)/shard_map/all_to_all | solution.py:501
  35.9 0.0 copy-done.3
  36.0 0.1 reshape.53
  36.1 0.1 reshape_reshape.3.map_ref
  36.2 11.7 %fourier_tables.1 = (bf16[2,672,2560]{2,1,0:T(8,128)(2,1)}, bf16[2,672,2560]{2,1,0:T(8,128)(2,1)}, bf16[1280,1280]{1,0:T(8,128)(2,1)S(1)}) custom-call(s32[32]{0:T(128)} %points_ref.2, s32[1,1280]{1,0:T(1,128)S(1)} %reshape_reshape.3.map_ref), custom_call_target="tpu_custom_call" | custom-call | flops 41287680 | bytes 17039360 | tf_op jit(solution)/shard_map/fourier_tables/pallas_call | solution.py:255
  47.9 6.0 %all-to-all-done = f32[32,40,128]{2,1,0:T(8,128)} async-done(((f32[32,40,128]{2,1,0:T(8,128)}), f32[32,40,128]{2,1,0:T(8,128)}, u32[]{:S(2)}, u32[]{:S(2)}) %all-to-all-start) | async-done | bytes 655392 | tf_op jit(solution)/shard_map/all_to_all | solution.py:501
  53.9 0.0 copy-done.1
  53.9 0.0 copy-done.2
  53.9 0.0 copy-start
  53.9 1.2 %copy-done = bf16[2,4,256,256]{3,2,1,0:T(8,128)(2,1)S(1)} copy-done((bf16[2,4,256,256]{3,2,1,0:T(8,128)(2,1)S(1)}, bf16[2,4,256,256]{3,2,1,0:T(8,128)(2,1)}, u32[]{:S(2)}) %copy-start) | copy-done | bytes 1048600
  55.1 0.0 copy-start.4
  55.1 13.7 %synthesis.1 = f32[4,2,5248]{2,1,0:T(2,128)} custom-call(s32[32]{0:T(128)} %points_ref.2, f32[8,4,40,128]{3,2,1,0:T(8,128)} %bitcast.3.refs_0_, bf16[2,4,256,256]{3,2,1,0:T(8,128)(2,1)S(1)} %copy-done, bf16[32,256]{1,0:T(8,128)(2,1)S(1)} %copy-done.2, bf16[256,256]{1,0:T(8,128)(2,1)S(1)} %copy-done.1, bf16[1280,1280]{1,0:T(8,128)(2,1)S(1)} %get-tuple-element.21.refs_4_, ...), custom_call_target="tpu_custom_call" | custom-call | flops 2642411520 | bytes 17039360 | tf_op jit(solution)/shard_map/synthesis/pallas_call | solution.py:422
  68.8 3.4 %all-to-all-start.1 = ((f32[4,2,5248]{2,1,0:T(2,128)}), f32[4,2,5248]{2,1,0:T(2,128)S(1)}, u32[]{:S(2)}, u32[]{:S(2)}) async-start(f32[4,2,5248]{2,1,0:T(2,128)} %synthesis.1), calls=%async_computation.1 | async-start | bytes 335872 | tf_op jit(solution)/shard_map/all_to_all | solution.py:507
  72.2 0.0 copy-done.4
  72.2 0.1 pad_add_fusion
  72.2 0.1 dynamic_slice.3
  72.3 4.8 %all-to-all-done.1 = f32[4,2,5248]{2,1,0:T(2,128)S(1)} async-done(((f32[4,2,5248]{2,1,0:T(2,128)}), f32[4,2,5248]{2,1,0:T(2,128)S(1)}, u32[]{:S(2)}, u32[]{:S(2)}) %all-to-all-start.1) | async-done | bytes 167968 | tf_op jit(solution)/shard_map/all_to_all | solution.py:507
  77.1 0.1 reshape.54
  77.3 1.7 %subtract_select_fusion = f32[1,8,5248]{2,1,0:T(8,128)} fusion(f32[1,8,5248]{2,1,0:T(8,128)S(1)} %reshape.54, f32[1,8,5248]{2,1,0:T(8,128)} %param.18, s32[8]{0:T(128)S(1)} %dynamic_slice.3), kind=kLoop, calls=%fused_computation | loop fusion | flops 125952 | bytes 503840 | tf_op jit(solution)/shard_map/jit(_where)/select_n | solution.py:514
  (1 shorter events, 0.0 us)
Async XLA Ops:
  1.9 34.1 %copy-start.3 = (s32[1280]{0:T(1024)S(1)}, s32[1280]{0:T(1024)}, u32[]{:S(2)}) copy-start(s32[1280]{0:T(1024)} %wave_map.1) | copy-start | bytes 15364
  1.9 52.0 %copy-start.1 = (bf16[256,256]{1,0:T(8,128)(2,1)S(1)}, bf16[256,256]{1,0:T(8,128)(2,1)}, u32[]{:S(2)}) copy-start(bf16[256,256]{1,0:T(8,128)(2,1)} %constant.25.clone.refs_3_) | copy-start | bytes 393220
  1.9 51.9 %copy-start.2 = (bf16[32,256]{1,0:T(8,128)(2,1)S(1)}, bf16[32,256]{1,0:T(8,128)(2,1)}, u32[]{:S(2)}) copy-start(bf16[32,256]{1,0:T(8,128)(2,1)} %constant.24.clone.refs_2_) | copy-start | bytes 49156
  15.2 4.1 %collective-permute-start.1 = (f32[32,40,128]{2,1,0:T(8,128)S(1)}, f32[32,40,128]{2,1,0:T(8,128)}, u32[]{:S(2)}, u32[]{:S(2)}) collective-permute-start(f32[32,40,128]{2,1,0:T(8,128)S(1)} %param.1), channel_id=1, source_target_pairs={{1,0},{2,1},{3,2},{5,4},{6,5},{7,6},{9,8},{10,9},{11,10},{13,12},{... | collective-permute-start | bytes 1966088 | tf_op jit(solution)/shard_map/cond/branch_1_fun/ppermute | solution.py:494
  21.3 32.5 %all-to-all-start = ((f32[32,40,128]{2,1,0:T(8,128)}), f32[32,40,128]{2,1,0:T(8,128)}, u32[]{:S(2)}, u32[]{:S(2)}) async-start(f32[32,40,128]{2,1,0:T(8,128)} %join.1), calls=%async_computation | async-start | bytes 1310720 | tf_op jit(solution)/shard_map/all_to_all | solution.py:501
  53.9 1.2 %copy-start = (bf16[2,4,256,256]{3,2,1,0:T(8,128)(2,1)S(1)}, bf16[2,4,256,256]{3,2,1,0:T(8,128)(2,1)}, u32[]{:S(2)}) copy-start(bf16[2,4,256,256]{3,2,1,0:T(8,128)(2,1)} %constant.23.clone.refs_1_) | copy-start | bytes 3145732
  55.1 17.1 %copy-start.4 = (s32[32]{0:T(128)S(1)}, s32[32]{0:T(128)}, u32[]{:S(2)}) copy-start(s32[32]{0:T(128)} %points_ref.2) | copy-start | bytes 388
  68.8 8.4 %all-to-all-start.1 = ((f32[4,2,5248]{2,1,0:T(2,128)}), f32[4,2,5248]{2,1,0:T(2,128)S(1)}, u32[]{:S(2)}, u32[]{:S(2)}) async-start(f32[4,2,5248]{2,1,0:T(2,128)} %synthesis.1), calls=%async_computation.1 | async-start | bytes 335872 | tf_op jit(solution)/shard_map/all_to_all | solution.py:507
